TPU v7x, 256 devices: a whole 4x4x8 slice. The times are simulated.
256 devices in a mesh: leaf: 16 (over z, core), front: 16 (over y, x).
Axes of the slice: x: 4, y: 4, z: 8, core: 2. Of those that a mesh axis runs over, the one named last changes fastest.
Arguments:
- leaf_source: float32 [16, 2048, 128], P('leaf', 'front'), may hold values from -6 to 6
- top_source: float32 [7, 512, 128], P(None, 'front'), may hold values from -6 to 6
- leaf_lower_inverse: bfloat16 [16, 2048, 2048], P('leaf', 'front'), as said below
- leaf_upper_inverse: bfloat16 [16, 2048, 2048], P('leaf', 'front'), as said below
- leaf_lower_block: bfloat16 [16, 1024, 2048], P('leaf', None, 'front'), may hold values from -0.09375 to 0.09375
- leaf_upper_block: bfloat16 [16, 2048, 1024], P('leaf', 'front'), may hold values from -0.1875 to 0.1875
- top_lower_inverse: bfloat16 [7, 512, 512], P(None, 'front'), as said below
- top_upper_inverse: bfloat16 [7, 512, 512], P(None, 'front'), as said below
- top_lower_block: bfloat16 [6, 512, 512], P(None, None, 'front'), may hold values from -0.25 to 0.25
- top_upper_block: bfloat16 [6, 512, 512], P(None, 'front'), may hold values from -0.25 to 0.25
- leaf_targets: int32 [16, 1024], P('leaf'), may hold values from 0 to 3583, as said below
- top_targets: int32 [6, 512], replicated, may hold values from 0 to 1535, as said below
Outputs:
- leaf_solution: float32 [16, 2048, 128], P('leaf', 'front')
- top_solution: float32 [7, 512, 128], P(None, 'front')
Inputs may be any that keep to these rules, and one draw needn't show every extreme that they name: `leaf_targets`: each update row of leaf l lands in one of its 3 ancestors: the separator of height h above leaf l has index 2**(h-1) - 1 + l * 2**(h-1) // 16. Rows may repeat. `top_targets`: each update row of separator s + 1 lands in a row of one of its ancestors in the binary tree of separators (the parent of separator s + 1 is separator (s + 1 - 1) // 2). Rows may repeat. `leaf_lower_inverse`: each block is the identity plus independent entries of deviation 0.6 / sqrt(2048). `leaf_upper_inverse`: as leaf_lower_inverse. `top_lower_inverse`: each block is the identity plus independent entries of deviation 0.6 / sqrt(512). `top_upper_inverse`: as top_lower_inverse.
All inputs are finite; a program needn't handle non-finite values.
Results may differ from a plain program's by a relative error of at most 0.022.
Values may be sent and summed in bfloat16 or wider, within the bound.
No kernel may reach another device: no remote copies, remote signals or barrier semaphores. Data moves between devices by JAX's collectives and lax.ppermute only.
A program may use at most 64 MiB of HBM per device.

v0:
```python
import jax
import jax.numpy as jnp
from jax import lax
from jax.experimental import pallas as pl
from jax.experimental.pallas import tpu as pltpu
from jax.sharding import PartitionSpec as P

BF = jnp.bfloat16
F32 = jnp.float32
FRONT = 16
LEAVES = 16
SUB = 2048
SEP = 512
UPD = 1024
RHS = 128
ROWS = SEP // FRONT
SPAN = 3 * SEP
HALF = SPAN // 2
PIECE = SUB // FRONT
NT = (((1,), (1,)), ((), ()))
NN = (((1,), (0,)), ((), ()))


def dot(a, b, dims):
    return lax.dot_general(a, b, dims, preferred_element_type=F32)


def split_dot(x, w, dims):
    head = x.astype(BF).astype(F32)
    both = jnp.concatenate([head, x - head], axis=0).astype(BF)
    out = dot(both, w, dims)
    return out[:8] + out[8:]


def fold(x):
    return jnp.concatenate([x[:, :HALF], x[:, HALF:]], axis=0)


def unfold(x):
    return jnp.concatenate([x[:8], x[8:]], axis=1)


def one_hot(first, count, places):
    rows = lax.broadcasted_iota(jnp.int32, (count, places.shape[1]), 0) + first
    return jnp.where(rows == places, 1.0, 0.0).astype(BF)


def leaf_places(targets):
    owner = targets >> 9
    height = jnp.where(owner > 0, 1, 0) + jnp.where(owner > 2, 1, 0)
    return (height << 9) | (targets & (SEP - 1))


def ancestor_places(targets):
    return jnp.where(targets >= SEP, SEP, 0) + (targets & (SEP - 1))


def prepare_kernel(source, low_inv, up_inv, low, up, send, mats, piece, sems):
    leaf = lax.axis_index("leaf")
    third = 3 + (leaf >> 2)
    second = 1 + (leaf >> 3)
    plans = [
        [(low_inv, third), (low_inv, second), (low_inv, 0), (up_inv, 0), (up, second - 1)],
        [(low, third - 1), (low, second - 1), (up_inv, second), (up, third - 1), (up_inv, third)],
    ]
    places = [mats.at[pl.ds(i * ROWS, ROWS)] for i in range(5)]
    start = pltpu.make_async_copy(source.at[0], piece, sems.at[5])
    start.start()
    for core, plan in enumerate(plans):

        @pl.when((leaf & 1) == core)
        def _(plan=plan):
            copies = [
                pltpu.make_async_copy(ref.at[index], place, sems.at[slot])
                for slot, ((ref, index), place) in enumerate(zip(plan, places))
            ]
            for copy in copies:
                copy.start()
            for copy in copies:
                copy.wait()

    start.wait()
    block = piece[...].astype(BF)
    for to in range(FRONT):
        send[to] = block


def pack_kernel(own, a, b, c, out):
    for k, ref in enumerate((own, a, b, c)):
        out[k] = ref[...]


def assemble_kernel(own, a, b, c, ahead, later):
    front = lax.axis_index("front")
    core = lax.axis_index("leaf") & 1
    y, x = front >> 2, front & 3
    for j, ref in enumerate((own, a, b, c)):
        for k in range(4):
            dy = jnp.where(core == 0, j, k)
            dx = jnp.where(core == 0, k, j)
            at = ((y - dy) & 3) * 4 + ((x - dx) & 3)
            rows = pl.ds(pl.multiple_of(at * ROWS, ROWS), ROWS)
            for i in range(5):
                part = ref[k, i * ROWS : i * ROWS + ROWS, :]
                if i < 2:
                    ahead[i, rows, :] = part
                else:
                    later[i - 2, rows, :] = part


def pick_kernel(block, targets, picked):
    places = leaf_places(targets[...])
    for part in range(3):
        rows = slice(part * SEP, part * SEP + SEP)
        picked[:, rows] = dot(block[0], one_hot(part * SEP, SEP, places), NT).astype(BF)


def leaf_forward_kernel(got, inverse, block, targets, top, solved_out, send):
    leaf = lax.axis_index("leaf")
    front = lax.axis_index("front")
    solved = dot(inverse[0], got[...].reshape(SUB, RHS), NN)
    solved_out[...] = solved
    update = dot(solved.T.astype(BF), block[0], NT)
    own = jnp.concatenate(
        [
            top[0] * (1 / 16),
            top[1 + (leaf >> 3)] * (1 / 8),
            top[3 + (leaf >> 2)] * (1 / 4),
            jnp.zeros((32, RHS), F32),
        ],
        axis=0,
    ).T
    lhs = jnp.concatenate([-update, own], axis=1).astype(BF)
    lane = lax.broadcasted_iota(jnp.int32, (1, RHS), 1)
    top_places = jnp.where(lane < 96, ((lane >> 5) << 9) + front * ROWS + (lane & 31), -1)
    places = jnp.concatenate([leaf_places(targets[...]), top_places], axis=1)
    low = dot(lhs, one_hot(0, HALF, places), NT)
    high = dot(lhs, one_hot(HALF, HALF, places), NT)
    for to in range(FRONT):
        rows = slice(to * 8, to * 8 + 8)
        send[to] = jnp.concatenate([low[rows], high[rows]], axis=0).astype(BF)


def top_forward_kernel(got, first, swapped, targets, send, hot2, hot3):
    leaf = lax.axis_index("leaf")
    hot2[...] = one_hot(0, SEP, targets[pl.ds(leaf >> 3, 1), :])
    hot3[...] = one_hot(0, 2 * SEP, ancestor_places(targets[pl.ds(2 + (leaf >> 2), 1), :]))
    total = got[0].astype(F32)
    for k in range(1, FRONT):
        total = total + got[k].astype(F32)
    total = unfold(total)

    def run(even, odd):
        target1 = total[:, :SEP]
        target2 = total[:, SEP : 2 * SEP]
        solved3 = split_dot(total[:, 2 * SEP :], even[0], NT)
        update3 = split_dot(solved3, odd[0], NN)
        spread3 = split_dot(update3, hot3[...], NT)
        target1 = target1 - spread3[:, :SEP]
        target2 = target2 - spread3[:, SEP:]
        solved2 = split_dot(target2, even[1], NT)
        update2 = split_dot(solved2, odd[1], NN)
        target1 = target1 - split_dot(update2, hot2[...], NT)
        send[...] = fold(jnp.concatenate([target1, solved2, solved3], axis=1)).astype(BF)

    @pl.when((leaf & 1) == 0)
    def _():
        run(first, swapped)

    @pl.when((leaf & 1) == 1)
    def _():
        run(swapped, first)


def group_kernel(own, a, b, c, send):
    total = (own[...].astype(F32) + a[...].astype(F32)) + (b[...].astype(F32) + c[...].astype(F32))
    send[...] = total.astype(BF)


def top_backward_kernel(own, near, far, other, later, swapped, hot2, hot3, send):
    core = lax.axis_index("leaf") & 1
    part = unfold(own[...].astype(F32))
    side = unfold(near[...].astype(F32))
    rest = unfold(far[...].astype(F32) + other[...].astype(F32))
    total1 = part[:, :SEP] + side[:, :SEP] + rest[:, :SEP]
    total2 = part[:, SEP : 2 * SEP] + side[:, SEP : 2 * SEP]
    total3 = part[:, 2 * SEP :]

    def run(first, last):
        mats = [first[0], first[1], first[2], last[0], last[1], last[2]]
        x1 = split_dot(split_dot(total1, mats[0], NT), mats[1], NT)
        picked2 = split_dot(x1, hot2[...], NN)
        x2 = split_dot(total2 - split_dot(picked2, mats[2], NT), mats[3], NT)
        picked3 = split_dot(jnp.concatenate([x1, x2], axis=1), hot3[...], NN)
        x3 = split_dot(total3 - split_dot(picked3, mats[4], NT), mats[5], NT)
        out = fold(jnp.concatenate([x1, x2, x3], axis=1)).astype(BF)
        for to in range(FRONT):
            send[to] = out

    @pl.when(core == 0)
    def _():
        run(later, swapped)

    @pl.when(core == 1)
    def _():
        run(swapped, later)


def leaf_backward_kernel(got, solved, picked, send, own, side):
    front = lax.axis_index("front")
    full = jnp.concatenate([unfold(got[k].astype(F32)) for k in range(FRONT)], axis=0).astype(BF)
    residue = (solved[...] - dot(picked[...], full, NT)).astype(BF)
    for to in range(FRONT):
        send[to] = residue
    row = lax.broadcasted_iota(jnp.int32, (96, SPAN), 0)
    column = lax.broadcasted_iota(jnp.int32, (96, SPAN), 1)
    pick = jnp.where(column == ((row >> 5) << 9) + front * ROWS + (row & 31), 1.0, 0.0).astype(BF)
    rows = dot(pick, full, NT)
    own[...] = rows
    side[...] = rows[32:96, :].astype(BF)


def finish_kernel(got, inverse, own, near, far, other, leaf_out, top_out):
    leaf = lax.axis_index("leaf")
    leaf_out[0] = dot(inverse[0], got[...].reshape(SUB, RHS), NN)
    second = leaf >> 3
    third = leaf >> 2
    top_out[0] = own[0:32, :]
    top_out[1 + second] = own[32:64, :]
    top_out[1 + (second ^ 1)] = far[0:32, :].astype(F32)
    top_out[3 + third] = own[64:96, :]
    top_out[3 + (third ^ 1)] = near[32:64, :].astype(F32)
    top_out[3 + (third ^ 2)] = far[32:64, :].astype(F32)
    top_out[3 + (third ^ 3)] = other[32:64, :].astype(F32)


VMEM = pl.BlockSpec(memory_space=pltpu.VMEM)
HBM = pl.BlockSpec(memory_space=pltpu.HBM)


def keep(x):
    return pltpu.with_memory_space_constraint(x, pltpu.HBM)


def call(kernel, outs, args, specs=None, scratch=(), flops=0, size=0):
    shapes = [jax.ShapeDtypeStruct(shape, kind) for shape, kind in outs]
    return pl.pallas_call(
        kernel,
        out_shape=shapes,
        in_specs=specs or [VMEM] * len(args),
        out_specs=[VMEM] * len(shapes),
        scratch_shapes=list(scratch),
        compiler_params=pltpu.CompilerParams(vmem_limit_bytes=16 * 1024 * 1024),
        cost_estimate=pl.CostEstimate(flops=flops, bytes_accessed=size, transcendentals=0),
    )(*args)


def swap(x, flip):
    return lax.ppermute(x, "leaf", [(i, i ^ flip) for i in range(LEAVES)])


def shifts(x, turn):
    def moved(leaf, front, k):
        y, x = front // 4, front % 4
        if (leaf + turn) % 2 == 0:
            return leaf * FRONT + y * 4 + (x + k) % 4
        return leaf * FRONT + (y + k) % 4 * 4 + x

    everyone = [(leaf, front) for leaf in range(LEAVES) for front in range(FRONT)]
    return [
        lax.ppermute(x, ("leaf", "front"), [(leaf * FRONT + front, moved(leaf, front, k)) for leaf, front in everyone])
        for k in (1, 2, 3)
    ]


def exchange(x, axis, groups=None):
    return lax.all_to_all(x, axis, 0, 0, tiled=True, axis_index_groups=groups)


def body(
    leaf_source,
    top_source,
    leaf_lower_inverse,
    leaf_upper_inverse,
    leaf_lower_block,
    leaf_upper_block,
    top_lower_inverse,
    top_upper_inverse,
    top_lower_block,
    top_upper_block,
    leaf_targets,
    top_targets,
):
    send, mats = call(
        prepare_kernel,
        [((FRONT, PIECE, RHS), BF), ((160, SEP), BF)],
        (
            keep(leaf_source),
            keep(top_lower_inverse),
            keep(top_upper_inverse),
            keep(jnp.swapaxes(top_lower_block, 1, 2)),
            keep(top_upper_block),
        ),
        specs=[HBM] * 5,
        scratch=[pltpu.VMEM((PIECE, RHS), F32), pltpu.SemaphoreType.DMA((6,))],
        size=1 << 20,
    )
    got = exchange(send, "front")
    got, mats, *parts = lax.optimization_barrier((got, mats, *shifts(mats, 0)))
    (mats,) = call(pack_kernel, [((4, 160, SEP), BF)], (mats, *parts), size=1 << 20)
    solved, send = call(
        leaf_forward_kernel,
        [((PIECE, RHS), F32), ((FRONT, 16, HALF), BF)],
        (got, leaf_lower_inverse, leaf_lower_block, leaf_targets, top_source),
        flops=2 * RHS * (PIECE * SUB + UPD * PIECE + UPD * SPAN),
        size=4 << 20,
    )
    parts = shifts(mats, 1)
    got = exchange(send, "front")
    got, *parts = lax.optimization_barrier((got, *parts))
    ahead, later = call(
        assemble_kernel, [((2, SEP, SEP), BF), ((3, SEP, SEP), BF)], (mats, *parts), size=5 << 20
    )
    send, hot2, hot3 = call(
        top_forward_kernel,
        [((16, HALF), BF), ((SEP, SEP), BF), ((2 * SEP, SEP), BF)],
        (got, ahead, swap(ahead, 1), top_targets),
        flops=2 * 256 * SEP * SEP * 8,
        size=4 << 20,
    )
    send, later = lax.optimization_barrier((send, later))
    (total,) = call(
        group_kernel, [((16, HALF), BF)], (send, swap(send, 1), swap(send, 2), swap(send, 3)), size=1 << 17
    )
    near, far, other = swap(total, 4), swap(total, 8), swap(total, 12)
    total, leaf_upper_block = lax.optimization_barrier((total, leaf_upper_block))
    (picked,) = call(
        pick_kernel,
        [((PIECE, SPAN), BF)],
        (leaf_upper_block, leaf_targets),
        flops=2 * UPD * SPAN * PIECE,
        size=2 << 20,
    )
    near, picked = lax.optimization_barrier((near, picked))
    (send,) = call(
        top_backward_kernel,
        [((FRONT, 16, HALF), BF)],
        (total, near, far, other, later, swap(later, 1), hot2, hot3),
        flops=2 * 256 * SEP * SEP * 9,
        size=5 << 20,
    )
    got = exchange(send, "front")
    send, own, side = call(
        leaf_backward_kernel,
        [((FRONT, PIECE, RHS), BF), ((96, RHS), F32), ((64, RHS), BF)],
        (got, solved, picked),
        flops=2 * RHS * 2 * PIECE * SPAN,
        size=2 << 20,
    )
    near, far, other = swap(side, 4), swap(side, 8), swap(side, 12)
    got = exchange(send, "front")
    leaf_solution, top_solution = call(
        finish_kernel,
        [((1, PIECE, RHS), F32), ((7, ROWS, RHS), F32)],
        (got, leaf_upper_inverse, own, near, far, other),
        flops=2 * RHS * PIECE * SUB,
        size=2 << 20,
    )
    return leaf_solution, top_solution


def solution(mesh):
    in_specs = (
        P("leaf", "front", None),
        P(None, "front", None),
        P("leaf", "front", None),
        P("leaf", "front", None),
        P("leaf", None, "front"),
        P("leaf", "front", None),
        P(None, "front", None),
        P(None, "front", None),
        P(None, None, "front"),
        P(None, "front", None),
        P("leaf", None),
        P(),
    )
    out_specs = (P("leaf", "front", None), P(None, "front", None))
    return jax.shard_map(body, mesh=mesh, in_specs=in_specs, out_specs=out_specs, check_vma=False)
```

profile of v0, /device:TPU:2, one launch (start us, length us, event | category | flops | bytes accessed | tf_op | source)
XLA Modules:
  0.0 101.8 jit_solution(4087937891574516680)
XLA Ops:
  0.7 1.8 %shard_map.131 = (bf16[16,128,128]{2,1,0:T(8,128)(2,1)}, bf16[160,512]{1,0:T(8,128)(2,1)S(1)}) custom-call(f32[1,128,128]{2,1,0:T(8,128)} %source.1, bf16[7,32,512]{2,1,0:T(8,128)(2,1)} %low_inv.1, bf16[7,32,512]{2,1,0:T(8,128)(2,1)} %up_inv.1, bf16[6,32,512]{2,1,0:T(8,128)(2,1)} %bitcast.1, bf16[6,32,512]{2,1,0:T(8,128)(2,1)} %up.1), custom_call_target="tpu_custom_call" | custom-call | bytes 1048576 | tf_op jit(solution)/shard_map/pallas_call | solution.py:247
  2.5 7.5 %all-to-all-start = ((bf16[16,128,128]{2,1,0:T(8,128)(2,1)}), bf16[16,128,128]{2,1,0:T(8,128)(2,1)S(1)}, u32[]{:S(2)}, u32[]{:S(2)}) async-start(bf16[16,128,128]{2,1,0:T(8,128)(2,1)} %get-tuple-element.29), calls=%async_computation | async-start | bytes 1048576 | tf_op jit(solution)/shard_map/all_to_all | solution.py:277
  10.2 2.7 %collective-permute-start.1 = (bf16[160,512]{1,0:T(8,128)(2,1)S(1)}, bf16[160,512]{1,0:T(8,128)(2,1)S(1)}, u32[]{:S(2)}, u32[]{:S(2)}) collective-permute-start(bf16[160,512]{1,0:T(8,128)(2,1)S(1)} %get-tuple-element.33.own), channel_id=1, source_target_pairs={{0,2},{1,3},{2,0},{3,1},{4,6},{5,7},{6,4},{7,5},{8,10},{9,11},{10,... | collective-permute-start | bytes 491528 | tf_op jit(solution)/shard_map/ppermute | solution.py:271
  12.9 1.8 %collective-permute-start = (bf16[160,512]{1,0:T(8,128)(2,1)S(1)}, bf16[160,512]{1,0:T(8,128)(2,1)S(1)}, u32[]{:S(2)}, u32[]{:S(2)}) collective-permute-start(bf16[160,512]{1,0:T(8,128)(2,1)S(1)} %get-tuple-element.33.own), channel_id=1, source_target_pairs={{0,1},{1,2},{2,3},{3,0},{4,5},{5,6},{6,7},{7,4},{8,9},{9,10},{10,1... | collective-permute-start | bytes 491528 | tf_op jit(solution)/shard_map/ppermute | solution.py:271
  14.7 4.5 %collective-permute-done.2.c = bf16[160,512]{1,0:T(8,128)(2,1)S(1)} collective-permute-done((bf16[160,512]{1,0:T(8,128)(2,1)S(1)}, bf16[160,512]{1,0:T(8,128)(2,1)S(1)}, u32[]{:S(2)}, u32[]{:S(2)}) %collective-permute-start.2) | collective-permute-done | bytes 163872 | tf_op jit(solution)/shard_map/ppermute | solution.py:271
  19.2 2.4 %collective-permute-done.1.b = bf16[160,512]{1,0:T(8,128)(2,1)S(1)} collective-permute-done((bf16[160,512]{1,0:T(8,128)(2,1)S(1)}, bf16[160,512]{1,0:T(8,128)(2,1)S(1)}, u32[]{:S(2)}, u32[]{:S(2)}) %collective-permute-start.1) | collective-permute-done | bytes 163872 | tf_op jit(solution)/shard_map/ppermute | solution.py:271
  21.6 2.8 %collective-permute-start.5 = (bf16[4,160,512]{2,1,0:T(8,128)(2,1)S(1)}, bf16[4,160,512]{2,1,0:T(8,128)(2,1)S(1)}, u32[]{:S(2)}, u32[]{:S(2)}) collective-permute-start(bf16[4,160,512]{2,1,0:T(8,128)(2,1)S(1)} %shard_map.133.own), channel_id=1, source_target_pairs={{0,12},{1,13},{2,14},{3,15},{4,0},{5,1},{6,2},{7,3},{8,4},{9,5},{1... | collective-permute-start | bytes 1966088 | tf_op jit(solution)/shard_map/ppermute | solution.py:271
  26.1 1.7 %shard_map.132 = (f32[128,128]{1,0:T(8,128)S(1)}, bf16[16,16,768]{2,1,0:T(8,128)(2,1)S(1)}) custom-call(bf16[16,128,128]{2,1,0:T(8,128)(2,1)S(1)} %all-to-all-done.got, bf16[1,128,2048]{2,1,0:T(8,128)(2,1)S(1)} %copy-done.1, bf16[1,1024,128]{2,1,0:T(8,128)(2,1)S(1)} %copy-done.2, s32[1,1024]{1,0:T(1,128)S(1)} %copy-done.6, f32[7,32,128]{2,1,0:T(8,128)S(1)} %copy-done.4), custom_call_target="tpu_custom_call" | custom-call | flops 503316480 | bytes 4194304 | tf_op jit(solution)/shard_map/pallas_call | solution.py:247
  27.8 20.0 %all_to_all.20.got = bf16[16,16,768]{2,1,0:T(8,128)(2,1)S(1)} all-to-all(bf16[16,16,768]{2,1,0:T(8,128)(2,1)S(1)} %get-tuple-element.32), channel_id=1, replica_groups=mesh['leaf'=16,'front'=16] {'front'}, dimensions={0} | all-to-all | bytes 786432 | tf_op jit(solution)/shard_map/all_to_all | solution.py:277
  48.1 2.6 %collective-permute-done.6.swapped = bf16[2,512,512]{2,1,0:T(8,128)(2,1)S(1)} collective-permute-done((bf16[2,512,512]{2,1,0:T(8,128)(2,1)S(1)}, bf16[2,512,512]{2,1,0:T(8,128)(2,1)S(1)}, u32[]{:S(2)}, u32[]{:S(2)}) %collective-permute-start.6) | collective-permute-done | bytes 1048608 | tf_op jit(solution)/shard_map/ppermute | solution.py:259
  50.7 1.6 %shard_map.135 = (bf16[16,768]{1,0:T(8,128)(2,1)S(1)}, bf16[512,512]{1,0:T(8,128)(2,1)S(1)}, bf16[1024,512]{1,0:T(8,128)(2,1)S(1)}) custom-call(bf16[16,16,768]{2,1,0:T(8,128)(2,1)S(1)} %all_to_all.20.got, bf16[2,512,512]{2,1,0:T(8,128)(2,1)S(1)} %get-tuple-element.41.first, bf16[2,512,512]{2,1,0:T(8,128)(2,1)S(1)} %collective-permute-done.6.swapped, ...), custom_call_target="tpu_custom_call" | custom-call | flops 1073741824 | bytes 4194304 | tf_op jit(solution)/shard_map/pallas_call | solution.py:247
  52.5 1.9 %collective-permute-start.9 = (bf16[16,768]{1,0:T(8,128)(2,1)S(1)}, bf16[16,768]{1,0:T(8,128)(2,1)S(1)}, u32[]{:S(2)}, u32[]{:S(2)}) collective-permute-start(bf16[16,768]{1,0:T(8,128)(2,1)S(1)} %get-tuple-element.44.own), channel_id=1, source_target_pairs={{0,48},{16,32},{32,16},{48,0},{64,112},{80,96},{96,80},{112,64},{1... | collective-permute-start | bytes 73736 | tf_op jit(solution)/shard_map/ppermute | solution.py:259
  54.5 1.3 %collective-permute-done.9.c = bf16[16,768]{1,0:T(8,128)(2,1)S(1)} collective-permute-done((bf16[16,768]{1,0:T(8,128)(2,1)S(1)}, bf16[16,768]{1,0:T(8,128)(2,1)S(1)}, u32[]{:S(2)}, u32[]{:S(2)}) %collective-permute-start.9) | collective-permute-done | bytes 24608 | tf_op jit(solution)/shard_map/ppermute | solution.py:259
  55.9 2.3 %collective-permute-done.8.b = bf16[16,768]{1,0:T(8,128)(2,1)S(1)} collective-permute-done((bf16[16,768]{1,0:T(8,128)(2,1)S(1)}, bf16[16,768]{1,0:T(8,128)(2,1)S(1)}, u32[]{:S(2)}, u32[]{:S(2)}) %collective-permute-start.8) | collective-permute-done | bytes 24608 | tf_op jit(solution)/shard_map/ppermute | solution.py:259
  58.2 5.5 %collective-permute-start.12 = (bf16[16,768]{1,0:T(8,128)(2,1)S(1)}, bf16[16,768]{1,0:T(8,128)(2,1)S(1)}, u32[]{:S(2)}, u32[]{:S(2)}) collective-permute-start(bf16[16,768]{1,0:T(8,128)(2,1)S(1)} %shard_map.136.own), channel_id=1, source_target_pairs={{0,192},{16,208},{32,224},{48,240},{64,128},{80,144},{96,160},{112... | collective-permute-start | bytes 73736 | tf_op jit(solution)/shard_map/ppermute | solution.py:259
  63.7 1.4 %collective-permute-start.11 = (bf16[16,768]{1,0:T(8,128)(2,1)S(1)}, bf16[16,768]{1,0:T(8,128)(2,1)S(1)}, u32[]{:S(2)}, u32[]{:S(2)}) collective-permute-start(bf16[16,768]{1,0:T(8,128)(2,1)S(1)} %shard_map.136.own), channel_id=1, source_target_pairs={{0,128},{16,144},{32,160},{48,176},{64,192},{80,208},{96,224},{112... | collective-permute-start | bytes 73736 | tf_op jit(solution)/shard_map/ppermute | solution.py:259
  67.3 2.9 %collective-permute-done.10.near = bf16[16,768]{1,0:T(8,128)(2,1)S(1)} collective-permute-done((bf16[16,768]{1,0:T(8,128)(2,1)S(1)}, bf16[16,768]{1,0:T(8,128)(2,1)S(1)}, u32[]{:S(2)}, u32[]{:S(2)}) %collective-permute-start.10) | collective-permute-done | bytes 24608 | tf_op jit(solution)/shard_map/ppermute | solution.py:259
  71.4 1.5 %shard_map.138 = bf16[16,16,768]{2,1,0:T(8,128)(2,1)S(1)} custom-call(bf16[16,768]{1,0:T(8,128)(2,1)S(1)} %shard_map.136.own, bf16[16,768]{1,0:T(8,128)(2,1)S(1)} %collective-permute-done.10.near, bf16[16,768]{1,0:T(8,128)(2,1)S(1)} %collective-permute-done.11.far, bf16[16,768]{1,0:T(8,128)(2,1)S(1)} %collective-permute-done.12.other, ...), custom_call_target="tpu_custom_call" | custom-call | flops 1207959552 | bytes 5242880 | tf_op jit(solution)/shard_map/pallas_call | solution.py:247
  73.0 12.2 %all_to_all.21.got = bf16[16,16,768]{2,1,0:T(8,128)(2,1)S(1)} all-to-all(bf16[16,16,768]{2,1,0:T(8,128)(2,1)S(1)} %shard_map.138), channel_id=1, replica_groups=mesh['leaf'=16,'front'=16] {'front'}, dimensions={0} | all-to-all | bytes 786432 | tf_op jit(solution)/shard_map/all_to_all | solution.py:277
  86.4 4.8 %all-to-all-start.3 = ((bf16[16,128,128]{2,1,0:T(8,128)(2,1)}), bf16[16,128,128]{2,1,0:T(8,128)(2,1)S(1)}, u32[]{:S(2)}, u32[]{:S(2)}) async-start(bf16[16,128,128]{2,1,0:T(8,128)(2,1)} %get-tuple-element.53), calls=%async_computation.3 | async-start | bytes 1048576 | tf_op jit(solution)/shard_map/all_to_all | solution.py:277
  91.2 2.0 %collective-permute-start.16 = (bf16[64,128]{1,0:T(8,128)(2,1)S(1)}, bf16[64,128]{1,0:T(8,128)(2,1)S(1)}, u32[]{:S(2)}, u32[]{:S(2)}) collective-permute-start(bf16[64,128]{1,0:T(8,128)(2,1)S(1)} %get-tuple-element.55), channel_id=1, source_target_pairs={{0,192},{16,208},{32,224},{48,240},{64,128},{80,144},{96,160},{112... | collective-permute-start | bytes 49160 | tf_op jit(solution)/shard_map/ppermute | solution.py:259
  93.2 3.0 %collective-permute-start.15 = (bf16[64,128]{1,0:T(8,128)(2,1)S(1)}, bf16[64,128]{1,0:T(8,128)(2,1)S(1)}, u32[]{:S(2)}, u32[]{:S(2)}) collective-permute-start(bf16[64,128]{1,0:T(8,128)(2,1)S(1)} %get-tuple-element.55), channel_id=1, source_target_pairs={{0,128},{16,144},{32,160},{48,176},{64,192},{80,208},{96,224},{112... | collective-permute-start | bytes 49160 | tf_op jit(solution)/shard_map/ppermute | solution.py:259
  96.2 1.5 %collective-permute-start.14 = (bf16[64,128]{1,0:T(8,128)(2,1)S(1)}, bf16[64,128]{1,0:T(8,128)(2,1)S(1)}, u32[]{:S(2)}, u32[]{:S(2)}) collective-permute-start(bf16[64,128]{1,0:T(8,128)(2,1)S(1)} %get-tuple-element.55), channel_id=1, source_target_pairs={{0,64},{16,80},{32,96},{48,112},{64,0},{80,16},{96,32},{112,48},{1... | collective-permute-start | bytes 49160 | tf_op jit(solution)/shard_map/ppermute | solution.py:259
  97.7 3.2 %collective-permute-done.15.far = bf16[64,128]{1,0:T(8,128)(2,1)S(1)} collective-permute-done((bf16[64,128]{1,0:T(8,128)(2,1)S(1)}, bf16[64,128]{1,0:T(8,128)(2,1)S(1)}, u32[]{:S(2)}, u32[]{:S(2)}) %collective-permute-start.15) | collective-permute-done | bytes 16416 | tf_op jit(solution)/shard_map/ppermute | solution.py:259
  (40 shorter events, 8.2 us)
Async XLA Ops:
  0.6 25.5 %copy-start.1 = (bf16[1,128,2048]{2,1,0:T(8,128)(2,1)S(1)}, bf16[1,128,2048]{2,1,0:T(8,128)(2,1)}, u32[]{:S(2)}) copy-start(bf16[1,128,2048]{2,1,0:T(8,128)(2,1)} %inverse.2) | copy-start | bytes 1572868
  0.6 25.5 %copy-start.2 = (bf16[1,1024,128]{2,1,0:T(8,128)(2,1)S(1)}, bf16[1,1024,128]{2,1,0:T(8,128)(2,1)}, u32[]{:S(2)}) copy-start(bf16[1,1024,128]{2,1,0:T(8,128)(2,1)} %block.1) | copy-start | bytes 786436
  0.7 25.5 %copy-start.4 = (f32[7,32,128]{2,1,0:T(8,128)S(1)}, f32[7,32,128]{2,1,0:T(8,128)}, u32[]{:S(2)}) copy-start(f32[7,32,128]{2,1,0:T(8,128)} %top.1) | copy-start | bytes 344068
  0.7 25.5 %copy-start.6 = (s32[1,1024]{1,0:T(1,128)S(1)}, s32[1,1024]{1,0:T(1,128)}, u32[]{:S(2)}) copy-start(s32[1,1024]{1,0:T(1,128)} %targets.5) | copy-start | bytes 12292
  2.5 19.1 %all-to-all-start = ((bf16[16,128,128]{2,1,0:T(8,128)(2,1)}), bf16[16,128,128]{2,1,0:T(8,128)(2,1)S(1)}, u32[]{:S(2)}, u32[]{:S(2)}) async-start(bf16[16,128,128]{2,1,0:T(8,128)(2,1)} %get-tuple-element.29), calls=%async_computation | async-start | bytes 1048576 | tf_op jit(solution)/shard_map/all_to_all | solution.py:277
  10.0 9.2 %collective-permute-start.2 = (bf16[160,512]{1,0:T(8,128)(2,1)S(1)}, bf16[160,512]{1,0:T(8,128)(2,1)S(1)}, u32[]{:S(2)}, u32[]{:S(2)}) collective-permute-start(bf16[160,512]{1,0:T(8,128)(2,1)S(1)} %get-tuple-element.33.own), channel_id=1, source_target_pairs={{0,3},{1,0},{2,1},{3,2},{4,7},{5,4},{6,5},{7,6},{8,11},{9,8},{10,9... | collective-permute-start | bytes 491528 | tf_op jit(solution)/shard_map/ppermute | solution.py:271
  10.2 11.4 %collective-permute-start.1 = (bf16[160,512]{1,0:T(8,128)(2,1)S(1)}, bf16[160,512]{1,0:T(8,128)(2,1)S(1)}, u32[]{:S(2)}, u32[]{:S(2)}) collective-permute-start(bf16[160,512]{1,0:T(8,128)(2,1)S(1)} %get-tuple-element.33.own), channel_id=1, source_target_pairs={{0,2},{1,3},{2,0},{3,1},{4,6},{5,7},{6,4},{7,5},{8,10},{9,11},{10,... | collective-permute-start | bytes 491528 | tf_op jit(solution)/shard_map/ppermute | solution.py:271
  12.9 8.6 %collective-permute-start = (bf16[160,512]{1,0:T(8,128)(2,1)S(1)}, bf16[160,512]{1,0:T(8,128)(2,1)S(1)}, u32[]{:S(2)}, u32[]{:S(2)}) collective-permute-start(bf16[160,512]{1,0:T(8,128)(2,1)S(1)} %get-tuple-element.33.own), channel_id=1, source_target_pairs={{0,1},{1,2},{2,3},{3,0},{4,5},{5,6},{6,7},{7,4},{8,9},{9,10},{10,1... | collective-permute-start | bytes 491528 | tf_op jit(solution)/shard_map/ppermute | solution.py:271
  21.6 26.1 %collective-permute-start.5 = (bf16[4,160,512]{2,1,0:T(8,128)(2,1)S(1)}, bf16[4,160,512]{2,1,0:T(8,128)(2,1)S(1)}, u32[]{:S(2)}, u32[]{:S(2)}) collective-permute-start(bf16[4,160,512]{2,1,0:T(8,128)(2,1)S(1)} %shard_map.133.own), channel_id=1, source_target_pairs={{0,12},{1,13},{2,14},{3,15},{4,0},{5,1},{6,2},{7,3},{8,4},{9,5},{1... | collective-permute-start | bytes 1966088 | tf_op jit(solution)/shard_map/ppermute | solution.py:271
  24.4 23.4 %collective-permute-start.4 = (bf16[4,160,512]{2,1,0:T(8,128)(2,1)S(1)}, bf16[4,160,512]{2,1,0:T(8,128)(2,1)S(1)}, u32[]{:S(2)}, u32[]{:S(2)}) collective-permute-start(bf16[4,160,512]{2,1,0:T(8,128)(2,1)S(1)} %shard_map.133.own), channel_id=1, source_target_pairs={{0,8},{1,9},{2,10},{3,11},{4,12},{5,13},{6,14},{7,15},{8,0},{9,1},... | collective-permute-start | bytes 1966088 | tf_op jit(solution)/shard_map/ppermute | solution.py:271
  25.2 22.5 %collective-permute-start.3 = (bf16[4,160,512]{2,1,0:T(8,128)(2,1)S(1)}, bf16[4,160,512]{2,1,0:T(8,128)(2,1)S(1)}, u32[]{:S(2)}, u32[]{:S(2)}) collective-permute-start(bf16[4,160,512]{2,1,0:T(8,128)(2,1)S(1)} %shard_map.133.own), channel_id=1, source_target_pairs={{0,4},{1,5},{2,6},{3,7},{4,8},{5,9},{6,10},{7,11},{8,12},{9,13},{1... | collective-permute-start | bytes 1966088 | tf_op jit(solution)/shard_map/ppermute | solution.py:271
  48.0 2.7 %collective-permute-start.6 = (bf16[2,512,512]{2,1,0:T(8,128)(2,1)S(1)}, bf16[2,512,512]{2,1,0:T(8,128)(2,1)S(1)}, u32[]{:S(2)}, u32[]{:S(2)}) collective-permute-start(bf16[2,512,512]{2,1,0:T(8,128)(2,1)S(1)} %get-tuple-element.41.first), channel_id=1, source_target_pairs={{0,16},{16,0},{32,48},{48,32},{64,80},{80,64},{96,112},{112,96},{1... | collective-permute-start | bytes 3145736 | tf_op jit(solution)/shard_map/ppermute | solution.py:259
  52.3 19.1 %collective-permute-start.13 = (bf16[3,512,512]{2,1,0:T(8,128)(2,1)S(1)}, bf16[3,512,512]{2,1,0:T(8,128)(2,1)S(1)}, u32[]{:S(2)}, u32[]{:S(2)}) collective-permute-start(bf16[3,512,512]{2,1,0:T(8,128)(2,1)S(1)} %get-tuple-element.48.later), channel_id=1, source_target_pairs={{0,16},{16,0},{32,48},{48,32},{64,80},{80,64},{96,112},{112,96},{1... | collective-permute-start | bytes 4718600 | tf_op jit(solution)/shard_map/ppermute | solution.py:259
  52.5 3.4 %collective-permute-start.9 = (bf16[16,768]{1,0:T(8,128)(2,1)S(1)}, bf16[16,768]{1,0:T(8,128)(2,1)S(1)}, u32[]{:S(2)}, u32[]{:S(2)}) collective-permute-start(bf16[16,768]{1,0:T(8,128)(2,1)S(1)} %get-tuple-element.44.own), channel_id=1, source_target_pairs={{0,48},{16,32},{32,16},{48,0},{64,112},{80,96},{96,80},{112,64},{1... | collective-permute-start | bytes 73736 | tf_op jit(solution)/shard_map/ppermute | solution.py:259
  54.4 3.8 %collective-permute-start.8 = (bf16[16,768]{1,0:T(8,128)(2,1)S(1)}, bf16[16,768]{1,0:T(8,128)(2,1)S(1)}, u32[]{:S(2)}, u32[]{:S(2)}) collective-permute-start(bf16[16,768]{1,0:T(8,128)(2,1)S(1)} %get-tuple-element.44.own), channel_id=1, source_target_pairs={{0,32},{16,48},{32,0},{48,16},{64,96},{80,112},{96,64},{112,80},{1... | collective-permute-start | bytes 73736 | tf_op jit(solution)/shard_map/ppermute | solution.py:259
  54.5 3.7 %collective-permute-start.7 = (bf16[16,768]{1,0:T(8,128)(2,1)S(1)}, bf16[16,768]{1,0:T(8,128)(2,1)S(1)}, u32[]{:S(2)}, u32[]{:S(2)}) collective-permute-start(bf16[16,768]{1,0:T(8,128)(2,1)S(1)} %get-tuple-element.44.own), channel_id=1, source_target_pairs={{0,16},{16,0},{32,48},{48,32},{64,80},{80,64},{96,112},{112,96},{1... | collective-permute-start | bytes 73736 | tf_op jit(solution)/shard_map/ppermute | solution.py:259
  58.2 12.0 %collective-permute-start.12 = (bf16[16,768]{1,0:T(8,128)(2,1)S(1)}, bf16[16,768]{1,0:T(8,128)(2,1)S(1)}, u32[]{:S(2)}, u32[]{:S(2)}) collective-permute-start(bf16[16,768]{1,0:T(8,128)(2,1)S(1)} %shard_map.136.own), channel_id=1, source_target_pairs={{0,192},{16,208},{32,224},{48,240},{64,128},{80,144},{96,160},{112... | collective-permute-start | bytes 73736 | tf_op jit(solution)/shard_map/ppermute | solution.py:259
  63.7 7.7 %collective-permute-start.11 = (bf16[16,768]{1,0:T(8,128)(2,1)S(1)}, bf16[16,768]{1,0:T(8,128)(2,1)S(1)}, u32[]{:S(2)}, u32[]{:S(2)}) collective-permute-start(bf16[16,768]{1,0:T(8,128)(2,1)S(1)} %shard_map.136.own), channel_id=1, source_target_pairs={{0,128},{16,144},{32,160},{48,176},{64,192},{80,208},{96,224},{112... | collective-permute-start | bytes 73736 | tf_op jit(solution)/shard_map/ppermute | solution.py:259
  65.1 5.1 %collective-permute-start.10 = (bf16[16,768]{1,0:T(8,128)(2,1)S(1)}, bf16[16,768]{1,0:T(8,128)(2,1)S(1)}, u32[]{:S(2)}, u32[]{:S(2)}) collective-permute-start(bf16[16,768]{1,0:T(8,128)(2,1)S(1)} %shard_map.136.own), channel_id=1, source_target_pairs={{0,64},{16,80},{32,96},{48,112},{64,0},{80,16},{96,32},{112,48},{1... | collective-permute-start | bytes 73736 | tf_op jit(solution)/shard_map/ppermute | solution.py:259
  73.0 27.9 %copy-start = (bf16[1,128,2048]{2,1,0:T(8,128)(2,1)S(1)}, bf16[1,128,2048]{2,1,0:T(8,128)(2,1)}, u32[]{:S(2)}) copy-start(bf16[1,128,2048]{2,1,0:T(8,128)(2,1)} %inverse.3) | copy-start | bytes 1572868
  86.4 14.5 %all-to-all-start.3 = ((bf16[16,128,128]{2,1,0:T(8,128)(2,1)}), bf16[16,128,128]{2,1,0:T(8,128)(2,1)S(1)}, u32[]{:S(2)}, u32[]{:S(2)}) async-start(bf16[16,128,128]{2,1,0:T(8,128)(2,1)} %get-tuple-element.53), calls=%async_computation.3 | async-start | bytes 1048576 | tf_op jit(solution)/shard_map/all_to_all | solution.py:277
  91.2 6.5 %collective-permute-start.16 = (bf16[64,128]{1,0:T(8,128)(2,1)S(1)}, bf16[64,128]{1,0:T(8,128)(2,1)S(1)}, u32[]{:S(2)}, u32[]{:S(2)}) collective-permute-start(bf16[64,128]{1,0:T(8,128)(2,1)S(1)} %get-tuple-element.55), channel_id=1, source_target_pairs={{0,192},{16,208},{32,224},{48,240},{64,128},{80,144},{96,160},{112... | collective-permute-start | bytes 49160 | tf_op jit(solution)/shard_map/ppermute | solution.py:259
  93.2 7.6 %collective-permute-start.15 = (bf16[64,128]{1,0:T(8,128)(2,1)S(1)}, bf16[64,128]{1,0:T(8,128)(2,1)S(1)}, u32[]{:S(2)}, u32[]{:S(2)}) collective-permute-start(bf16[64,128]{1,0:T(8,128)(2,1)S(1)} %get-tuple-element.55), channel_id=1, source_target_pairs={{0,128},{16,144},{32,160},{48,176},{64,192},{80,208},{96,224},{112... | collective-permute-start | bytes 49160 | tf_op jit(solution)/shard_map/ppermute | solution.py:259
  96.2 4.7 %collective-permute-start.14 = (bf16[64,128]{1,0:T(8,128)(2,1)S(1)}, bf16[64,128]{1,0:T(8,128)(2,1)S(1)}, u32[]{:S(2)}, u32[]{:S(2)}) collective-permute-start(bf16[64,128]{1,0:T(8,128)(2,1)S(1)} %get-tuple-element.55), channel_id=1, source_target_pairs={{0,64},{16,80},{32,96},{48,112},{64,0},{80,16},{96,32},{112,48},{1... | collective-permute-start | bytes 49160 | tf_op jit(solution)/shard_map/ppermute | solution.py:259
  (2 other events, 41.1 us)
where the time goes:
time: 102 us
  starting transfers between devices  38.3 us (38%)
  blocking collectives  32.1 us (31%)
  waiting for transfers between devices  20.5 us (20%)
  Pallas kernels  10.1 us (10%)
    all_to_all x2, blocking collectives, exchange(): return lax.all_to_all(x, axis, 0, 0, tiled=True, axis_index_groups=groups)  32.1 us
    ppermute x11, starting transfers between devices, swap(): return lax.ppermute(x, 'leaf', [(i, i ^ flip) for i in range(LEAVES)])  16.8 us
    ppermute x11, waiting for transfers between devices, swap(): return lax.ppermute(x, 'leaf', [(i, i ^ flip) for i in range(LEAVES)])  13.6 us
    all_to_all x2, starting transfers between devices, exchange(): return lax.all_to_all(x, axis, 0, 0, tiled=True, axis_index_groups=groups)  12.3 us
    pallas_call x10, Pallas kernels, call(): pl.pallas_call(kernel, out_shape=shapes, in_specs=specs or [VMEM] * len(a...  10.1 us
    ppermute x6, starting transfers between devices, shifts(): lax.ppermute(x, ('leaf', 'front'), [(leaf * FRONT + front, moved(leaf, fr...  9.17 us
    ppermute x6, waiting for transfers between devices, shifts(): lax.ppermute(x, ('leaf', 'front'), [(leaf * FRONT + front, moved(leaf, fr...  6.88 us
  transfers between devices with their start and end apart: 19, of which 8 were waited for; matrix products, arithmetic and copies ran while one was open for 0% of the time, Pallas kernels for 3%

commit v1 on v0

--- a/solution.py
+++ b/solution.py
@@ -33,7 +33,8 @@
 
 
 def fold(x):
-    return jnp.concatenate([x[:, :HALF], x[:, HALF:]], axis=0)
+    half = x.shape[1] // 2
+    return jnp.concatenate([x[:, :half], x[:, half:]], axis=0)
 
 
 def unfold(x):
@@ -90,7 +91,7 @@
         out[k] = ref[...]
 
 
-def assemble_kernel(own, a, b, c, ahead, later):
+def assemble_kernel(own, a, b, c, ahead, second, later):
     front = lax.axis_index("front")
     core = lax.axis_index("leaf") & 1
     y, x = front >> 2, front & 3
@@ -103,7 +104,7 @@
             for i in range(5):
                 part = ref[k, i * ROWS : i * ROWS + ROWS, :]
                 if i < 2:
-                    ahead[i, rows, :] = part
+                    (ahead, second)[i][rows, :] = part
                 else:
                     later[i - 2, rows, :] = part
 
@@ -115,12 +116,18 @@
         picked[:, rows] = dot(block[0], one_hot(part * SEP, SEP, places), NT).astype(BF)
 
 
-def leaf_forward_kernel(got, inverse, block, targets, top, solved_out, send):
+def spread_kernel(block, targets, spread):
+    places = leaf_places(targets[...])
+    for part in range(3):
+        hot = one_hot(part * SEP, SEP, places)
+        spread[part * SEP : part * SEP + SEP, :] = dot(hot, block[0], NN).astype(BF)
+
+
+def leaf_forward_kernel(got, inverse, spread, top, solved_out, send):
     leaf = lax.axis_index("leaf")
     front = lax.axis_index("front")
     solved = dot(inverse[0], got[...].reshape(SUB, RHS), NN)
     solved_out[...] = solved
-    update = dot(solved.T.astype(BF), block[0], NT)
     own = jnp.concatenate(
         [
             top[0] * (1 / 16),
@@ -130,15 +137,12 @@
         ],
         axis=0,
     ).T
-    lhs = jnp.concatenate([-update, own], axis=1).astype(BF)
-    lane = lax.broadcasted_iota(jnp.int32, (1, RHS), 1)
-    top_places = jnp.where(lane < 96, ((lane >> 5) << 9) + front * ROWS + (lane & 31), -1)
-    places = jnp.concatenate([leaf_places(targets[...]), top_places], axis=1)
-    low = dot(lhs, one_hot(0, HALF, places), NT)
-    high = dot(lhs, one_hot(HALF, HALF, places), NT)
+    row = lax.broadcasted_iota(jnp.int32, (RHS, SPAN), 0)
+    column = lax.broadcasted_iota(jnp.int32, (RHS, SPAN), 1)
+    hot = jnp.where(column == ((row >> 5) << 9) + front * ROWS + (row & 31), 1.0, 0.0).astype(BF)
+    total = dot(own.astype(BF), hot, NN) - dot(solved.T.astype(BF), spread[...], NT)
     for to in range(FRONT):
-        rows = slice(to * 8, to * 8 + 8)
-        send[to] = jnp.concatenate([low[rows], high[rows]], axis=0).astype(BF)
+        send[to] = fold(total[to * 8 : to * 8 + 8]).astype(BF)
 
 
 def top_forward_kernel(got, first, swapped, targets, send, hot2, hot3):
@@ -151,17 +155,10 @@
     total = unfold(total)
 
     def run(even, odd):
-        target1 = total[:, :SEP]
-        target2 = total[:, SEP : 2 * SEP]
-        solved3 = split_dot(total[:, 2 * SEP :], even[0], NT)
-        update3 = split_dot(solved3, odd[0], NN)
-        spread3 = split_dot(update3, hot3[...], NT)
-        target1 = target1 - spread3[:, :SEP]
-        target2 = target2 - spread3[:, SEP:]
-        solved2 = split_dot(target2, even[1], NT)
-        update2 = split_dot(solved2, odd[1], NN)
-        target1 = target1 - split_dot(update2, hot2[...], NT)
-        send[...] = fold(jnp.concatenate([target1, solved2, solved3], axis=1)).astype(BF)
+        solved3 = split_dot(total[:, 2 * SEP :], even[...], NT)
+        update3 = split_dot(solved3, odd[...], NN)
+        above = total[:, : 2 * SEP] - split_dot(update3, hot3[...], NT)
+        send[...] = fold(jnp.concatenate([above, solved3], axis=1)).astype(BF)
 
     @pl.when((leaf & 1) == 0)
     def _():
@@ -172,17 +169,33 @@
         run(swapped, first)
 
 
-def group_kernel(own, a, b, c, send):
+def group_kernel(own, a, b, c, first, swapped, hot2, far, near, other):
+    core = lax.axis_index("leaf") & 1
     total = (own[...].astype(F32) + a[...].astype(F32)) + (b[...].astype(F32) + c[...].astype(F32))
-    send[...] = total.astype(BF)
+    total = unfold(total)
+
+    def run(even, odd):
+        solved2 = split_dot(total[:, SEP : 2 * SEP], even[...], NT)
+        update2 = split_dot(solved2, odd[...], NN)
+        target1 = total[:, :SEP] - split_dot(update2, hot2[...], NT)
+        far[...] = fold(jnp.concatenate([target1, solved2, total[:, 2 * SEP :]], axis=1)).astype(BF)
+        near[...] = fold(jnp.concatenate([target1, solved2], axis=1)).astype(BF)
+        other[...] = fold(target1).astype(BF)
+
+    @pl.when(core == 0)
+    def _():
+        run(first, swapped)
+
+    @pl.when(core == 1)
+    def _():
+        run(swapped, first)
 
 
 def top_backward_kernel(own, near, far, other, later, swapped, hot2, hot3, send):
     core = lax.axis_index("leaf") & 1
     part = unfold(own[...].astype(F32))
     side = unfold(near[...].astype(F32))
-    rest = unfold(far[...].astype(F32) + other[...].astype(F32))
-    total1 = part[:, :SEP] + side[:, :SEP] + rest[:, :SEP]
+    total1 = part[:, :SEP] + side[:, :SEP] + unfold(far[...].astype(F32))[:, :SEP] + unfold(other[...].astype(F32))
     total2 = part[:, SEP : 2 * SEP] + side[:, SEP : 2 * SEP]
     total3 = part[:, 2 * SEP :]
 
@@ -206,7 +219,7 @@
         run(swapped, later)
 
 
-def leaf_backward_kernel(got, solved, picked, send, own, side):
+def leaf_backward_kernel(got, solved, picked, send, own, side, last):
     front = lax.axis_index("front")
     full = jnp.concatenate([unfold(got[k].astype(F32)) for k in range(FRONT)], axis=0).astype(BF)
     residue = (solved[...] - dot(picked[...], full, NT)).astype(BF)
@@ -218,6 +231,7 @@
     rows = dot(pick, full, NT)
     own[...] = rows
     side[...] = rows[32:96, :].astype(BF)
+    last[...] = rows[64:96, :].astype(BF)
 
 
 def finish_kernel(got, inverse, own, near, far, other, leaf_out, top_out):
@@ -229,9 +243,9 @@
     top_out[1 + second] = own[32:64, :]
     top_out[1 + (second ^ 1)] = far[0:32, :].astype(F32)
     top_out[3 + third] = own[64:96, :]
-    top_out[3 + (third ^ 1)] = near[32:64, :].astype(F32)
+    top_out[3 + (third ^ 1)] = near[...].astype(F32)
     top_out[3 + (third ^ 2)] = far[32:64, :].astype(F32)
-    top_out[3 + (third ^ 3)] = other[32:64, :].astype(F32)
+    top_out[3 + (third ^ 3)] = other[...].astype(F32)
 
 
 VMEM = pl.BlockSpec(memory_space=pltpu.VMEM)
@@ -305,34 +319,49 @@
         scratch=[pltpu.VMEM((PIECE, RHS), F32), pltpu.SemaphoreType.DMA((6,))],
         size=1 << 20,
     )
+    leaf_lower_block, send = lax.optimization_barrier((leaf_lower_block, send))
+    (spread,) = call(
+        spread_kernel,
+        [((SPAN, PIECE), BF)],
+        (leaf_lower_block, leaf_targets),
+        flops=2 * UPD * SPAN * PIECE,
+        size=2 << 20,
+    )
     got = exchange(send, "front")
-    got, mats, *parts = lax.optimization_barrier((got, mats, *shifts(mats, 0)))
+    got, mats, spread, *parts = lax.optimization_barrier((got, mats, spread, *shifts(mats, 0)))
     (mats,) = call(pack_kernel, [((4, 160, SEP), BF)], (mats, *parts), size=1 << 20)
     solved, send = call(
         leaf_forward_kernel,
         [((PIECE, RHS), F32), ((FRONT, 16, HALF), BF)],
-        (got, leaf_lower_inverse, leaf_lower_block, leaf_targets, top_source),
-        flops=2 * RHS * (PIECE * SUB + UPD * PIECE + UPD * SPAN),
+        (got, leaf_lower_inverse, spread, top_source),
+        flops=2 * RHS * (PIECE * SUB + 2 * PIECE * SPAN),
         size=4 << 20,
     )
     parts = shifts(mats, 1)
     got = exchange(send, "front")
     got, *parts = lax.optimization_barrier((got, *parts))
-    ahead, later = call(
-        assemble_kernel, [((2, SEP, SEP), BF), ((3, SEP, SEP), BF)], (mats, *parts), size=5 << 20
+    ahead, second, later = call(
+        assemble_kernel,
+        [((SEP, SEP), BF), ((SEP, SEP), BF), ((3, SEP, SEP), BF)],
+        (mats, *parts),
+        size=5 << 20,
     )
     send, hot2, hot3 = call(
         top_forward_kernel,
         [((16, HALF), BF), ((SEP, SEP), BF), ((2 * SEP, SEP), BF)],
         (got, ahead, swap(ahead, 1), top_targets),
-        flops=2 * 256 * SEP * SEP * 8,
+        flops=2 * 256 * SEP * SEP * 4,
         size=4 << 20,
     )
-    send, later = lax.optimization_barrier((send, later))
-    (total,) = call(
-        group_kernel, [((16, HALF), BF)], (send, swap(send, 1), swap(send, 2), swap(send, 3)), size=1 << 17
-    )
-    near, far, other = swap(total, 4), swap(total, 8), swap(total, 12)
+    send, second, later = lax.optimization_barrier((send, second, later))
+    total, near, other = call(
+        group_kernel,
+        [((16, HALF), BF), ((16, SEP), BF), ((16, SEP // 2), BF)],
+        (send, swap(send, 1), swap(send, 2), swap(send, 3), second, swap(second, 1), hot2),
+        flops=2 * 256 * SEP * SEP * 3,
+        size=2 << 20,
+    )
+    near, far, other = swap(near, 4), swap(total, 8), swap(other, 12)
     total, leaf_upper_block = lax.optimization_barrier((total, leaf_upper_block))
     (picked,) = call(
         pick_kernel,
@@ -350,14 +379,14 @@
         size=5 << 20,
     )
     got = exchange(send, "front")
-    send, own, side = call(
+    send, own, side, last = call(
         leaf_backward_kernel,
-        [((FRONT, PIECE, RHS), BF), ((96, RHS), F32), ((64, RHS), BF)],
+        [((FRONT, PIECE, RHS), BF), ((96, RHS), F32), ((64, RHS), BF), ((32, RHS), BF)],
         (got, solved, picked),
         flops=2 * RHS * 2 * PIECE * SPAN,
         size=2 << 20,
     )
-    near, far, other = swap(side, 4), swap(side, 8), swap(side, 12)
+    near, far, other = swap(last, 4), swap(side, 8), swap(last, 12)
     got = exchange(send, "front")
     leaf_solution, top_solution = call(
         finish_kernel,

time: 102 us -> 101 us (level)
  waiting for transfers between devices: 20.5 us -> 17.5 us
  blocking collectives: 32.1 us -> 33.2 us
    ppermute x11 -> x12, waiting for transfers between devices: 13.6 us -> 11.7 us  [swap(): return lax.ppermute(x, 'leaf', [(i, i ^ flip) for i in range(LEAVES)])]
    all_to_all x2, blocking collectives: 32.1 us -> 33.2 us  [exchange(): return lax.all_to_all(x, axis, 0, 0, tiled=True, axis_index_groups=groups)]
    ppermute x6, waiting for transfers between devices: 6.88 us -> 5.79 us  [shifts(): lax.ppermute(x, ('leaf', 'front'), [(leaf * FRONT + front, moved(leaf, fr...]
    ppermute x11 -> x12, starting transfers between devices: 16.8 us -> 17 us  [swap(): return lax.ppermute(x, 'leaf', [(i, i ^ flip) for i in range(LEAVES)])]
    pallas_call x10 -> x11, Pallas kernels: 10.1 us -> 10.1 us  [call(): pl.pallas_call(kernel, out_shape=shapes, in_specs=specs or [VMEM] * len(a...]
  transfers between devices with their start and end apart: 19 -> 20, of which waited for: 8 -> 8; matrix products, arithmetic and copies ran while one was open for 0% -> 0% of each run, Pallas kernels for 3% -> 3%
where the time goes in v1:
time: 101 us; the launch traced here: 100 us
  starting transfers between devices  38.5 us (38%)
  blocking collectives  33.2 us (33%)
  waiting for transfers between devices  17.5 us (17%)
  Pallas kernels  10.1 us (10%)
    all_to_all x2, blocking collectives, exchange(): return lax.all_to_all(x, axis, 0, 0, tiled=True, axis_index_groups=groups)  33.2 us
    ppermute x12, starting transfers between devices, swap(): return lax.ppermute(x, 'leaf', [(i, i ^ flip) for i in range(LEAVES)])  17 us
    all_to_all x2, starting transfers between devices, exchange(): return lax.all_to_all(x, axis, 0, 0, tiled=True, axis_index_groups=groups)  12.3 us
    ppermute x12, waiting for transfers between devices, swap(): return lax.ppermute(x, 'leaf', [(i, i ^ flip) for i in range(LEAVES)])  11.7 us
    pallas_call x11, Pallas kernels, call(): pl.pallas_call(kernel, out_shape=shapes, in_specs=specs or [VMEM] * len(a...  10.1 us
    ppermute x6, starting transfers between devices, shifts(): lax.ppermute(x, ('leaf', 'front'), [(leaf * FRONT + front, moved(leaf, fr...  9.25 us
    ppermute x6, waiting for transfers between devices, shifts(): lax.ppermute(x, ('leaf', 'front'), [(leaf * FRONT + front, moved(leaf, fr...  5.79 us
  transfers between devices with their start and end apart: 20, of which 8 were waited for; matrix products, arithmetic and copies ran while one was open for 0% of the time, Pallas kernels for 3%

profile of v1, /device:TPU:2, one launch (start us, length us, event | category | flops | bytes accessed | tf_op | source)
XLA Modules:
  0.0 100.1 jit_solution(2288189796278895499)
XLA Ops:
  0.7 1.8 %shard_map.131 = (bf16[16,128,128]{2,1,0:T(8,128)(2,1)}, bf16[160,512]{1,0:T(8,128)(2,1)S(1)}) custom-call(f32[1,128,128]{2,1,0:T(8,128)} %source.1, bf16[7,32,512]{2,1,0:T(8,128)(2,1)} %low_inv.1, bf16[7,32,512]{2,1,0:T(8,128)(2,1)} %up_inv.1, bf16[6,32,512]{2,1,0:T(8,128)(2,1)} %bitcast.1, bf16[6,32,512]{2,1,0:T(8,128)(2,1)} %up.1), custom_call_target="tpu_custom_call" | custom-call | bytes 1048576 | tf_op jit(solution)/shard_map/pallas_call | solution.py:261
  2.5 7.5 %all-to-all-start = ((bf16[16,128,128]{2,1,0:T(8,128)(2,1)}), bf16[16,128,128]{2,1,0:T(8,128)(2,1)S(1)}, u32[]{:S(2)}, u32[]{:S(2)}) async-start(bf16[16,128,128]{2,1,0:T(8,128)(2,1)} %get-tuple-element.39), calls=%async_computation | async-start | bytes 1048576 | tf_op jit(solution)/shard_map/all_to_all | solution.py:291
  10.1 2.8 %collective-permute-start.1 = (bf16[160,512]{1,0:T(8,128)(2,1)S(1)}, bf16[160,512]{1,0:T(8,128)(2,1)S(1)}, u32[]{:S(2)}, u32[]{:S(2)}) collective-permute-start(bf16[160,512]{1,0:T(8,128)(2,1)S(1)} %get-tuple-element.45.own), channel_id=1, source_target_pairs={{0,2},{1,3},{2,0},{3,1},{4,6},{5,7},{6,4},{7,5},{8,10},{9,11},{10,... | collective-permute-start | bytes 491528 | tf_op jit(solution)/shard_map/ppermute | solution.py:285
  13.0 1.8 %collective-permute-start = (bf16[160,512]{1,0:T(8,128)(2,1)S(1)}, bf16[160,512]{1,0:T(8,128)(2,1)S(1)}, u32[]{:S(2)}, u32[]{:S(2)}) collective-permute-start(bf16[160,512]{1,0:T(8,128)(2,1)S(1)} %get-tuple-element.45.own), channel_id=1, source_target_pairs={{0,1},{1,2},{2,3},{3,0},{4,5},{5,6},{6,7},{7,4},{8,9},{9,10},{10,1... | collective-permute-start | bytes 491528 | tf_op jit(solution)/shard_map/ppermute | solution.py:285
  15.7 3.4 %collective-permute-done.2.c = bf16[160,512]{1,0:T(8,128)(2,1)S(1)} collective-permute-done((bf16[160,512]{1,0:T(8,128)(2,1)S(1)}, bf16[160,512]{1,0:T(8,128)(2,1)S(1)}, u32[]{:S(2)}, u32[]{:S(2)}) %collective-permute-start.2) | collective-permute-done | bytes 163872 | tf_op jit(solution)/shard_map/ppermute | solution.py:285
  19.1 2.4 %collective-permute-done.1.b = bf16[160,512]{1,0:T(8,128)(2,1)S(1)} collective-permute-done((bf16[160,512]{1,0:T(8,128)(2,1)S(1)}, bf16[160,512]{1,0:T(8,128)(2,1)S(1)}, u32[]{:S(2)}, u32[]{:S(2)}) %collective-permute-start.1) | collective-permute-done | bytes 163872 | tf_op jit(solution)/shard_map/ppermute | solution.py:285
  21.6 2.8 %collective-permute-start.5 = (bf16[4,160,512]{2,1,0:T(8,128)(2,1)S(1)}, bf16[4,160,512]{2,1,0:T(8,128)(2,1)S(1)}, u32[]{:S(2)}, u32[]{:S(2)}) collective-permute-start(bf16[4,160,512]{2,1,0:T(8,128)(2,1)S(1)} %shard_map.134.own), channel_id=1, source_target_pairs={{0,12},{1,13},{2,14},{3,15},{4,0},{5,1},{6,2},{7,3},{8,4},{9,5},{1... | collective-permute-start | bytes 1966088 | tf_op jit(solution)/shard_map/ppermute | solution.py:285
  26.6 21.1 %all_to_all.20.got = bf16[16,16,768]{2,1,0:T(8,128)(2,1)S(1)} all-to-all(bf16[16,16,768]{2,1,0:T(8,128)(2,1)S(1)} %get-tuple-element.44), channel_id=1, replica_groups=mesh['leaf'=16,'front'=16] {'front'}, dimensions={0} | all-to-all | bytes 786432 | tf_op jit(solution)/shard_map/all_to_all | solution.py:291
  48.1 1.9 %collective-permute-done.6.swapped = bf16[512,512]{1,0:T(8,128)(2,1)S(1)} collective-permute-done((bf16[512,512]{1,0:T(8,128)(2,1)S(1)}, bf16[512,512]{1,0:T(8,128)(2,1)S(1)}, u32[]{:S(2)}, u32[]{:S(2)}) %collective-permute-start.6) | collective-permute-done | bytes 524320 | tf_op jit(solution)/shard_map/ppermute | solution.py:273
  50.0 1.0 %shard_map.136 = (bf16[16,768]{1,0:T(8,128)(2,1)S(1)}, bf16[512,512]{1,0:T(8,128)(2,1)S(1)}, bf16[1024,512]{1,0:T(8,128)(2,1)S(1)}) custom-call(bf16[16,16,768]{2,1,0:T(8,128)(2,1)S(1)} %all_to_all.20.got, bf16[512,512]{1,0:T(8,128)(2,1)S(1)} %get-tuple-element.53.first, bf16[512,512]{1,0:T(8,128)(2,1)S(1)} %collective-permute-done.6.swapped, ...), custom_call_target="tpu_custom_call" | custom-call | flops 536870912 | bytes 4194304 | tf_op jit(solution)/shard_map/pallas_call | solution.py:261
  51.6 1.7 %collective-permute-start.9 = (bf16[16,768]{1,0:T(8,128)(2,1)S(1)}, bf16[16,768]{1,0:T(8,128)(2,1)S(1)}, u32[]{:S(2)}, u32[]{:S(2)}) collective-permute-start(bf16[16,768]{1,0:T(8,128)(2,1)S(1)} %get-tuple-element.57.own), channel_id=1, source_target_pairs={{0,48},{16,32},{32,16},{48,0},{64,112},{80,96},{96,80},{112,64},{1... | collective-permute-start | bytes 73736 | tf_op jit(solution)/shard_map/ppermute | solution.py:273
  53.6 1.2 %collective-permute-done.9.c = bf16[16,768]{1,0:T(8,128)(2,1)S(1)} collective-permute-done((bf16[16,768]{1,0:T(8,128)(2,1)S(1)}, bf16[16,768]{1,0:T(8,128)(2,1)S(1)}, u32[]{:S(2)}, u32[]{:S(2)}) %collective-permute-start.9) | collective-permute-done | bytes 24608 | tf_op jit(solution)/shard_map/ppermute | solution.py:273
  54.8 2.3 %collective-permute-done.8.b = bf16[16,768]{1,0:T(8,128)(2,1)S(1)} collective-permute-done((bf16[16,768]{1,0:T(8,128)(2,1)S(1)}, bf16[16,768]{1,0:T(8,128)(2,1)S(1)}, u32[]{:S(2)}, u32[]{:S(2)}) %collective-permute-start.8) | collective-permute-done | bytes 24608 | tf_op jit(solution)/shard_map/ppermute | solution.py:273
  57.6 6.3 %collective-permute-start.12 = (bf16[16,768]{1,0:T(8,128)(2,1)S(1)}, bf16[16,768]{1,0:T(8,128)(2,1)S(1)}, u32[]{:S(2)}, u32[]{:S(2)}) collective-permute-start(bf16[16,768]{1,0:T(8,128)(2,1)S(1)} %get-tuple-element.61.own), channel_id=1, source_target_pairs={{0,128},{16,144},{32,160},{48,176},{64,192},{80,208},{96,224},{112... | collective-permute-start | bytes 73736 | tf_op jit(solution)/shard_map/ppermute | solution.py:273
  65.4 1.2 %shard_map.138.picked = bf16[128,1536]{1,0:T(8,128)(2,1)S(1)} custom-call(bf16[1,128,1024]{2,1,0:T(8,128)(2,1)S(1)} %copy-done.4, s32[1,1024]{1,0:T(1,128)S(1)} %copy-done.6), custom_call_target="tpu_custom_call" | custom-call | flops 402653184 | bytes 2097152 | tf_op jit(solution)/shard_map/pallas_call | solution.py:261
  66.6 2.6 %collective-permute-done.11.near = bf16[16,512]{1,0:T(8,128)(2,1)S(1)} collective-permute-done((bf16[16,512]{1,0:T(8,128)(2,1)S(1)}, bf16[16,512]{1,0:T(8,128)(2,1)S(1)}, u32[]{:S(2)}, u32[]{:S(2)}) %collective-permute-start.11) | collective-permute-done | bytes 16416 | tf_op jit(solution)/shard_map/ppermute | solution.py:273
  69.7 1.5 %shard_map.139 = bf16[16,16,768]{2,1,0:T(8,128)(2,1)S(1)} custom-call(bf16[16,768]{1,0:T(8,128)(2,1)S(1)} %get-tuple-element.61.own, bf16[16,512]{1,0:T(8,128)(2,1)S(1)} %collective-permute-done.11.near, bf16[16,768]{1,0:T(8,128)(2,1)S(1)} %collective-permute-done.12.far, bf16[16,256]{1,0:T(8,128)(2,1)S(1)} %collective-permute-done.13.other, ...), custom_call_target="tpu_custom_call" | custom-call | flops 1207959552 | bytes 5242880 | tf_op jit(solution)/shard_map/pallas_call | solution.py:261
  71.3 12.2 %all_to_all.21.got = bf16[16,16,768]{2,1,0:T(8,128)(2,1)S(1)} all-to-all(bf16[16,16,768]{2,1,0:T(8,128)(2,1)S(1)} %shard_map.139), channel_id=1, replica_groups=mesh['leaf'=16,'front'=16] {'front'}, dimensions={0} | all-to-all | bytes 786432 | tf_op jit(solution)/shard_map/all_to_all | solution.py:291
  83.4 1.2 %shard_map.140 = (bf16[16,128,128]{2,1,0:T(8,128)(2,1)}, f32[96,128]{1,0:T(8,128)S(1)}, bf16[64,128]{1,0:T(8,128)(2,1)S(1)}, bf16[32,128]{1,0:T(8,128)(2,1)S(1)}) custom-call(bf16[16,16,768]{2,1,0:T(8,128)(2,1)S(1)} %all_to_all.21.got, f32[128,128]{1,0:T(8,128)S(1)} %get-tuple-element.68.solved, bf16[128,1536]{1,0:T(8,128)(2,1)S(1)} %shard_map.138.picked), custom_call_target="tpu_custom_call" | custom-call | flops 100663296 | bytes 2097152 | tf_op jit(solution)/shard_map/pallas_call | solution.py:261
  84.6 4.8 %all-to-all-start.3 = ((bf16[16,128,128]{2,1,0:T(8,128)(2,1)}), bf16[16,128,128]{2,1,0:T(8,128)(2,1)S(1)}, u32[]{:S(2)}, u32[]{:S(2)}) async-start(bf16[16,128,128]{2,1,0:T(8,128)(2,1)} %get-tuple-element.70), calls=%async_computation.3 | async-start | bytes 1048576 | tf_op jit(solution)/shard_map/all_to_all | solution.py:291
  89.5 3.9 %collective-permute-start.16 = (bf16[64,128]{1,0:T(8,128)(2,1)S(1)}, bf16[64,128]{1,0:T(8,128)(2,1)S(1)}, u32[]{:S(2)}, u32[]{:S(2)}) collective-permute-start(bf16[64,128]{1,0:T(8,128)(2,1)S(1)} %get-tuple-element.73), channel_id=1, source_target_pairs={{0,128},{16,144},{32,160},{48,176},{64,192},{80,208},{96,224},{112... | collective-permute-start | bytes 49160 | tf_op jit(solution)/shard_map/ppermute | solution.py:273
  93.4 1.1 %collective-permute-start.17 = (bf16[32,128]{1,0:T(8,128)(2,1)S(1)}, bf16[32,128]{1,0:T(8,128)(2,1)S(1)}, u32[]{:S(2)}, u32[]{:S(2)}) collective-permute-start(bf16[32,128]{1,0:T(8,128)(2,1)S(1)} %get-tuple-element.72), channel_id=1, source_target_pairs={{0,192},{16,208},{32,224},{48,240},{64,128},{80,144},{96,160},{112... | collective-permute-start | bytes 24584 | tf_op jit(solution)/shard_map/ppermute | solution.py:273
  94.5 1.5 %collective-permute-start.15 = (bf16[32,128]{1,0:T(8,128)(2,1)S(1)}, bf16[32,128]{1,0:T(8,128)(2,1)S(1)}, u32[]{:S(2)}, u32[]{:S(2)}) collective-permute-start(bf16[32,128]{1,0:T(8,128)(2,1)S(1)} %get-tuple-element.72), channel_id=1, source_target_pairs={{0,64},{16,80},{32,96},{48,112},{64,0},{80,16},{96,32},{112,48},{1... | collective-permute-start | bytes 24584 | tf_op jit(solution)/shard_map/ppermute | solution.py:273
  96.0 3.2 %collective-permute-done.17.other = bf16[32,128]{1,0:T(8,128)(2,1)S(1)} collective-permute-done((bf16[32,128]{1,0:T(8,128)(2,1)S(1)}, bf16[32,128]{1,0:T(8,128)(2,1)S(1)}, u32[]{:S(2)}, u32[]{:S(2)}) %collective-permute-start.17) | collective-permute-done | bytes 8224 | tf_op jit(solution)/shard_map/ppermute | solution.py:273
  (43 shorter events, 8.3 us)
Async XLA Ops:
  2.5 19.1 %all-to-all-start = ((bf16[16,128,128]{2,1,0:T(8,128)(2,1)}), bf16[16,128,128]{2,1,0:T(8,128)(2,1)S(1)}, u32[]{:S(2)}, u32[]{:S(2)}) async-start(bf16[16,128,128]{2,1,0:T(8,128)(2,1)} %get-tuple-element.39), calls=%async_computation | async-start | bytes 1048576 | tf_op jit(solution)/shard_map/all_to_all | solution.py:291
  9.9 16.1 %copy-start = (bf16[1,128,2048]{2,1,0:T(8,128)(2,1)S(1)}, bf16[1,128,2048]{2,1,0:T(8,128)(2,1)}, u32[]{:S(2)}) copy-start(bf16[1,128,2048]{2,1,0:T(8,128)(2,1)} %inverse.2) | copy-start | bytes 1572868
  10.0 9.1 %collective-permute-start.2 = (bf16[160,512]{1,0:T(8,128)(2,1)S(1)}, bf16[160,512]{1,0:T(8,128)(2,1)S(1)}, u32[]{:S(2)}, u32[]{:S(2)}) collective-permute-start(bf16[160,512]{1,0:T(8,128)(2,1)S(1)} %get-tuple-element.45.own), channel_id=1, source_target_pairs={{0,3},{1,0},{2,1},{3,2},{4,7},{5,4},{6,5},{7,6},{8,11},{9,8},{10,9... | collective-permute-start | bytes 491528 | tf_op jit(solution)/shard_map/ppermute | solution.py:285
  10.1 11.4 %collective-permute-start.1 = (bf16[160,512]{1,0:T(8,128)(2,1)S(1)}, bf16[160,512]{1,0:T(8,128)(2,1)S(1)}, u32[]{:S(2)}, u32[]{:S(2)}) collective-permute-start(bf16[160,512]{1,0:T(8,128)(2,1)S(1)} %get-tuple-element.45.own), channel_id=1, source_target_pairs={{0,2},{1,3},{2,0},{3,1},{4,6},{5,7},{6,4},{7,5},{8,10},{9,11},{10,... | collective-permute-start | bytes 491528 | tf_op jit(solution)/shard_map/ppermute | solution.py:285
  13.0 8.5 %collective-permute-start = (bf16[160,512]{1,0:T(8,128)(2,1)S(1)}, bf16[160,512]{1,0:T(8,128)(2,1)S(1)}, u32[]{:S(2)}, u32[]{:S(2)}) collective-permute-start(bf16[160,512]{1,0:T(8,128)(2,1)S(1)} %get-tuple-element.45.own), channel_id=1, source_target_pairs={{0,1},{1,2},{2,3},{3,0},{4,5},{5,6},{6,7},{7,4},{8,9},{9,10},{10,1... | collective-permute-start | bytes 491528 | tf_op jit(solution)/shard_map/ppermute | solution.py:285
  21.6 26.1 %collective-permute-start.5 = (bf16[4,160,512]{2,1,0:T(8,128)(2,1)S(1)}, bf16[4,160,512]{2,1,0:T(8,128)(2,1)S(1)}, u32[]{:S(2)}, u32[]{:S(2)}) collective-permute-start(bf16[4,160,512]{2,1,0:T(8,128)(2,1)S(1)} %shard_map.134.own), channel_id=1, source_target_pairs={{0,12},{1,13},{2,14},{3,15},{4,0},{5,1},{6,2},{7,3},{8,4},{9,5},{1... | collective-permute-start | bytes 1966088 | tf_op jit(solution)/shard_map/ppermute | solution.py:285
  24.3 23.4 %collective-permute-start.4 = (bf16[4,160,512]{2,1,0:T(8,128)(2,1)S(1)}, bf16[4,160,512]{2,1,0:T(8,128)(2,1)S(1)}, u32[]{:S(2)}, u32[]{:S(2)}) collective-permute-start(bf16[4,160,512]{2,1,0:T(8,128)(2,1)S(1)} %shard_map.134.own), channel_id=1, source_target_pairs={{0,8},{1,9},{2,10},{3,11},{4,12},{5,13},{6,14},{7,15},{8,0},{9,1},... | collective-permute-start | bytes 1966088 | tf_op jit(solution)/shard_map/ppermute | solution.py:285
  25.2 22.5 %collective-permute-start.3 = (bf16[4,160,512]{2,1,0:T(8,128)(2,1)S(1)}, bf16[4,160,512]{2,1,0:T(8,128)(2,1)S(1)}, u32[]{:S(2)}, u32[]{:S(2)}) collective-permute-start(bf16[4,160,512]{2,1,0:T(8,128)(2,1)S(1)} %shard_map.134.own), channel_id=1, source_target_pairs={{0,4},{1,5},{2,6},{3,7},{4,8},{5,9},{6,10},{7,11},{8,12},{9,13},{1... | collective-permute-start | bytes 1966088 | tf_op jit(solution)/shard_map/ppermute | solution.py:285
  26.6 23.4 %copy-start.5 = (s32[6,512]{1,0:T(8,128)S(1)}, s32[6,512]{1,0:T(8,128)}, u32[]{:S(2)}) copy-start(s32[6,512]{1,0:T(8,128)} %targets.4) | copy-start | bytes 36868
  48.0 17.5 %copy-start.4 = (bf16[1,128,1024]{2,1,0:T(8,128)(2,1)S(1)}, bf16[1,128,1024]{2,1,0:T(8,128)(2,1)}, u32[]{:S(2)}) copy-start(bf16[1,128,1024]{2,1,0:T(8,128)(2,1)} %block.1) | copy-start | bytes 786436
  48.0 2.0 %collective-permute-start.6 = (bf16[512,512]{1,0:T(8,128)(2,1)S(1)}, bf16[512,512]{1,0:T(8,128)(2,1)S(1)}, u32[]{:S(2)}, u32[]{:S(2)}) collective-permute-start(bf16[512,512]{1,0:T(8,128)(2,1)S(1)} %get-tuple-element.53.first), channel_id=1, source_target_pairs={{0,16},{16,0},{32,48},{48,32},{64,80},{80,64},{96,112},{112,96},{1... | collective-permute-start | bytes 1572872 | tf_op jit(solution)/shard_map/ppermute | solution.py:273
  51.0 18.7 %collective-permute-start.14 = (bf16[3,512,512]{2,1,0:T(8,128)(2,1)S(1)}, bf16[3,512,512]{2,1,0:T(8,128)(2,1)S(1)}, u32[]{:S(2)}, u32[]{:S(2)}) collective-permute-start(bf16[3,512,512]{2,1,0:T(8,128)(2,1)S(1)} %get-tuple-element.66.later), channel_id=1, source_target_pairs={{0,16},{16,0},{32,48},{48,32},{64,80},{80,64},{96,112},{112,96},{1... | collective-permute-start | bytes 4718600 | tf_op jit(solution)/shard_map/ppermute | solution.py:273
  51.2 5.9 %collective-permute-start.10 = (bf16[512,512]{1,0:T(8,128)(2,1)S(1)}, bf16[512,512]{1,0:T(8,128)(2,1)S(1)}, u32[]{:S(2)}, u32[]{:S(2)}) collective-permute-start(bf16[512,512]{1,0:T(8,128)(2,1)S(1)} %get-tuple-element.58.first), channel_id=1, source_target_pairs={{0,16},{16,0},{32,48},{48,32},{64,80},{80,64},{96,112},{112,96},{1... | collective-permute-start | bytes 1572872 | tf_op jit(solution)/shard_map/ppermute | solution.py:273
  51.6 3.3 %collective-permute-start.9 = (bf16[16,768]{1,0:T(8,128)(2,1)S(1)}, bf16[16,768]{1,0:T(8,128)(2,1)S(1)}, u32[]{:S(2)}, u32[]{:S(2)}) collective-permute-start(bf16[16,768]{1,0:T(8,128)(2,1)S(1)} %get-tuple-element.57.own), channel_id=1, source_target_pairs={{0,48},{16,32},{32,16},{48,0},{64,112},{80,96},{96,80},{112,64},{1... | collective-permute-start | bytes 73736 | tf_op jit(solution)/shard_map/ppermute | solution.py:273
  53.2 3.8 %collective-permute-start.8 = (bf16[16,768]{1,0:T(8,128)(2,1)S(1)}, bf16[16,768]{1,0:T(8,128)(2,1)S(1)}, u32[]{:S(2)}, u32[]{:S(2)}) collective-permute-start(bf16[16,768]{1,0:T(8,128)(2,1)S(1)} %get-tuple-element.57.own), channel_id=1, source_target_pairs={{0,32},{16,48},{32,0},{48,16},{64,96},{80,112},{96,64},{112,80},{1... | collective-permute-start | bytes 73736 | tf_op jit(solution)/shard_map/ppermute | solution.py:273
  53.5 3.6 %collective-permute-start.7 = (bf16[16,768]{1,0:T(8,128)(2,1)S(1)}, bf16[16,768]{1,0:T(8,128)(2,1)S(1)}, u32[]{:S(2)}, u32[]{:S(2)}) collective-permute-start(bf16[16,768]{1,0:T(8,128)(2,1)S(1)} %get-tuple-element.57.own), channel_id=1, source_target_pairs={{0,16},{16,0},{32,48},{48,32},{64,80},{80,64},{96,112},{112,96},{1... | collective-permute-start | bytes 73736 | tf_op jit(solution)/shard_map/ppermute | solution.py:273
  57.6 12.1 %collective-permute-start.12 = (bf16[16,768]{1,0:T(8,128)(2,1)S(1)}, bf16[16,768]{1,0:T(8,128)(2,1)S(1)}, u32[]{:S(2)}, u32[]{:S(2)}) collective-permute-start(bf16[16,768]{1,0:T(8,128)(2,1)S(1)} %get-tuple-element.61.own), channel_id=1, source_target_pairs={{0,128},{16,144},{32,160},{48,176},{64,192},{80,208},{96,224},{112... | collective-permute-start | bytes 73736 | tf_op jit(solution)/shard_map/ppermute | solution.py:273
  64.0 5.8 %collective-permute-start.13 = (bf16[16,256]{1,0:T(8,128)(2,1)S(1)}, bf16[16,256]{1,0:T(8,128)(2,1)S(1)}, u32[]{:S(2)}, u32[]{:S(2)}) collective-permute-start(bf16[16,256]{1,0:T(8,128)(2,1)S(1)} %get-tuple-element.65), channel_id=1, source_target_pairs={{0,192},{16,208},{32,224},{48,240},{64,128},{80,144},{96,160},{112... | collective-permute-start | bytes 24584 | tf_op jit(solution)/shard_map/ppermute | solution.py:273
  64.5 4.7 %collective-permute-start.11 = (bf16[16,512]{1,0:T(8,128)(2,1)S(1)}, bf16[16,512]{1,0:T(8,128)(2,1)S(1)}, u32[]{:S(2)}, u32[]{:S(2)}) collective-permute-start(bf16[16,512]{1,0:T(8,128)(2,1)S(1)} %get-tuple-element.62), channel_id=1, source_target_pairs={{0,64},{16,80},{32,96},{48,112},{64,0},{80,16},{96,32},{112,48},{1... | collective-permute-start | bytes 49160 | tf_op jit(solution)/shard_map/ppermute | solution.py:273
  71.3 27.9 %copy-start.1 = (bf16[1,128,2048]{2,1,0:T(8,128)(2,1)S(1)}, bf16[1,128,2048]{2,1,0:T(8,128)(2,1)}, u32[]{:S(2)}) copy-start(bf16[1,128,2048]{2,1,0:T(8,128)(2,1)} %inverse.3) | copy-start | bytes 1572868
  84.6 14.5 %all-to-all-start.3 = ((bf16[16,128,128]{2,1,0:T(8,128)(2,1)}), bf16[16,128,128]{2,1,0:T(8,128)(2,1)S(1)}, u32[]{:S(2)}, u32[]{:S(2)}) async-start(bf16[16,128,128]{2,1,0:T(8,128)(2,1)} %get-tuple-element.70), calls=%async_computation.3 | async-start | bytes 1048576 | tf_op jit(solution)/shard_map/all_to_all | solution.py:291
  89.5 9.7 %collective-permute-start.16 = (bf16[64,128]{1,0:T(8,128)(2,1)S(1)}, bf16[64,128]{1,0:T(8,128)(2,1)S(1)}, u32[]{:S(2)}, u32[]{:S(2)}) collective-permute-start(bf16[64,128]{1,0:T(8,128)(2,1)S(1)} %get-tuple-element.73), channel_id=1, source_target_pairs={{0,128},{16,144},{32,160},{48,176},{64,192},{80,208},{96,224},{112... | collective-permute-start | bytes 49160 | tf_op jit(solution)/shard_map/ppermute | solution.py:273
  93.4 5.8 %collective-permute-start.17 = (bf16[32,128]{1,0:T(8,128)(2,1)S(1)}, bf16[32,128]{1,0:T(8,128)(2,1)S(1)}, u32[]{:S(2)}, u32[]{:S(2)}) collective-permute-start(bf16[32,128]{1,0:T(8,128)(2,1)S(1)} %get-tuple-element.72), channel_id=1, source_target_pairs={{0,192},{16,208},{32,224},{48,240},{64,128},{80,144},{96,160},{112... | collective-permute-start | bytes 24584 | tf_op jit(solution)/shard_map/ppermute | solution.py:273
  94.5 4.7 %collective-permute-start.15 = (bf16[32,128]{1,0:T(8,128)(2,1)S(1)}, bf16[32,128]{1,0:T(8,128)(2,1)S(1)}, u32[]{:S(2)}, u32[]{:S(2)}) collective-permute-start(bf16[32,128]{1,0:T(8,128)(2,1)S(1)} %get-tuple-element.72), channel_id=1, source_target_pairs={{0,64},{16,80},{32,96},{48,112},{64,0},{80,16},{96,32},{112,48},{1... | collective-permute-start | bytes 24584 | tf_op jit(solution)/shard_map/ppermute | solution.py:273
  (3 other events, 44.3 us)

commit v2 on v1

--- a/solution.py
+++ b/solution.py
@@ -1,3 +1,5 @@
+import functools
+
 import jax
 import jax.numpy as jnp
 from jax import lax
@@ -56,7 +58,7 @@
     return jnp.where(targets >= SEP, SEP, 0) + (targets & (SEP - 1))
 
 
-def prepare_kernel(source, low_inv, up_inv, low, up, send, mats, piece, sems):
+def prepare_kernel(source, low_inv, up_inv, low, up, send, piece, sems):
     leaf = lax.axis_index("leaf")
     third = 3 + (leaf >> 2)
     second = 1 + (leaf >> 3)
@@ -64,7 +66,7 @@
         [(low_inv, third), (low_inv, second), (low_inv, 0), (up_inv, 0), (up, second - 1)],
         [(low, third - 1), (low, second - 1), (up_inv, second), (up, third - 1), (up_inv, third)],
     ]
-    places = [mats.at[pl.ds(i * ROWS, ROWS)] for i in range(5)]
+    places = [send.at[pl.ds(i * ROWS + ROWS, ROWS)] for i in range(5)]
     start = pltpu.make_async_copy(source.at[0], piece, sems.at[5])
     start.start()
     for core, plan in enumerate(plans):
@@ -82,31 +84,35 @@
 
     start.wait()
     block = piece[...].astype(BF)
-    for to in range(FRONT):
-        send[to] = block
-
-
-def pack_kernel(own, a, b, c, out):
+    send[0:ROWS, :] = jnp.concatenate([block[q * ROWS : q * ROWS + ROWS] for q in range(4)], axis=1)
+
+
+def pack_kernel(own, a, b, c, early, later):
     for k, ref in enumerate((own, a, b, c)):
-        out[k] = ref[...]
-
-
-def assemble_kernel(own, a, b, c, ahead, second, later):
+        early[k] = ref[0:64, :]
+        later[k] = ref[64:192, :]
+
+
+def origin(j, k):
     front = lax.axis_index("front")
     core = lax.axis_index("leaf") & 1
     y, x = front >> 2, front & 3
+    dy = jnp.where(core == 0, j, k)
+    dx = jnp.where(core == 0, k, j)
+    return ((y - dy) & 3) * 4 + ((x - dx) & 3)
+
+
+def assemble_kernel(skip, own, a, b, c, *outs):
     for j, ref in enumerate((own, a, b, c)):
         for k in range(4):
-            dy = jnp.where(core == 0, j, k)
-            dx = jnp.where(core == 0, k, j)
-            at = ((y - dy) & 3) * 4 + ((x - dx) & 3)
-            rows = pl.ds(pl.multiple_of(at * ROWS, ROWS), ROWS)
-            for i in range(5):
-                part = ref[k, i * ROWS : i * ROWS + ROWS, :]
-                if i < 2:
-                    (ahead, second)[i][rows, :] = part
-                else:
-                    later[i - 2, rows, :] = part
+            rows = pl.ds(pl.multiple_of(origin(j, k) * ROWS, ROWS), ROWS)
+            for i, out in enumerate(outs):
+                first = (skip + i) * ROWS
+                out[rows, :] = ref[k, first : first + ROWS, :]
+
+
+def assemble_later_kernel(own, a, b, c, second, out):
+    assemble_kernel(0, own, a, b, c, second, *[out.at[i] for i in range(3)])
 
 
 def pick_kernel(block, targets, picked):
@@ -116,19 +122,28 @@
         picked[:, rows] = dot(block[0], one_hot(part * SEP, SEP, places), NT).astype(BF)
 
 
-def spread_kernel(block, targets, spread):
+def spread_kernel(block, targets, top_targets, spread, hot2, hot3):
+    leaf = lax.axis_index("leaf")
+    hot2[...] = one_hot(0, SEP, top_targets[pl.ds(leaf >> 3, 1), :])
+    hot3[...] = one_hot(0, 2 * SEP, ancestor_places(top_targets[pl.ds(2 + (leaf >> 2), 1), :]))
     places = leaf_places(targets[...])
     for part in range(3):
         hot = one_hot(part * SEP, SEP, places)
         spread[part * SEP : part * SEP + SEP, :] = dot(hot, block[0], NN).astype(BF)
 
 
-def leaf_forward_kernel(got, inverse, spread, top, solved_out, send):
+def leaf_forward_kernel(own, a, b, c, inverse, spread, top, solved_out, send, source):
     leaf = lax.axis_index("leaf")
     front = lax.axis_index("front")
-    solved = dot(inverse[0], got[...].reshape(SUB, RHS), NN)
+    for j, ref in enumerate((own, a, b, c)):
+        for k in range(4):
+            at = origin(j, k) * PIECE
+            for q in range(4):
+                rows = pl.ds(pl.multiple_of(at + q * ROWS, ROWS), ROWS)
+                source[rows, :] = ref[k, 0:ROWS, q * RHS : q * RHS + RHS]
+    solved = dot(inverse[0], source[...], NN)
     solved_out[...] = solved
-    own = jnp.concatenate(
+    mine = jnp.concatenate(
         [
             top[0] * (1 / 16),
             top[1 + (leaf >> 3)] * (1 / 8),
@@ -140,15 +155,13 @@
     row = lax.broadcasted_iota(jnp.int32, (RHS, SPAN), 0)
     column = lax.broadcasted_iota(jnp.int32, (RHS, SPAN), 1)
     hot = jnp.where(column == ((row >> 5) << 9) + front * ROWS + (row & 31), 1.0, 0.0).astype(BF)
-    total = dot(own.astype(BF), hot, NN) - dot(solved.T.astype(BF), spread[...], NT)
+    total = dot(mine.astype(BF), hot, NN) - dot(solved.T.astype(BF), spread[...], NT)
     for to in range(FRONT):
         send[to] = fold(total[to * 8 : to * 8 + 8]).astype(BF)
 
 
-def top_forward_kernel(got, first, swapped, targets, send, hot2, hot3):
+def top_forward_kernel(got, first, swapped, hot3, send):
     leaf = lax.axis_index("leaf")
-    hot2[...] = one_hot(0, SEP, targets[pl.ds(leaf >> 3, 1), :])
-    hot3[...] = one_hot(0, 2 * SEP, ancestor_places(targets[pl.ds(2 + (leaf >> 2), 1), :]))
     total = got[0].astype(F32)
     for k in range(1, FRONT):
         total = total + got[k].astype(F32)
@@ -305,9 +318,9 @@
     leaf_targets,
     top_targets,
 ):
-    send, mats = call(
+    (send,) = call(
         prepare_kernel,
-        [((FRONT, PIECE, RHS), BF), ((160, SEP), BF)],
+        [((192, SEP), BF)],
         (
             keep(leaf_source),
             keep(top_lower_inverse),
@@ -319,37 +332,42 @@
         scratch=[pltpu.VMEM((PIECE, RHS), F32), pltpu.SemaphoreType.DMA((6,))],
         size=1 << 20,
     )
-    leaf_lower_block, send = lax.optimization_barrier((leaf_lower_block, send))
-    (spread,) = call(
+    early, later = call(
+        pack_kernel,
+        [((4, 64, SEP), BF), ((4, 128, SEP), BF)],
+        (send, *shifts(send, 0)),
+        size=1 << 20,
+    )
+    parts = shifts(early, 1)
+    send, leaf_lower_block = lax.optimization_barrier((send, leaf_lower_block))
+    spread, hot2, hot3 = call(
         spread_kernel,
-        [((SPAN, PIECE), BF)],
-        (leaf_lower_block, leaf_targets),
+        [((SPAN, PIECE), BF), ((SEP, SEP), BF), ((2 * SEP, SEP), BF)],
+        (leaf_lower_block, leaf_targets, top_targets),
         flops=2 * UPD * SPAN * PIECE,
         size=2 << 20,
     )
-    got = exchange(send, "front")
-    got, mats, spread, *parts = lax.optimization_barrier((got, mats, spread, *shifts(mats, 0)))
-    (mats,) = call(pack_kernel, [((4, 160, SEP), BF)], (mats, *parts), size=1 << 20)
+    later, spread, *parts = lax.optimization_barrier((later, spread, *parts))
+    (ahead,) = call(functools.partial(assemble_kernel, 1), [((SEP, SEP), BF)], (early, *parts), size=1 << 20)
+    swapped = swap(ahead, 1)
     solved, send = call(
         leaf_forward_kernel,
         [((PIECE, RHS), F32), ((FRONT, 16, HALF), BF)],
-        (got, leaf_lower_inverse, spread, top_source),
-        flops=2 * RHS * (PIECE * SUB + 2 * PIECE * SPAN),
+        (early, *parts, leaf_lower_inverse, spread, top_source),
+        scratch=[pltpu.VMEM((SUB, RHS), BF)],
+        flops=2 * RHS * (PIECE * SUB + UPD * PIECE + UPD * SPAN),
         size=4 << 20,
     )
-    parts = shifts(mats, 1)
+    parts = shifts(later, 1)
     got = exchange(send, "front")
     got, *parts = lax.optimization_barrier((got, *parts))
-    ahead, second, later = call(
-        assemble_kernel,
-        [((SEP, SEP), BF), ((SEP, SEP), BF), ((3, SEP, SEP), BF)],
-        (mats, *parts),
-        size=5 << 20,
-    )
-    send, hot2, hot3 = call(
+    second, later = call(
+        assemble_later_kernel, [((SEP, SEP), BF), ((3, SEP, SEP), BF)], (later, *parts), size=4 << 20
+    )
+    (send,) = call(
         top_forward_kernel,
-        [((16, HALF), BF), ((SEP, SEP), BF), ((2 * SEP, SEP), BF)],
-        (got, ahead, swap(ahead, 1), top_targets),
+        [((16, HALF), BF)],
+        (got, ahead, swapped, hot3),
         flops=2 * 256 * SEP * SEP * 4,
         size=4 << 20,
     )

time: 101 us -> 98.1 us (0.971)
  starting transfers between devices: 38.5 us -> 33.3 us
  waiting for transfers between devices: 17.5 us -> 22.6 us
  blocking collectives: 33.2 us -> 31.7 us
    all_to_all x2 -> x1, starting transfers between devices: 12.3 us -> 4.82 us  [exchange(): return lax.all_to_all(x, axis, 0, 0, tiled=True, axis_index_groups=groups)]
    ppermute x6 -> x9, waiting for transfers between devices: 5.79 us -> 12.9 us  [shifts(): lax.ppermute(x, ('leaf', 'front'), [(leaf * FRONT + front, moved(leaf, fr...]
    ppermute x6 -> x9, starting transfers between devices: 9.25 us -> 11.6 us  [shifts(): lax.ppermute(x, ('leaf', 'front'), [(leaf * FRONT + front, moved(leaf, fr...]
    ppermute x12, waiting for transfers between devices: 11.7 us -> 9.73 us  [swap(): return lax.ppermute(x, 'leaf', [(i, i ^ flip) for i in range(LEAVES)])]
    all_to_all x2, blocking collectives: 33.2 us -> 31.7 us  [exchange(): return lax.all_to_all(x, axis, 0, 0, tiled=True, axis_index_groups=groups)]
    pallas_call x11 -> x12, Pallas kernels: 10.1 us -> 9.35 us  [call(): pl.pallas_call(kernel, out_shape=shapes, in_specs=specs or [VMEM] * len(a...]
  transfers between devices with their start and end apart: 20 -> 22, of which waited for: 8 -> 11; matrix products, arithmetic and copies ran while one was open for 0% -> 0% of each run, Pallas kernels for 3% -> 4%
where the time goes in v2:
time: 98.1 us; the launch traced here: 97.8 us
  starting transfers between devices  33.3 us (34%)
  blocking collectives  31.7 us (32%)
  waiting for transfers between devices  22.6 us (23%)
  Pallas kernels  9.35 us (10%)
    all_to_all x2, blocking collectives, exchange(): return lax.all_to_all(x, axis, 0, 0, tiled=True, axis_index_groups=groups)  31.7 us
    ppermute x12, starting transfers between devices, swap(): return lax.ppermute(x, 'leaf', [(i, i ^ flip) for i in range(LEAVES)])  16.9 us
    ppermute x9, waiting for transfers between devices, shifts(): lax.ppermute(x, ('leaf', 'front'), [(leaf * FRONT + front, moved(leaf, fr...  12.9 us
    ppermute x9, starting transfers between devices, shifts(): lax.ppermute(x, ('leaf', 'front'), [(leaf * FRONT + front, moved(leaf, fr...  11.6 us
    ppermute x12, waiting for transfers between devices, swap(): return lax.ppermute(x, 'leaf', [(i, i ^ flip) for i in range(LEAVES)])  9.73 us
    pallas_call x12, Pallas kernels, call(): pl.pallas_call(kernel, out_shape=shapes, in_specs=specs or [VMEM] * len(a...  9.35 us
    all_to_all x1, starting transfers between devices, exchange(): return lax.all_to_all(x, axis, 0, 0, tiled=True, axis_index_groups=groups)  4.82 us
  transfers between devices with their start and end apart: 22, of which 11 were waited for; matrix products, arithmetic and copies ran while one was open for 0% of the time, Pallas kernels for 4%

profile of v2, /device:TPU:2, one launch (start us, length us, event | category | flops | bytes accessed | tf_op | source)
XLA Modules:
  0.0 97.8 jit_solution(18324389228259242465)
XLA Ops:
  1.6 2.3 %collective-permute-start.2 = (bf16[192,512]{1,0:T(8,128)(2,1)S(1)}, bf16[192,512]{1,0:T(8,128)(2,1)S(1)}, u32[]{:S(2)}, u32[]{:S(2)}) collective-permute-start(bf16[192,512]{1,0:T(8,128)(2,1)S(1)} %shard_map.131.own), channel_id=1, source_target_pairs={{0,3},{1,0},{2,1},{3,2},{4,7},{5,4},{6,5},{7,6},{8,11},{9,8},{10,9... | collective-permute-start | bytes 589832 | tf_op jit(solution)/shard_map/ppermute | solution.py:298
  4.7 1.8 %collective-permute-start = (bf16[192,512]{1,0:T(8,128)(2,1)S(1)}, bf16[192,512]{1,0:T(8,128)(2,1)S(1)}, u32[]{:S(2)}, u32[]{:S(2)}) collective-permute-start(bf16[192,512]{1,0:T(8,128)(2,1)S(1)} %shard_map.131.own), channel_id=1, source_target_pairs={{0,1},{1,2},{2,3},{3,0},{4,5},{5,6},{6,7},{7,4},{8,9},{9,10},{10,1... | collective-permute-start | bytes 589832 | tf_op jit(solution)/shard_map/ppermute | solution.py:298
  7.4 3.8 %collective-permute-done.1.b = bf16[192,512]{1,0:T(8,128)(2,1)S(1)} collective-permute-done((bf16[192,512]{1,0:T(8,128)(2,1)S(1)}, bf16[192,512]{1,0:T(8,128)(2,1)S(1)}, u32[]{:S(2)}, u32[]{:S(2)}) %collective-permute-start.1) | collective-permute-done | bytes 196640 | tf_op jit(solution)/shard_map/ppermute | solution.py:298
  11.6 3.1 %collective-permute-start.5 = (bf16[4,64,512]{2,1,0:T(8,128)(2,1)S(1)}, bf16[4,64,512]{2,1,0:T(8,128)(2,1)S(1)}, u32[]{:S(2)}, u32[]{:S(2)}) collective-permute-start(bf16[4,64,512]{2,1,0:T(8,128)(2,1)S(1)} %get-tuple-element.35.own), channel_id=1, source_target_pairs={{0,12},{1,13},{2,14},{3,15},{4,0},{5,1},{6,2},{7,3},{8,4},{9,5},{1... | collective-permute-start | bytes 786440 | tf_op jit(solution)/shard_map/ppermute | solution.py:298
  15.3 1.0 collective-permute-start.3
  16.3 1.3 %shard_map.133 = (bf16[1536,128]{1,0:T(8,128)(2,1)S(1)}, bf16[512,512]{1,0:T(8,128)(2,1)S(1)}, bf16[1024,512]{1,0:T(8,128)(2,1)S(1)}) custom-call(bf16[1,1024,128]{2,1,0:T(8,128)(2,1)S(1)} %copy-done.3, s32[1,1024]{1,0:T(1,128)S(1)} %copy-done.6, s32[6,512]{1,0:T(8,128)S(1)} %copy-done.5), custom_call_target="tpu_custom_call" | custom-call | flops 402653184 | bytes 2097152 | tf_op jit(solution)/shard_map/pallas_call | solution.py:274
  17.6 3.8 %collective-permute-done.5.c = bf16[4,64,512]{2,1,0:T(8,128)(2,1)S(1)} collective-permute-done((bf16[4,64,512]{2,1,0:T(8,128)(2,1)S(1)}, bf16[4,64,512]{2,1,0:T(8,128)(2,1)S(1)}, u32[]{:S(2)}, u32[]{:S(2)}) %collective-permute-start.5) | collective-permute-done | bytes 262176 | tf_op jit(solution)/shard_map/ppermute | solution.py:298
  21.4 1.3 %collective-permute-done.4.b = bf16[4,64,512]{2,1,0:T(8,128)(2,1)S(1)} collective-permute-done((bf16[4,64,512]{2,1,0:T(8,128)(2,1)S(1)}, bf16[4,64,512]{2,1,0:T(8,128)(2,1)S(1)}, u32[]{:S(2)}, u32[]{:S(2)}) %collective-permute-start.4) | collective-permute-done | bytes 262176 | tf_op jit(solution)/shard_map/ppermute | solution.py:298
  22.7 2.7 %collective-permute-done.3.a = bf16[4,64,512]{2,1,0:T(8,128)(2,1)S(1)} collective-permute-done((bf16[4,64,512]{2,1,0:T(8,128)(2,1)S(1)}, bf16[4,64,512]{2,1,0:T(8,128)(2,1)S(1)}, u32[]{:S(2)}, u32[]{:S(2)}) %collective-permute-start.3) | collective-permute-done | bytes 262176 | tf_op jit(solution)/shard_map/ppermute | solution.py:298
  28.3 18.2 %all_to_all.15.got = bf16[16,16,768]{2,1,0:T(8,128)(2,1)S(1)} all-to-all(bf16[16,16,768]{2,1,0:T(8,128)(2,1)S(1)} %get-tuple-element.43), channel_id=1, replica_groups=mesh['leaf'=16,'front'=16] {'front'}, dimensions={0} | all-to-all | bytes 786432 | tf_op jit(solution)/shard_map/all_to_all | solution.py:304
  48.1 1.6 %collective-permute-start.12 = (bf16[16,768]{1,0:T(8,128)(2,1)S(1)}, bf16[16,768]{1,0:T(8,128)(2,1)S(1)}, u32[]{:S(2)}, u32[]{:S(2)}) collective-permute-start(bf16[16,768]{1,0:T(8,128)(2,1)S(1)} %shard_map.136.own), channel_id=1, source_target_pairs={{0,48},{16,32},{32,16},{48,0},{64,112},{80,96},{96,80},{112,64},{1... | collective-permute-start | bytes 73736 | tf_op jit(solution)/shard_map/ppermute | solution.py:286
  50.2 1.2 %collective-permute-done.12.c = bf16[16,768]{1,0:T(8,128)(2,1)S(1)} collective-permute-done((bf16[16,768]{1,0:T(8,128)(2,1)S(1)}, bf16[16,768]{1,0:T(8,128)(2,1)S(1)}, u32[]{:S(2)}, u32[]{:S(2)}) %collective-permute-start.12) | collective-permute-done | bytes 24608 | tf_op jit(solution)/shard_map/ppermute | solution.py:286
  51.4 2.2 %collective-permute-done.11.b = bf16[16,768]{1,0:T(8,128)(2,1)S(1)} collective-permute-done((bf16[16,768]{1,0:T(8,128)(2,1)S(1)}, bf16[16,768]{1,0:T(8,128)(2,1)S(1)}, u32[]{:S(2)}, u32[]{:S(2)}) %collective-permute-start.11) | collective-permute-done | bytes 24608 | tf_op jit(solution)/shard_map/ppermute | solution.py:286
  54.1 6.3 %collective-permute-start.15 = (bf16[16,768]{1,0:T(8,128)(2,1)S(1)}, bf16[16,768]{1,0:T(8,128)(2,1)S(1)}, u32[]{:S(2)}, u32[]{:S(2)}) collective-permute-start(bf16[16,768]{1,0:T(8,128)(2,1)S(1)} %get-tuple-element.56.own), channel_id=1, source_target_pairs={{0,128},{16,144},{32,160},{48,176},{64,192},{80,208},{96,224},{112... | collective-permute-start | bytes 73736 | tf_op jit(solution)/shard_map/ppermute | solution.py:286
  62.0 1.2 %shard_map.139.picked = bf16[128,1536]{1,0:T(8,128)(2,1)S(1)} custom-call(bf16[1,128,1024]{2,1,0:T(8,128)(2,1)S(1)} %copy-done.4, s32[1,1024]{1,0:T(1,128)S(1)} %copy-done.6), custom_call_target="tpu_custom_call" | custom-call | flops 402653184 | bytes 2097152 | tf_op jit(solution)/shard_map/pallas_call | solution.py:274
  63.1 2.7 %collective-permute-done.14.near = bf16[16,512]{1,0:T(8,128)(2,1)S(1)} collective-permute-done((bf16[16,512]{1,0:T(8,128)(2,1)S(1)}, bf16[16,512]{1,0:T(8,128)(2,1)S(1)}, u32[]{:S(2)}, u32[]{:S(2)}) %collective-permute-start.14) | collective-permute-done | bytes 16416 | tf_op jit(solution)/shard_map/ppermute | solution.py:286
  66.2 1.5 %shard_map.140 = bf16[16,16,768]{2,1,0:T(8,128)(2,1)S(1)} custom-call(bf16[16,768]{1,0:T(8,128)(2,1)S(1)} %get-tuple-element.56.own, bf16[16,512]{1,0:T(8,128)(2,1)S(1)} %collective-permute-done.14.near, bf16[16,768]{1,0:T(8,128)(2,1)S(1)} %collective-permute-done.15.far, bf16[16,256]{1,0:T(8,128)(2,1)S(1)} %collective-permute-done.16.other, ...), custom_call_target="tpu_custom_call" | custom-call | flops 1207959552 | bytes 5242880 | tf_op jit(solution)/shard_map/pallas_call | solution.py:274
  67.8 13.4 %all_to_all.16.got = bf16[16,16,768]{2,1,0:T(8,128)(2,1)S(1)} all-to-all(bf16[16,16,768]{2,1,0:T(8,128)(2,1)S(1)} %shard_map.140), channel_id=1, replica_groups=mesh['leaf'=16,'front'=16] {'front'}, dimensions={0} | all-to-all | bytes 786432 | tf_op jit(solution)/shard_map/all_to_all | solution.py:304
  81.2 1.2 %shard_map.141 = (bf16[16,128,128]{2,1,0:T(8,128)(2,1)}, f32[96,128]{1,0:T(8,128)S(1)}, bf16[64,128]{1,0:T(8,128)(2,1)S(1)}, bf16[32,128]{1,0:T(8,128)(2,1)S(1)}) custom-call(bf16[16,16,768]{2,1,0:T(8,128)(2,1)S(1)} %all_to_all.16.got, f32[128,128]{1,0:T(8,128)S(1)} %get-tuple-element.62.solved, bf16[128,1536]{1,0:T(8,128)(2,1)S(1)} %shard_map.139.picked), custom_call_target="tpu_custom_call" | custom-call | flops 100663296 | bytes 2097152 | tf_op jit(solution)/shard_map/pallas_call | solution.py:274
  82.4 4.8 %all-to-all-start.2 = ((bf16[16,128,128]{2,1,0:T(8,128)(2,1)}), bf16[16,128,128]{2,1,0:T(8,128)(2,1)S(1)}, u32[]{:S(2)}, u32[]{:S(2)}) async-start(bf16[16,128,128]{2,1,0:T(8,128)(2,1)} %get-tuple-element.64), calls=%async_computation.2 | async-start | bytes 1048576 | tf_op jit(solution)/shard_map/all_to_all | solution.py:304
  87.2 3.9 %collective-permute-start.19 = (bf16[64,128]{1,0:T(8,128)(2,1)S(1)}, bf16[64,128]{1,0:T(8,128)(2,1)S(1)}, u32[]{:S(2)}, u32[]{:S(2)}) collective-permute-start(bf16[64,128]{1,0:T(8,128)(2,1)S(1)} %get-tuple-element.67), channel_id=1, source_target_pairs={{0,128},{16,144},{32,160},{48,176},{64,192},{80,208},{96,224},{112... | collective-permute-start | bytes 49160 | tf_op jit(solution)/shard_map/ppermute | solution.py:286
  91.1 1.1 %collective-permute-start.20 = (bf16[32,128]{1,0:T(8,128)(2,1)S(1)}, bf16[32,128]{1,0:T(8,128)(2,1)S(1)}, u32[]{:S(2)}, u32[]{:S(2)}) collective-permute-start(bf16[32,128]{1,0:T(8,128)(2,1)S(1)} %get-tuple-element.66), channel_id=1, source_target_pairs={{0,192},{16,208},{32,224},{48,240},{64,128},{80,144},{96,160},{112... | collective-permute-start | bytes 24584 | tf_op jit(solution)/shard_map/ppermute | solution.py:286
  92.2 1.5 %collective-permute-start.18 = (bf16[32,128]{1,0:T(8,128)(2,1)S(1)}, bf16[32,128]{1,0:T(8,128)(2,1)S(1)}, u32[]{:S(2)}, u32[]{:S(2)}) collective-permute-start(bf16[32,128]{1,0:T(8,128)(2,1)S(1)} %get-tuple-element.66), channel_id=1, source_target_pairs={{0,64},{16,80},{32,96},{48,112},{64,0},{80,16},{96,32},{112,48},{1... | collective-permute-start | bytes 24584 | tf_op jit(solution)/shard_map/ppermute | solution.py:286
  93.7 3.2 %collective-permute-done.20.other = bf16[32,128]{1,0:T(8,128)(2,1)S(1)} collective-permute-done((bf16[32,128]{1,0:T(8,128)(2,1)S(1)}, bf16[32,128]{1,0:T(8,128)(2,1)S(1)}, u32[]{:S(2)}, u32[]{:S(2)}) %collective-permute-start.20) | collective-permute-done | bytes 8224 | tf_op jit(solution)/shard_map/ppermute | solution.py:286
  (48 shorter events, 11.9 us)
Async XLA Ops:
  1.6 5.7 %collective-permute-start.2 = (bf16[192,512]{1,0:T(8,128)(2,1)S(1)}, bf16[192,512]{1,0:T(8,128)(2,1)S(1)}, u32[]{:S(2)}, u32[]{:S(2)}) collective-permute-start(bf16[192,512]{1,0:T(8,128)(2,1)S(1)} %shard_map.131.own), channel_id=1, source_target_pairs={{0,3},{1,0},{2,1},{3,2},{4,7},{5,4},{6,5},{7,6},{8,11},{9,8},{10,9... | collective-permute-start | bytes 589832 | tf_op jit(solution)/shard_map/ppermute | solution.py:298
  4.0 7.2 %collective-permute-start.1 = (bf16[192,512]{1,0:T(8,128)(2,1)S(1)}, bf16[192,512]{1,0:T(8,128)(2,1)S(1)}, u32[]{:S(2)}, u32[]{:S(2)}) collective-permute-start(bf16[192,512]{1,0:T(8,128)(2,1)S(1)} %shard_map.131.own), channel_id=1, source_target_pairs={{0,2},{1,3},{2,0},{3,1},{4,6},{5,7},{6,4},{7,5},{8,10},{9,11},{10,... | collective-permute-start | bytes 589832 | tf_op jit(solution)/shard_map/ppermute | solution.py:298
  4.7 6.9 %collective-permute-start = (bf16[192,512]{1,0:T(8,128)(2,1)S(1)}, bf16[192,512]{1,0:T(8,128)(2,1)S(1)}, u32[]{:S(2)}, u32[]{:S(2)}) collective-permute-start(bf16[192,512]{1,0:T(8,128)(2,1)S(1)} %shard_map.131.own), channel_id=1, source_target_pairs={{0,1},{1,2},{2,3},{3,0},{4,5},{5,6},{6,7},{7,4},{8,9},{9,10},{10,1... | collective-permute-start | bytes 589832 | tf_op jit(solution)/shard_map/ppermute | solution.py:298
  11.6 16.0 %copy-start.1 = (bf16[1,128,2048]{2,1,0:T(8,128)(2,1)S(1)}, bf16[1,128,2048]{2,1,0:T(8,128)(2,1)}, u32[]{:S(2)}) copy-start(bf16[1,128,2048]{2,1,0:T(8,128)(2,1)} %inverse.2) | copy-start | bytes 1572868
  11.6 9.8 %collective-permute-start.5 = (bf16[4,64,512]{2,1,0:T(8,128)(2,1)S(1)}, bf16[4,64,512]{2,1,0:T(8,128)(2,1)S(1)}, u32[]{:S(2)}, u32[]{:S(2)}) collective-permute-start(bf16[4,64,512]{2,1,0:T(8,128)(2,1)S(1)} %get-tuple-element.35.own), channel_id=1, source_target_pairs={{0,12},{1,13},{2,14},{3,15},{4,0},{5,1},{6,2},{7,3},{8,4},{9,5},{1... | collective-permute-start | bytes 786440 | tf_op jit(solution)/shard_map/ppermute | solution.py:298
  14.7 8.0 %collective-permute-start.4 = (bf16[4,64,512]{2,1,0:T(8,128)(2,1)S(1)}, bf16[4,64,512]{2,1,0:T(8,128)(2,1)S(1)}, u32[]{:S(2)}, u32[]{:S(2)}) collective-permute-start(bf16[4,64,512]{2,1,0:T(8,128)(2,1)S(1)} %get-tuple-element.35.own), channel_id=1, source_target_pairs={{0,8},{1,9},{2,10},{3,11},{4,12},{5,13},{6,14},{7,15},{8,0},{9,1},... | collective-permute-start | bytes 786440 | tf_op jit(solution)/shard_map/ppermute | solution.py:298
  15.3 10.1 %collective-permute-start.3 = (bf16[4,64,512]{2,1,0:T(8,128)(2,1)S(1)}, bf16[4,64,512]{2,1,0:T(8,128)(2,1)S(1)}, u32[]{:S(2)}, u32[]{:S(2)}) collective-permute-start(bf16[4,64,512]{2,1,0:T(8,128)(2,1)S(1)} %get-tuple-element.35.own), channel_id=1, source_target_pairs={{0,4},{1,5},{2,6},{3,7},{4,8},{5,9},{6,10},{7,11},{8,12},{9,13},{1... | collective-permute-start | bytes 786440 | tf_op jit(solution)/shard_map/ppermute | solution.py:298
  25.4 21.2 %collective-permute-start.8 = (bf16[4,128,512]{2,1,0:T(8,128)(2,1)S(1)}, bf16[4,128,512]{2,1,0:T(8,128)(2,1)S(1)}, u32[]{:S(2)}, u32[]{:S(2)}) collective-permute-start(bf16[4,128,512]{2,1,0:T(8,128)(2,1)S(1)} %get-tuple-element.44.own), channel_id=1, source_target_pairs={{0,12},{1,13},{2,14},{3,15},{4,0},{5,1},{6,2},{7,3},{8,4},{9,5},{1... | collective-permute-start | bytes 1572872 | tf_op jit(solution)/shard_map/ppermute | solution.py:298
  26.0 20.6 %collective-permute-start.7 = (bf16[4,128,512]{2,1,0:T(8,128)(2,1)S(1)}, bf16[4,128,512]{2,1,0:T(8,128)(2,1)S(1)}, u32[]{:S(2)}, u32[]{:S(2)}) collective-permute-start(bf16[4,128,512]{2,1,0:T(8,128)(2,1)S(1)} %get-tuple-element.44.own), channel_id=1, source_target_pairs={{0,8},{1,9},{2,10},{3,11},{4,12},{5,13},{6,14},{7,15},{8,0},{9,1},... | collective-permute-start | bytes 1572872 | tf_op jit(solution)/shard_map/ppermute | solution.py:298
  26.6 20.0 %collective-permute-start.6 = (bf16[4,128,512]{2,1,0:T(8,128)(2,1)S(1)}, bf16[4,128,512]{2,1,0:T(8,128)(2,1)S(1)}, u32[]{:S(2)}, u32[]{:S(2)}) collective-permute-start(bf16[4,128,512]{2,1,0:T(8,128)(2,1)S(1)} %get-tuple-element.44.own), channel_id=1, source_target_pairs={{0,4},{1,5},{2,6},{3,7},{4,8},{5,9},{6,10},{7,11},{8,12},{9,13},{1... | collective-permute-start | bytes 1572872 | tf_op jit(solution)/shard_map/ppermute | solution.py:298
  27.5 19.3 %collective-permute-start.9 = (bf16[512,512]{1,0:T(8,128)(2,1)S(1)}, bf16[512,512]{1,0:T(8,128)(2,1)S(1)}, u32[]{:S(2)}, u32[]{:S(2)}) collective-permute-start(bf16[512,512]{1,0:T(8,128)(2,1)S(1)} %shard_map.135.first), channel_id=1, source_target_pairs={{0,16},{16,0},{32,48},{48,32},{64,80},{80,64},{96,112},{112,96},{1... | collective-permute-start | bytes 1572872 | tf_op jit(solution)/shard_map/ppermute | solution.py:286
  47.6 18.6 %collective-permute-start.17 = (bf16[3,512,512]{2,1,0:T(8,128)(2,1)S(1)}, bf16[3,512,512]{2,1,0:T(8,128)(2,1)S(1)}, u32[]{:S(2)}, u32[]{:S(2)}) collective-permute-start(bf16[3,512,512]{2,1,0:T(8,128)(2,1)S(1)} %get-tuple-element.61.later), channel_id=1, source_target_pairs={{0,16},{16,0},{32,48},{48,32},{64,80},{80,64},{96,112},{112,96},{1... | collective-permute-start | bytes 4718600 | tf_op jit(solution)/shard_map/ppermute | solution.py:286
  47.6 6.0 %collective-permute-start.13 = (bf16[512,512]{1,0:T(8,128)(2,1)S(1)}, bf16[512,512]{1,0:T(8,128)(2,1)S(1)}, u32[]{:S(2)}, u32[]{:S(2)}) collective-permute-start(bf16[512,512]{1,0:T(8,128)(2,1)S(1)} %get-tuple-element.53.first), channel_id=1, source_target_pairs={{0,16},{16,0},{32,48},{48,32},{64,80},{80,64},{96,112},{112,96},{1... | collective-permute-start | bytes 1572872 | tf_op jit(solution)/shard_map/ppermute | solution.py:286
  48.1 3.3 %collective-permute-start.12 = (bf16[16,768]{1,0:T(8,128)(2,1)S(1)}, bf16[16,768]{1,0:T(8,128)(2,1)S(1)}, u32[]{:S(2)}, u32[]{:S(2)}) collective-permute-start(bf16[16,768]{1,0:T(8,128)(2,1)S(1)} %shard_map.136.own), channel_id=1, source_target_pairs={{0,48},{16,32},{32,16},{48,0},{64,112},{80,96},{96,80},{112,64},{1... | collective-permute-start | bytes 73736 | tf_op jit(solution)/shard_map/ppermute | solution.py:286
  49.7 3.8 %collective-permute-start.11 = (bf16[16,768]{1,0:T(8,128)(2,1)S(1)}, bf16[16,768]{1,0:T(8,128)(2,1)S(1)}, u32[]{:S(2)}, u32[]{:S(2)}) collective-permute-start(bf16[16,768]{1,0:T(8,128)(2,1)S(1)} %shard_map.136.own), channel_id=1, source_target_pairs={{0,32},{16,48},{32,0},{48,16},{64,96},{80,112},{96,64},{112,80},{1... | collective-permute-start | bytes 73736 | tf_op jit(solution)/shard_map/ppermute | solution.py:286
  50.1 3.5 %collective-permute-start.10 = (bf16[16,768]{1,0:T(8,128)(2,1)S(1)}, bf16[16,768]{1,0:T(8,128)(2,1)S(1)}, u32[]{:S(2)}, u32[]{:S(2)}) collective-permute-start(bf16[16,768]{1,0:T(8,128)(2,1)S(1)} %shard_map.136.own), channel_id=1, source_target_pairs={{0,16},{16,0},{32,48},{48,32},{64,80},{80,64},{96,112},{112,96},{1... | collective-permute-start | bytes 73736 | tf_op jit(solution)/shard_map/ppermute | solution.py:286
  54.1 12.1 %collective-permute-start.15 = (bf16[16,768]{1,0:T(8,128)(2,1)S(1)}, bf16[16,768]{1,0:T(8,128)(2,1)S(1)}, u32[]{:S(2)}, u32[]{:S(2)}) collective-permute-start(bf16[16,768]{1,0:T(8,128)(2,1)S(1)} %get-tuple-element.56.own), channel_id=1, source_target_pairs={{0,128},{16,144},{32,160},{48,176},{64,192},{80,208},{96,224},{112... | collective-permute-start | bytes 73736 | tf_op jit(solution)/shard_map/ppermute | solution.py:286
  60.5 5.8 %collective-permute-start.16 = (bf16[16,256]{1,0:T(8,128)(2,1)S(1)}, bf16[16,256]{1,0:T(8,128)(2,1)S(1)}, u32[]{:S(2)}, u32[]{:S(2)}) collective-permute-start(bf16[16,256]{1,0:T(8,128)(2,1)S(1)} %get-tuple-element.60), channel_id=1, source_target_pairs={{0,192},{16,208},{32,224},{48,240},{64,128},{80,144},{96,160},{112... | collective-permute-start | bytes 24584 | tf_op jit(solution)/shard_map/ppermute | solution.py:286
  61.0 4.8 %collective-permute-start.14 = (bf16[16,512]{1,0:T(8,128)(2,1)S(1)}, bf16[16,512]{1,0:T(8,128)(2,1)S(1)}, u32[]{:S(2)}, u32[]{:S(2)}) collective-permute-start(bf16[16,512]{1,0:T(8,128)(2,1)S(1)} %get-tuple-element.57), channel_id=1, source_target_pairs={{0,64},{16,80},{32,96},{48,112},{64,0},{80,16},{96,32},{112,48},{1... | collective-permute-start | bytes 49160 | tf_op jit(solution)/shard_map/ppermute | solution.py:286
  67.8 29.1 %copy-start = (bf16[1,128,2048]{2,1,0:T(8,128)(2,1)S(1)}, bf16[1,128,2048]{2,1,0:T(8,128)(2,1)}, u32[]{:S(2)}) copy-start(bf16[1,128,2048]{2,1,0:T(8,128)(2,1)} %inverse.3) | copy-start | bytes 1572868
  82.4 14.5 %all-to-all-start.2 = ((bf16[16,128,128]{2,1,0:T(8,128)(2,1)}), bf16[16,128,128]{2,1,0:T(8,128)(2,1)S(1)}, u32[]{:S(2)}, u32[]{:S(2)}) async-start(bf16[16,128,128]{2,1,0:T(8,128)(2,1)} %get-tuple-element.64), calls=%async_computation.2 | async-start | bytes 1048576 | tf_op jit(solution)/shard_map/all_to_all | solution.py:304
  87.2 9.7 %collective-permute-start.19 = (bf16[64,128]{1,0:T(8,128)(2,1)S(1)}, bf16[64,128]{1,0:T(8,128)(2,1)S(1)}, u32[]{:S(2)}, u32[]{:S(2)}) collective-permute-start(bf16[64,128]{1,0:T(8,128)(2,1)S(1)} %get-tuple-element.67), channel_id=1, source_target_pairs={{0,128},{16,144},{32,160},{48,176},{64,192},{80,208},{96,224},{112... | collective-permute-start | bytes 49160 | tf_op jit(solution)/shard_map/ppermute | solution.py:286
  91.1 5.8 %collective-permute-start.20 = (bf16[32,128]{1,0:T(8,128)(2,1)S(1)}, bf16[32,128]{1,0:T(8,128)(2,1)S(1)}, u32[]{:S(2)}, u32[]{:S(2)}) collective-permute-start(bf16[32,128]{1,0:T(8,128)(2,1)S(1)} %get-tuple-element.66), channel_id=1, source_target_pairs={{0,192},{16,208},{32,224},{48,240},{64,128},{80,144},{96,160},{112... | collective-permute-start | bytes 24584 | tf_op jit(solution)/shard_map/ppermute | solution.py:286
  92.2 4.7 %collective-permute-start.18 = (bf16[32,128]{1,0:T(8,128)(2,1)S(1)}, bf16[32,128]{1,0:T(8,128)(2,1)S(1)}, u32[]{:S(2)}, u32[]{:S(2)}) collective-permute-start(bf16[32,128]{1,0:T(8,128)(2,1)S(1)} %get-tuple-element.66), channel_id=1, source_target_pairs={{0,64},{16,80},{32,96},{48,112},{64,0},{80,16},{96,32},{112,48},{1... | collective-permute-start | bytes 24584 | tf_op jit(solution)/shard_map/ppermute | solution.py:286
  (5 other events, 78.2 us)

commit v3 on v2

--- a/solution.py
+++ b/solution.py
@@ -347,7 +347,7 @@
         flops=2 * UPD * SPAN * PIECE,
         size=2 << 20,
     )
-    later, spread, *parts = lax.optimization_barrier((later, spread, *parts))
+    spread, *parts = lax.optimization_barrier((spread, *parts))
     (ahead,) = call(functools.partial(assemble_kernel, 1), [((SEP, SEP), BF)], (early, *parts), size=1 << 20)
     swapped = swap(ahead, 1)
     solved, send = call(

time: 98.1 us -> 95.6 us (0.975)
  blocking collectives: 31.7 us -> 12.5 us
  starting transfers between devices: 33.3 us -> 41.4 us
  waiting for transfers between devices: 22.6 us -> 28.3 us
  local copies, waits for them, and re-layouts: 0.04 us -> 1.42 us
  Pallas kernels: 9.35 us -> 10.7 us
    all_to_all x2 -> x1, blocking collectives: 31.7 us -> 12.5 us  [exchange(): return lax.all_to_all(x, axis, 0, 0, tiled=True, axis_index_groups=groups)]
    all_to_all x1 -> x2, waiting for transfers between devices: 0.01 us -> 6.75 us  [exchange(): return lax.all_to_all(x, axis, 0, 0, tiled=True, axis_index_groups=groups)]
    all_to_all x1 -> x2, starting transfers between devices: 4.82 us -> 10.9 us  [exchange(): return lax.all_to_all(x, axis, 0, 0, tiled=True, axis_index_groups=groups)]
    ppermute x9, starting transfers between devices: 11.6 us -> 13.6 us  [shifts(): lax.ppermute(x, ('leaf', 'front'), [(leaf * FRONT + front, moved(leaf, fr...]
    pallas_call x12, Pallas kernels: 9.35 us -> 10.7 us  [call(): pl.pallas_call(kernel, out_shape=shapes, in_specs=specs or [VMEM] * len(a...]
    unnamed x14 -> x20, local copies, waits for them, and re-layouts: 0.04 us -> 1.42 us
    ppermute x9, waiting for transfers between devices: 12.9 us -> 11.9 us  [shifts(): lax.ppermute(x, ('leaf', 'front'), [(leaf * FRONT + front, moved(leaf, fr...]
  transfers between devices with their start and end apart: 22 -> 23, of which waited for: 11 -> 12; matrix products, arithmetic and copies ran while one was open for 0% -> 0% of each run, Pallas kernels for 4% -> 6%
where the time goes in v3:
time: 95.6 us; the launch traced here: 95.2 us
  starting transfers between devices  41.4 us (43%)
  waiting for transfers between devices  28.3 us (30%)
  blocking collectives  12.5 us (13%)
  Pallas kernels  10.7 us (11%)
  local copies, waits for them, and re-layouts  1.42 us (1%)
    ppermute x12, starting transfers between devices, swap(): return lax.ppermute(x, 'leaf', [(i, i ^ flip) for i in range(LEAVES)])  16.9 us
    ppermute x9, starting transfers between devices, shifts(): lax.ppermute(x, ('leaf', 'front'), [(leaf * FRONT + front, moved(leaf, fr...  13.6 us
    all_to_all x1, blocking collectives, exchange(): return lax.all_to_all(x, axis, 0, 0, tiled=True, axis_index_groups=groups)  12.5 us
    ppermute x9, waiting for transfers between devices, shifts(): lax.ppermute(x, ('leaf', 'front'), [(leaf * FRONT + front, moved(leaf, fr...  11.9 us
    all_to_all x2, starting transfers between devices, exchange(): return lax.all_to_all(x, axis, 0, 0, tiled=True, axis_index_groups=groups)  10.9 us
    pallas_call x12, Pallas kernels, call(): pl.pallas_call(kernel, out_shape=shapes, in_specs=specs or [VMEM] * len(a...  10.7 us
    ppermute x12, waiting for transfers between devices, swap(): return lax.ppermute(x, 'leaf', [(i, i ^ flip) for i in range(LEAVES)])  9.7 us
    all_to_all x2, waiting for transfers between devices, exchange(): return lax.all_to_all(x, axis, 0, 0, tiled=True, axis_index_groups=groups)  6.75 us
  transfers between devices with their start and end apart: 23, of which 12 were waited for; matrix products, arithmetic and copies ran while one was open for 0% of the time, Pallas kernels for 6%

profile of v3, /device:TPU:2, one launch (start us, length us, event | category | flops | bytes accessed | tf_op | source)
XLA Modules:
  0.0 95.2 jit_solution(1622935454819413208)
XLA Ops:
  1.6 2.3 %collective-permute-start.2 = (bf16[192,512]{1,0:T(8,128)(2,1)S(1)}, bf16[192,512]{1,0:T(8,128)(2,1)S(1)}, u32[]{:S(2)}, u32[]{:S(2)}) collective-permute-start(bf16[192,512]{1,0:T(8,128)(2,1)S(1)} %shard_map.131.own), channel_id=1, source_target_pairs={{0,3},{1,0},{2,1},{3,2},{4,7},{5,4},{6,5},{7,6},{8,11},{9,8},{10,9... | collective-permute-start | bytes 589832 | tf_op jit(solution)/shard_map/ppermute | solution.py:298
  4.7 1.8 %collective-permute-start = (bf16[192,512]{1,0:T(8,128)(2,1)S(1)}, bf16[192,512]{1,0:T(8,128)(2,1)S(1)}, u32[]{:S(2)}, u32[]{:S(2)}) collective-permute-start(bf16[192,512]{1,0:T(8,128)(2,1)S(1)} %shard_map.131.own), channel_id=1, source_target_pairs={{0,1},{1,2},{2,3},{3,0},{4,5},{5,6},{6,7},{7,4},{8,9},{9,10},{10,1... | collective-permute-start | bytes 589832 | tf_op jit(solution)/shard_map/ppermute | solution.py:298
  7.4 3.8 %collective-permute-done.1.b = bf16[192,512]{1,0:T(8,128)(2,1)S(1)} collective-permute-done((bf16[192,512]{1,0:T(8,128)(2,1)S(1)}, bf16[192,512]{1,0:T(8,128)(2,1)S(1)}, u32[]{:S(2)}, u32[]{:S(2)}) %collective-permute-start.1) | collective-permute-done | bytes 196640 | tf_op jit(solution)/shard_map/ppermute | solution.py:298
  11.6 3.1 %collective-permute-start.5 = (bf16[4,64,512]{2,1,0:T(8,128)(2,1)S(1)}, bf16[4,64,512]{2,1,0:T(8,128)(2,1)S(1)}, u32[]{:S(2)}, u32[]{:S(2)}) collective-permute-start(bf16[4,64,512]{2,1,0:T(8,128)(2,1)S(1)} %get-tuple-element.34.own), channel_id=1, source_target_pairs={{0,12},{1,13},{2,14},{3,15},{4,0},{5,1},{6,2},{7,3},{8,4},{9,5},{1... | collective-permute-start | bytes 786440 | tf_op jit(solution)/shard_map/ppermute | solution.py:298
  16.3 1.3 %shard_map.133 = (bf16[1536,128]{1,0:T(8,128)(2,1)S(1)}, bf16[512,512]{1,0:T(8,128)(2,1)S(1)}, bf16[1024,512]{1,0:T(8,128)(2,1)S(1)}) custom-call(bf16[1,1024,128]{2,1,0:T(8,128)(2,1)S(1)} %copy-done.6, s32[1,1024]{1,0:T(1,128)S(1)} %copy-done.9, s32[6,512]{1,0:T(8,128)S(1)} %copy-done.8), custom_call_target="tpu_custom_call" | custom-call | flops 402653184 | bytes 2097152 | tf_op jit(solution)/shard_map/pallas_call | solution.py:274
  17.6 2.3 %collective-permute-start.8 = (bf16[4,128,512]{2,1,0:T(8,128)(2,1)S(1)}, bf16[4,128,512]{2,1,0:T(8,128)(2,1)}, u32[]{:S(2)}, u32[]{:S(2)}) collective-permute-start(bf16[4,128,512]{2,1,0:T(8,128)(2,1)S(1)} %get-tuple-element.42.own), channel_id=1, source_target_pairs={{0,12},{1,13},{2,14},{3,15},{4,0},{5,1},{6,2},{7,3},{8,4},{9,5},{1... | collective-permute-start | bytes 1572872 | tf_op jit(solution)/shard_map/ppermute | solution.py:298
  19.9 1.7 %collective-permute-start.7 = (bf16[4,128,512]{2,1,0:T(8,128)(2,1)S(1)}, bf16[4,128,512]{2,1,0:T(8,128)(2,1)}, u32[]{:S(2)}, u32[]{:S(2)}) collective-permute-start(bf16[4,128,512]{2,1,0:T(8,128)(2,1)S(1)} %get-tuple-element.42.own), channel_id=1, source_target_pairs={{0,8},{1,9},{2,10},{3,11},{4,12},{5,13},{6,14},{7,15},{8,0},{9,1},... | collective-permute-start | bytes 1572872 | tf_op jit(solution)/shard_map/ppermute | solution.py:298
  22.7 2.7 %collective-permute-done.3.a = bf16[4,64,512]{2,1,0:T(8,128)(2,1)S(1)} collective-permute-done((bf16[4,64,512]{2,1,0:T(8,128)(2,1)S(1)}, bf16[4,64,512]{2,1,0:T(8,128)(2,1)S(1)}, u32[]{:S(2)}, u32[]{:S(2)}) %collective-permute-start.3) | collective-permute-done | bytes 262176 | tf_op jit(solution)/shard_map/ppermute | solution.py:298
  27.7 6.1 %all-to-all-start = ((bf16[16,16,768]{2,1,0:T(8,128)(2,1)}), bf16[16,16,768]{2,1,0:T(8,128)(2,1)S(1)}, u32[]{:S(2)}, u32[]{:S(2)}) async-start(bf16[16,16,768]{2,1,0:T(8,128)(2,1)} %copy-done.2), calls=%async_computation | async-start | bytes 786432 | tf_op jit(solution)/shard_map/all_to_all | solution.py:304
  33.8 3.0 %collective-permute-done.6.a = bf16[4,128,512]{2,1,0:T(8,128)(2,1)} collective-permute-done((bf16[4,128,512]{2,1,0:T(8,128)(2,1)S(1)}, bf16[4,128,512]{2,1,0:T(8,128)(2,1)}, u32[]{:S(2)}, u32[]{:S(2)}) %collective-permute-start.6) | collective-permute-done | bytes 524320 | tf_op jit(solution)/shard_map/ppermute | solution.py:298
  36.8 6.8 %all-to-all-done.got = bf16[16,16,768]{2,1,0:T(8,128)(2,1)S(1)} async-done(((bf16[16,16,768]{2,1,0:T(8,128)(2,1)}), bf16[16,16,768]{2,1,0:T(8,128)(2,1)S(1)}, u32[]{:S(2)}, u32[]{:S(2)}) %all-to-all-start) | async-done | bytes 393248 | tf_op jit(solution)/shard_map/all_to_all | solution.py:304
  43.5 1.6 %shard_map.137 = (bf16[512,512]{1,0:T(8,128)(2,1)S(1)}, bf16[3,512,512]{2,1,0:T(8,128)(2,1)S(1)}) custom-call(bf16[4,128,512]{2,1,0:T(8,128)(2,1)S(1)} %get-tuple-element.42.own, bf16[4,128,512]{2,1,0:T(8,128)(2,1)} %collective-permute-done.6.a, bf16[4,128,512]{2,1,0:T(8,128)(2,1)} %collective-permute-done.7.b, bf16[4,128,512]{2,1,0:T(8,128)(2,1)} %collective-permute-done.8.c), custom_call_target="tpu_custom_call" | custom-call | bytes 4194304 | tf_op jit(solution)/shard_map/pallas_call | solution.py:274
  46.4 1.6 %collective-permute-start.12 = (bf16[16,768]{1,0:T(8,128)(2,1)S(1)}, bf16[16,768]{1,0:T(8,128)(2,1)S(1)}, u32[]{:S(2)}, u32[]{:S(2)}) collective-permute-start(bf16[16,768]{1,0:T(8,128)(2,1)S(1)} %shard_map.136.own), channel_id=1, source_target_pairs={{0,48},{16,32},{32,16},{48,0},{64,112},{80,96},{96,80},{112,64},{1... | collective-permute-start | bytes 73736 | tf_op jit(solution)/shard_map/ppermute | solution.py:286
  48.4 1.2 %collective-permute-done.12.c = bf16[16,768]{1,0:T(8,128)(2,1)S(1)} collective-permute-done((bf16[16,768]{1,0:T(8,128)(2,1)S(1)}, bf16[16,768]{1,0:T(8,128)(2,1)S(1)}, u32[]{:S(2)}, u32[]{:S(2)}) %collective-permute-start.12) | collective-permute-done | bytes 24608 | tf_op jit(solution)/shard_map/ppermute | solution.py:286
  49.7 2.2 %collective-permute-done.11.b = bf16[16,768]{1,0:T(8,128)(2,1)S(1)} collective-permute-done((bf16[16,768]{1,0:T(8,128)(2,1)S(1)}, bf16[16,768]{1,0:T(8,128)(2,1)S(1)}, u32[]{:S(2)}, u32[]{:S(2)}) %collective-permute-start.11) | collective-permute-done | bytes 24608 | tf_op jit(solution)/shard_map/ppermute | solution.py:286
  52.4 6.3 %collective-permute-start.15 = (bf16[16,768]{1,0:T(8,128)(2,1)S(1)}, bf16[16,768]{1,0:T(8,128)(2,1)S(1)}, u32[]{:S(2)}, u32[]{:S(2)}) collective-permute-start(bf16[16,768]{1,0:T(8,128)(2,1)S(1)} %get-tuple-element.54.own), channel_id=1, source_target_pairs={{0,128},{16,144},{32,160},{48,176},{64,192},{80,208},{96,224},{112... | collective-permute-start | bytes 73736 | tf_op jit(solution)/shard_map/ppermute | solution.py:286
  61.4 2.7 %collective-permute-done.14.near = bf16[16,512]{1,0:T(8,128)(2,1)S(1)} collective-permute-done((bf16[16,512]{1,0:T(8,128)(2,1)S(1)}, bf16[16,512]{1,0:T(8,128)(2,1)S(1)}, u32[]{:S(2)}, u32[]{:S(2)}) %collective-permute-start.14) | collective-permute-done | bytes 16416 | tf_op jit(solution)/shard_map/ppermute | solution.py:286
  64.5 1.5 %shard_map.140 = bf16[16,16,768]{2,1,0:T(8,128)(2,1)S(1)} custom-call(bf16[16,768]{1,0:T(8,128)(2,1)S(1)} %get-tuple-element.54.own, bf16[16,512]{1,0:T(8,128)(2,1)S(1)} %collective-permute-done.14.near, bf16[16,768]{1,0:T(8,128)(2,1)S(1)} %collective-permute-done.15.far, bf16[16,256]{1,0:T(8,128)(2,1)S(1)} %collective-permute-done.16.other, ...), custom_call_target="tpu_custom_call" | custom-call | flops 1207959552 | bytes 5242880 | tf_op jit(solution)/shard_map/pallas_call | solution.py:274
  66.1 12.5 %all_to_all.15.got = bf16[16,16,768]{2,1,0:T(8,128)(2,1)S(1)} all-to-all(bf16[16,16,768]{2,1,0:T(8,128)(2,1)S(1)} %shard_map.140), channel_id=1, replica_groups=mesh['leaf'=16,'front'=16] {'front'}, dimensions={0} | all-to-all | bytes 786432 | tf_op jit(solution)/shard_map/all_to_all | solution.py:304
  78.5 1.2 %shard_map.141 = (bf16[16,128,128]{2,1,0:T(8,128)(2,1)}, f32[96,128]{1,0:T(8,128)S(1)}, bf16[64,128]{1,0:T(8,128)(2,1)S(1)}, bf16[32,128]{1,0:T(8,128)(2,1)S(1)}) custom-call(bf16[16,16,768]{2,1,0:T(8,128)(2,1)S(1)} %all_to_all.15.got, f32[128,128]{1,0:T(8,128)S(1)} %copy-done.5, bf16[128,1536]{1,0:T(8,128)(2,1)S(1)} %shard_map.139.picked), custom_call_target="tpu_custom_call" | custom-call | flops 100663296 | bytes 2097152 | tf_op jit(solution)/shard_map/pallas_call | solution.py:274
  79.8 4.8 %all-to-all-start.2 = ((bf16[16,128,128]{2,1,0:T(8,128)(2,1)}), bf16[16,128,128]{2,1,0:T(8,128)(2,1)S(1)}, u32[]{:S(2)}, u32[]{:S(2)}) async-start(bf16[16,128,128]{2,1,0:T(8,128)(2,1)} %get-tuple-element.62), calls=%async_computation.2 | async-start | bytes 1048576 | tf_op jit(solution)/shard_map/all_to_all | solution.py:304
  84.6 3.9 %collective-permute-start.19 = (bf16[64,128]{1,0:T(8,128)(2,1)S(1)}, bf16[64,128]{1,0:T(8,128)(2,1)S(1)}, u32[]{:S(2)}, u32[]{:S(2)}) collective-permute-start(bf16[64,128]{1,0:T(8,128)(2,1)S(1)} %get-tuple-element.65), channel_id=1, source_target_pairs={{0,128},{16,144},{32,160},{48,176},{64,192},{80,208},{96,224},{112... | collective-permute-start | bytes 49160 | tf_op jit(solution)/shard_map/ppermute | solution.py:286
  89.6 1.5 %collective-permute-start.18 = (bf16[32,128]{1,0:T(8,128)(2,1)S(1)}, bf16[32,128]{1,0:T(8,128)(2,1)S(1)}, u32[]{:S(2)}, u32[]{:S(2)}) collective-permute-start(bf16[32,128]{1,0:T(8,128)(2,1)S(1)} %get-tuple-element.64), channel_id=1, source_target_pairs={{0,64},{16,80},{32,96},{48,112},{64,0},{80,16},{96,32},{112,48},{1... | collective-permute-start | bytes 24584 | tf_op jit(solution)/shard_map/ppermute | solution.py:286
  91.1 3.2 %collective-permute-done.20.other = bf16[32,128]{1,0:T(8,128)(2,1)S(1)} collective-permute-done((bf16[32,128]{1,0:T(8,128)(2,1)S(1)}, bf16[32,128]{1,0:T(8,128)(2,1)S(1)}, u32[]{:S(2)}, u32[]{:S(2)}) %collective-permute-start.20) | collective-permute-done | bytes 8224 | tf_op jit(solution)/shard_map/ppermute | solution.py:286
  (55 shorter events, 15.4 us)
Async XLA Ops:
  1.6 5.7 %collective-permute-start.2 = (bf16[192,512]{1,0:T(8,128)(2,1)S(1)}, bf16[192,512]{1,0:T(8,128)(2,1)S(1)}, u32[]{:S(2)}, u32[]{:S(2)}) collective-permute-start(bf16[192,512]{1,0:T(8,128)(2,1)S(1)} %shard_map.131.own), channel_id=1, source_target_pairs={{0,3},{1,0},{2,1},{3,2},{4,7},{5,4},{6,5},{7,6},{8,11},{9,8},{10,9... | collective-permute-start | bytes 589832 | tf_op jit(solution)/shard_map/ppermute | solution.py:298
  4.0 7.2 %collective-permute-start.1 = (bf16[192,512]{1,0:T(8,128)(2,1)S(1)}, bf16[192,512]{1,0:T(8,128)(2,1)S(1)}, u32[]{:S(2)}, u32[]{:S(2)}) collective-permute-start(bf16[192,512]{1,0:T(8,128)(2,1)S(1)} %shard_map.131.own), channel_id=1, source_target_pairs={{0,2},{1,3},{2,0},{3,1},{4,6},{5,7},{6,4},{7,5},{8,10},{9,11},{10,... | collective-permute-start | bytes 589832 | tf_op jit(solution)/shard_map/ppermute | solution.py:298
  4.7 6.9 %collective-permute-start = (bf16[192,512]{1,0:T(8,128)(2,1)S(1)}, bf16[192,512]{1,0:T(8,128)(2,1)S(1)}, u32[]{:S(2)}, u32[]{:S(2)}) collective-permute-start(bf16[192,512]{1,0:T(8,128)(2,1)S(1)} %shard_map.131.own), channel_id=1, source_target_pairs={{0,1},{1,2},{2,3},{3,0},{4,5},{5,6},{6,7},{7,4},{8,9},{9,10},{10,1... | collective-permute-start | bytes 589832 | tf_op jit(solution)/shard_map/ppermute | solution.py:298
  11.6 10.0 %collective-permute-start.5 = (bf16[4,64,512]{2,1,0:T(8,128)(2,1)S(1)}, bf16[4,64,512]{2,1,0:T(8,128)(2,1)S(1)}, u32[]{:S(2)}, u32[]{:S(2)}) collective-permute-start(bf16[4,64,512]{2,1,0:T(8,128)(2,1)S(1)} %get-tuple-element.34.own), channel_id=1, source_target_pairs={{0,12},{1,13},{2,14},{3,15},{4,0},{5,1},{6,2},{7,3},{8,4},{9,5},{1... | collective-permute-start | bytes 786440 | tf_op jit(solution)/shard_map/ppermute | solution.py:298
  14.7 8.0 %collective-permute-start.4 = (bf16[4,64,512]{2,1,0:T(8,128)(2,1)S(1)}, bf16[4,64,512]{2,1,0:T(8,128)(2,1)S(1)}, u32[]{:S(2)}, u32[]{:S(2)}) collective-permute-start(bf16[4,64,512]{2,1,0:T(8,128)(2,1)S(1)} %get-tuple-element.34.own), channel_id=1, source_target_pairs={{0,8},{1,9},{2,10},{3,11},{4,12},{5,13},{6,14},{7,15},{8,0},{9,1},... | collective-permute-start | bytes 786440 | tf_op jit(solution)/shard_map/ppermute | solution.py:298
  15.3 10.1 %collective-permute-start.3 = (bf16[4,64,512]{2,1,0:T(8,128)(2,1)S(1)}, bf16[4,64,512]{2,1,0:T(8,128)(2,1)S(1)}, u32[]{:S(2)}, u32[]{:S(2)}) collective-permute-start(bf16[4,64,512]{2,1,0:T(8,128)(2,1)S(1)} %get-tuple-element.34.own), channel_id=1, source_target_pairs={{0,4},{1,5},{2,6},{3,7},{4,8},{5,9},{6,10},{7,11},{8,12},{9,13},{1... | collective-permute-start | bytes 786440 | tf_op jit(solution)/shard_map/ppermute | solution.py:298
  17.6 16.2 %collective-permute-start.8 = (bf16[4,128,512]{2,1,0:T(8,128)(2,1)S(1)}, bf16[4,128,512]{2,1,0:T(8,128)(2,1)}, u32[]{:S(2)}, u32[]{:S(2)}) collective-permute-start(bf16[4,128,512]{2,1,0:T(8,128)(2,1)S(1)} %get-tuple-element.42.own), channel_id=1, source_target_pairs={{0,12},{1,13},{2,14},{3,15},{4,0},{5,1},{6,2},{7,3},{8,4},{9,5},{1... | collective-permute-start | bytes 1572872 | tf_op jit(solution)/shard_map/ppermute | solution.py:298
  19.9 13.8 %collective-permute-start.7 = (bf16[4,128,512]{2,1,0:T(8,128)(2,1)S(1)}, bf16[4,128,512]{2,1,0:T(8,128)(2,1)}, u32[]{:S(2)}, u32[]{:S(2)}) collective-permute-start(bf16[4,128,512]{2,1,0:T(8,128)(2,1)S(1)} %get-tuple-element.42.own), channel_id=1, source_target_pairs={{0,8},{1,9},{2,10},{3,11},{4,12},{5,13},{6,14},{7,15},{8,0},{9,1},... | collective-permute-start | bytes 1572872 | tf_op jit(solution)/shard_map/ppermute | solution.py:298
  21.6 15.1 %collective-permute-start.6 = (bf16[4,128,512]{2,1,0:T(8,128)(2,1)S(1)}, bf16[4,128,512]{2,1,0:T(8,128)(2,1)}, u32[]{:S(2)}, u32[]{:S(2)}) collective-permute-start(bf16[4,128,512]{2,1,0:T(8,128)(2,1)S(1)} %get-tuple-element.42.own), channel_id=1, source_target_pairs={{0,4},{1,5},{2,6},{3,7},{4,8},{5,9},{6,10},{7,11},{8,12},{9,13},{1... | collective-permute-start | bytes 1572872 | tf_op jit(solution)/shard_map/ppermute | solution.py:298
  25.5 19.6 %collective-permute-start.9 = (bf16[512,512]{1,0:T(8,128)(2,1)S(1)}, bf16[512,512]{1,0:T(8,128)(2,1)S(1)}, u32[]{:S(2)}, u32[]{:S(2)}) collective-permute-start(bf16[512,512]{1,0:T(8,128)(2,1)S(1)} %shard_map.135.first), channel_id=1, source_target_pairs={{0,16},{16,0},{32,48},{48,32},{64,80},{80,64},{96,112},{112,96},{1... | collective-permute-start | bytes 1572872 | tf_op jit(solution)/shard_map/ppermute | solution.py:286
  27.7 15.8 %all-to-all-start = ((bf16[16,16,768]{2,1,0:T(8,128)(2,1)}), bf16[16,16,768]{2,1,0:T(8,128)(2,1)S(1)}, u32[]{:S(2)}, u32[]{:S(2)}) async-start(bf16[16,16,768]{2,1,0:T(8,128)(2,1)} %copy-done.2), calls=%async_computation | async-start | bytes 786432 | tf_op jit(solution)/shard_map/all_to_all | solution.py:304
  45.9 18.6 %collective-permute-start.17 = (bf16[3,512,512]{2,1,0:T(8,128)(2,1)S(1)}, bf16[3,512,512]{2,1,0:T(8,128)(2,1)S(1)}, u32[]{:S(2)}, u32[]{:S(2)}) collective-permute-start(bf16[3,512,512]{2,1,0:T(8,128)(2,1)S(1)} %get-tuple-element.59.later), channel_id=1, source_target_pairs={{0,16},{16,0},{32,48},{48,32},{64,80},{80,64},{96,112},{112,96},{1... | collective-permute-start | bytes 4718600 | tf_op jit(solution)/shard_map/ppermute | solution.py:286
  45.9 6.0 %collective-permute-start.13 = (bf16[512,512]{1,0:T(8,128)(2,1)S(1)}, bf16[512,512]{1,0:T(8,128)(2,1)S(1)}, u32[]{:S(2)}, u32[]{:S(2)}) collective-permute-start(bf16[512,512]{1,0:T(8,128)(2,1)S(1)} %get-tuple-element.51.first), channel_id=1, source_target_pairs={{0,16},{16,0},{32,48},{48,32},{64,80},{80,64},{96,112},{112,96},{1... | collective-permute-start | bytes 1572872 | tf_op jit(solution)/shard_map/ppermute | solution.py:286
  46.4 3.3 %collective-permute-start.12 = (bf16[16,768]{1,0:T(8,128)(2,1)S(1)}, bf16[16,768]{1,0:T(8,128)(2,1)S(1)}, u32[]{:S(2)}, u32[]{:S(2)}) collective-permute-start(bf16[16,768]{1,0:T(8,128)(2,1)S(1)} %shard_map.136.own), channel_id=1, source_target_pairs={{0,48},{16,32},{32,16},{48,0},{64,112},{80,96},{96,80},{112,64},{1... | collective-permute-start | bytes 73736 | tf_op jit(solution)/shard_map/ppermute | solution.py:286
  48.0 3.8 %collective-permute-start.11 = (bf16[16,768]{1,0:T(8,128)(2,1)S(1)}, bf16[16,768]{1,0:T(8,128)(2,1)S(1)}, u32[]{:S(2)}, u32[]{:S(2)}) collective-permute-start(bf16[16,768]{1,0:T(8,128)(2,1)S(1)} %shard_map.136.own), channel_id=1, source_target_pairs={{0,32},{16,48},{32,0},{48,16},{64,96},{80,112},{96,64},{112,80},{1... | collective-permute-start | bytes 73736 | tf_op jit(solution)/shard_map/ppermute | solution.py:286
  48.4 3.5 %collective-permute-start.10 = (bf16[16,768]{1,0:T(8,128)(2,1)S(1)}, bf16[16,768]{1,0:T(8,128)(2,1)S(1)}, u32[]{:S(2)}, u32[]{:S(2)}) collective-permute-start(bf16[16,768]{1,0:T(8,128)(2,1)S(1)} %shard_map.136.own), channel_id=1, source_target_pairs={{0,16},{16,0},{32,48},{48,32},{64,80},{80,64},{96,112},{112,96},{1... | collective-permute-start | bytes 73736 | tf_op jit(solution)/shard_map/ppermute | solution.py:286
  52.4 12.1 %collective-permute-start.15 = (bf16[16,768]{1,0:T(8,128)(2,1)S(1)}, bf16[16,768]{1,0:T(8,128)(2,1)S(1)}, u32[]{:S(2)}, u32[]{:S(2)}) collective-permute-start(bf16[16,768]{1,0:T(8,128)(2,1)S(1)} %get-tuple-element.54.own), channel_id=1, source_target_pairs={{0,128},{16,144},{32,160},{48,176},{64,192},{80,208},{96,224},{112... | collective-permute-start | bytes 73736 | tf_op jit(solution)/shard_map/ppermute | solution.py:286
  58.7 5.8 %collective-permute-start.16 = (bf16[16,256]{1,0:T(8,128)(2,1)S(1)}, bf16[16,256]{1,0:T(8,128)(2,1)S(1)}, u32[]{:S(2)}, u32[]{:S(2)}) collective-permute-start(bf16[16,256]{1,0:T(8,128)(2,1)S(1)} %get-tuple-element.58), channel_id=1, source_target_pairs={{0,192},{16,208},{32,224},{48,240},{64,128},{80,144},{96,160},{112... | collective-permute-start | bytes 24584 | tf_op jit(solution)/shard_map/ppermute | solution.py:286
  59.3 4.8 %collective-permute-start.14 = (bf16[16,512]{1,0:T(8,128)(2,1)S(1)}, bf16[16,512]{1,0:T(8,128)(2,1)S(1)}, u32[]{:S(2)}, u32[]{:S(2)}) collective-permute-start(bf16[16,512]{1,0:T(8,128)(2,1)S(1)} %get-tuple-element.55), channel_id=1, source_target_pairs={{0,64},{16,80},{32,96},{48,112},{64,0},{80,16},{96,32},{112,48},{1... | collective-permute-start | bytes 49160 | tf_op jit(solution)/shard_map/ppermute | solution.py:286
  66.0 28.2 %copy-start = (bf16[1,128,2048]{2,1,0:T(8,128)(2,1)S(1)}, bf16[1,128,2048]{2,1,0:T(8,128)(2,1)}, u32[]{:S(2)}) copy-start(bf16[1,128,2048]{2,1,0:T(8,128)(2,1)} %inverse.3) | copy-start | bytes 1572868
  79.8 14.5 %all-to-all-start.2 = ((bf16[16,128,128]{2,1,0:T(8,128)(2,1)}), bf16[16,128,128]{2,1,0:T(8,128)(2,1)S(1)}, u32[]{:S(2)}, u32[]{:S(2)}) async-start(bf16[16,128,128]{2,1,0:T(8,128)(2,1)} %get-tuple-element.62), calls=%async_computation.2 | async-start | bytes 1048576 | tf_op jit(solution)/shard_map/all_to_all | solution.py:304
  84.6 9.7 %collective-permute-start.19 = (bf16[64,128]{1,0:T(8,128)(2,1)S(1)}, bf16[64,128]{1,0:T(8,128)(2,1)S(1)}, u32[]{:S(2)}, u32[]{:S(2)}) collective-permute-start(bf16[64,128]{1,0:T(8,128)(2,1)S(1)} %get-tuple-element.65), channel_id=1, source_target_pairs={{0,128},{16,144},{32,160},{48,176},{64,192},{80,208},{96,224},{112... | collective-permute-start | bytes 49160 | tf_op jit(solution)/shard_map/ppermute | solution.py:286
  88.5 5.8 %collective-permute-start.20 = (bf16[32,128]{1,0:T(8,128)(2,1)S(1)}, bf16[32,128]{1,0:T(8,128)(2,1)S(1)}, u32[]{:S(2)}, u32[]{:S(2)}) collective-permute-start(bf16[32,128]{1,0:T(8,128)(2,1)S(1)} %get-tuple-element.64), channel_id=1, source_target_pairs={{0,192},{16,208},{32,224},{48,240},{64,128},{80,144},{96,160},{112... | collective-permute-start | bytes 24584 | tf_op jit(solution)/shard_map/ppermute | solution.py:286
  89.6 4.6 %collective-permute-start.18 = (bf16[32,128]{1,0:T(8,128)(2,1)S(1)}, bf16[32,128]{1,0:T(8,128)(2,1)S(1)}, u32[]{:S(2)}, u32[]{:S(2)}) collective-permute-start(bf16[32,128]{1,0:T(8,128)(2,1)S(1)} %get-tuple-element.64), channel_id=1, source_target_pairs={{0,64},{16,80},{32,96},{48,112},{64,0},{80,16},{96,32},{112,48},{1... | collective-permute-start | bytes 24584 | tf_op jit(solution)/shard_map/ppermute | solution.py:286
  (9 other events, 108.7 us)

commit v4 on v3

--- a/solution.py
+++ b/solution.py
@@ -132,7 +132,7 @@
         spread[part * SEP : part * SEP + SEP, :] = dot(hot, block[0], NN).astype(BF)
 
 
-def leaf_forward_kernel(own, a, b, c, inverse, spread, top, solved_out, send, source):
+def leaf_forward_kernel(own, a, b, c, inverse, spread, top, solved_out, send, source, held, sem):
     leaf = lax.axis_index("leaf")
     front = lax.axis_index("front")
     for j, ref in enumerate((own, a, b, c)):
@@ -142,7 +142,9 @@
                 rows = pl.ds(pl.multiple_of(at + q * ROWS, ROWS), ROWS)
                 source[rows, :] = ref[k, 0:ROWS, q * RHS : q * RHS + RHS]
     solved = dot(inverse[0], source[...], NN)
-    solved_out[...] = solved
+    held[...] = solved
+    copy = pltpu.make_async_copy(held, solved_out, sem)
+    copy.start()
     mine = jnp.concatenate(
         [
             top[0] * (1 / 16),
@@ -158,6 +160,7 @@
     total = dot(mine.astype(BF), hot, NN) - dot(solved.T.astype(BF), spread[...], NT)
     for to in range(FRONT):
         send[to] = fold(total[to * 8 : to * 8 + 8]).astype(BF)
+    copy.wait()
 
 
 def top_forward_kernel(got, first, swapped, hot3, send):
@@ -232,10 +235,14 @@
         run(swapped, later)
 
 
-def leaf_backward_kernel(got, solved, picked, send, own, side, last):
+def leaf_backward_kernel(got, solved, picked, send, own, side, last, held, sem):
+    copy = pltpu.make_async_copy(solved, held, sem)
+    copy.start()
     front = lax.axis_index("front")
     full = jnp.concatenate([unfold(got[k].astype(F32)) for k in range(FRONT)], axis=0).astype(BF)
-    residue = (solved[...] - dot(picked[...], full, NT)).astype(BF)
+    change = dot(picked[...], full, NT)
+    copy.wait()
+    residue = (held[...] - change).astype(BF)
     for to in range(FRONT):
         send[to] = residue
     row = lax.broadcasted_iota(jnp.int32, (96, SPAN), 0)
@@ -269,13 +276,13 @@
     return pltpu.with_memory_space_constraint(x, pltpu.HBM)
 
 
-def call(kernel, outs, args, specs=None, scratch=(), flops=0, size=0):
-    shapes = [jax.ShapeDtypeStruct(shape, kind) for shape, kind in outs]
+def call(kernel, outs, args, specs=None, out_specs=None, scratch=(), flops=0, size=0):
+    shapes = [jax.ShapeDtypeStruct(*out) if isinstance(out, tuple) else out for out in outs]
     return pl.pallas_call(
         kernel,
         out_shape=shapes,
         in_specs=specs or [VMEM] * len(args),
-        out_specs=[VMEM] * len(shapes),
+        out_specs=out_specs or [VMEM] * len(shapes),
         scratch_shapes=list(scratch),
         compiler_params=pltpu.CompilerParams(vmem_limit_bytes=16 * 1024 * 1024),
         cost_estimate=pl.CostEstimate(flops=flops, bytes_accessed=size, transcendentals=0),
@@ -339,7 +346,7 @@
         size=1 << 20,
     )
     parts = shifts(early, 1)
-    send, leaf_lower_block = lax.optimization_barrier((send, leaf_lower_block))
+    parts[2], leaf_lower_block = lax.optimization_barrier((parts[2], leaf_lower_block))
     spread, hot2, hot3 = call(
         spread_kernel,
         [((SPAN, PIECE), BF), ((SEP, SEP), BF), ((2 * SEP, SEP), BF)],
@@ -352,9 +359,10 @@
     swapped = swap(ahead, 1)
     solved, send = call(
         leaf_forward_kernel,
-        [((PIECE, RHS), F32), ((FRONT, 16, HALF), BF)],
+        [pltpu.HBM((PIECE, RHS), F32), ((FRONT, 16, HALF), BF)],
         (early, *parts, leaf_lower_inverse, spread, top_source),
-        scratch=[pltpu.VMEM((SUB, RHS), BF)],
+        out_specs=[HBM, VMEM],
+        scratch=[pltpu.VMEM((SUB, RHS), BF), pltpu.VMEM((PIECE, RHS), F32), pltpu.SemaphoreType.DMA],
         flops=2 * RHS * (PIECE * SUB + UPD * PIECE + UPD * SPAN),
         size=4 << 20,
     )
@@ -401,6 +409,8 @@
         leaf_backward_kernel,
         [((FRONT, PIECE, RHS), BF), ((96, RHS), F32), ((64, RHS), BF), ((32, RHS), BF)],
         (got, solved, picked),
+        specs=[VMEM, HBM, VMEM],
+        scratch=[pltpu.VMEM((PIECE, RHS), F32), pltpu.SemaphoreType.DMA],
         flops=2 * RHS * 2 * PIECE * SPAN,
         size=2 << 20,
     )

time: 95.6 us -> 95.8 us (level)
  no operation moved by 1% of the time
where the time goes in v4:
time: 95.8 us; the launch traced here: 95.4 us
  starting transfers between devices  42 us (44%)
  waiting for transfers between devices  28 us (29%)
  blocking collectives  12.4 us (13%)
  Pallas kernels  11.3 us (12%)
    ppermute x12, starting transfers between devices, swap(): return lax.ppermute(x, 'leaf', [(i, i ^ flip) for i in range(LEAVES)])  16.9 us
    ppermute x9, starting transfers between devices, shifts(): lax.ppermute(x, ('leaf', 'front'), [(leaf * FRONT + front, moved(leaf, fr...  13.5 us
    all_to_all x1, blocking collectives, exchange(): return lax.all_to_all(x, axis, 0, 0, tiled=True, axis_index_groups=groups)  12.4 us
    all_to_all x2, starting transfers between devices, exchange(): return lax.all_to_all(x, axis, 0, 0, tiled=True, axis_index_groups=groups)  11.6 us
    ppermute x9, waiting for transfers between devices, shifts(): lax.ppermute(x, ('leaf', 'front'), [(leaf * FRONT + front, moved(leaf, fr...  11.5 us
    pallas_call x12, Pallas kernels, call(): pl.pallas_call(kernel, out_shape=shapes, in_specs=specs or [VMEM] * len(a...  11.3 us
    ppermute x12, waiting for transfers between devices, swap(): return lax.ppermute(x, 'leaf', [(i, i ^ flip) for i in range(LEAVES)])  9.71 us
    all_to_all x2, waiting for transfers between devices, exchange(): return lax.all_to_all(x, axis, 0, 0, tiled=True, axis_index_groups=groups)  6.73 us
  transfers between devices with their start and end apart: 23, of which 12 were waited for; matrix products, arithmetic and copies ran while one was open for 0% of the time, Pallas kernels for 6%

profile of v4, /device:TPU:2, one launch (start us, length us, event | category | flops | bytes accessed | tf_op | source)
XLA Modules:
  0.0 95.4 jit_solution(14809638945871864435)
XLA Ops:
  1.6 2.3 %collective-permute-start.2 = (bf16[192,512]{1,0:T(8,128)(2,1)S(1)}, bf16[192,512]{1,0:T(8,128)(2,1)S(1)}, u32[]{:S(2)}, u32[]{:S(2)}) collective-permute-start(bf16[192,512]{1,0:T(8,128)(2,1)S(1)} %shard_map.131.own), channel_id=1, source_target_pairs={{0,3},{1,0},{2,1},{3,2},{4,7},{5,4},{6,5},{7,6},{8,11},{9,8},{10,9... | collective-permute-start | bytes 589832 | tf_op jit(solution)/shard_map/ppermute | solution.py:305
  4.7 1.8 %collective-permute-start = (bf16[192,512]{1,0:T(8,128)(2,1)S(1)}, bf16[192,512]{1,0:T(8,128)(2,1)S(1)}, u32[]{:S(2)}, u32[]{:S(2)}) collective-permute-start(bf16[192,512]{1,0:T(8,128)(2,1)S(1)} %shard_map.131.own), channel_id=1, source_target_pairs={{0,1},{1,2},{2,3},{3,0},{4,5},{5,6},{6,7},{7,4},{8,9},{9,10},{10,1... | collective-permute-start | bytes 589832 | tf_op jit(solution)/shard_map/ppermute | solution.py:305
  7.4 3.8 %collective-permute-done.1.b = bf16[192,512]{1,0:T(8,128)(2,1)S(1)} collective-permute-done((bf16[192,512]{1,0:T(8,128)(2,1)S(1)}, bf16[192,512]{1,0:T(8,128)(2,1)S(1)}, u32[]{:S(2)}, u32[]{:S(2)}) %collective-permute-start.1) | collective-permute-done | bytes 196640 | tf_op jit(solution)/shard_map/ppermute | solution.py:305
  11.6 3.1 %collective-permute-start.3 = (bf16[4,64,512]{2,1,0:T(8,128)(2,1)S(1)}, bf16[4,64,512]{2,1,0:T(8,128)(2,1)S(1)}, u32[]{:S(2)}, u32[]{:S(2)}) collective-permute-start(bf16[4,64,512]{2,1,0:T(8,128)(2,1)S(1)} %get-tuple-element.35.own), channel_id=1, source_target_pairs={{0,12},{1,13},{2,14},{3,15},{4,0},{5,1},{6,2},{7,3},{8,4},{9,5},{1... | collective-permute-start | bytes 786440 | tf_op jit(solution)/shard_map/ppermute | solution.py:305
  16.3 2.3 %collective-permute-start.8 = (bf16[4,128,512]{2,1,0:T(8,128)(2,1)S(1)}, bf16[4,128,512]{2,1,0:T(8,128)(2,1)}, u32[]{:S(2)}, u32[]{:S(2)}) collective-permute-start(bf16[4,128,512]{2,1,0:T(8,128)(2,1)S(1)} %get-tuple-element.44.own), channel_id=1, source_target_pairs={{0,12},{1,13},{2,14},{3,15},{4,0},{5,1},{6,2},{7,3},{8,4},{9,5},{1... | collective-permute-start | bytes 1572872 | tf_op jit(solution)/shard_map/ppermute | solution.py:305
  18.6 1.7 %collective-permute-start.7 = (bf16[4,128,512]{2,1,0:T(8,128)(2,1)S(1)}, bf16[4,128,512]{2,1,0:T(8,128)(2,1)}, u32[]{:S(2)}, u32[]{:S(2)}) collective-permute-start(bf16[4,128,512]{2,1,0:T(8,128)(2,1)S(1)} %get-tuple-element.44.own), channel_id=1, source_target_pairs={{0,8},{1,9},{2,10},{3,11},{4,12},{5,13},{6,14},{7,15},{8,0},{9,1},... | collective-permute-start | bytes 1572872 | tf_op jit(solution)/shard_map/ppermute | solution.py:305
  21.4 1.3 %shard_map.133 = (bf16[1536,128]{1,0:T(8,128)(2,1)S(1)}, bf16[512,512]{1,0:T(8,128)(2,1)S(1)}, bf16[1024,512]{1,0:T(8,128)(2,1)S(1)}) custom-call(bf16[1,1024,128]{2,1,0:T(8,128)(2,1)S(1)} %copy-done.5, s32[1,1024]{1,0:T(1,128)S(1)} %copy-done.8, s32[6,512]{1,0:T(8,128)S(1)} %copy-done.7), custom_call_target="tpu_custom_call" | custom-call | flops 402653184 | bytes 2097152 | tf_op jit(solution)/shard_map/pallas_call | solution.py:281
  22.7 2.7 %collective-permute-done.4.a = bf16[4,64,512]{2,1,0:T(8,128)(2,1)S(1)} collective-permute-done((bf16[4,64,512]{2,1,0:T(8,128)(2,1)S(1)}, bf16[4,64,512]{2,1,0:T(8,128)(2,1)S(1)}, u32[]{:S(2)}, u32[]{:S(2)}) %collective-permute-start.4) | collective-permute-done | bytes 262176 | tf_op jit(solution)/shard_map/ppermute | solution.py:305
  27.4 6.7 %all-to-all-start = ((bf16[16,16,768]{2,1,0:T(8,128)(2,1)}), bf16[16,16,768]{2,1,0:T(8,128)(2,1)S(1)}, u32[]{:S(2)}, u32[]{:S(2)}) async-start(bf16[16,16,768]{2,1,0:T(8,128)(2,1)} %copy-done.2), calls=%async_computation | async-start | bytes 786432 | tf_op jit(solution)/shard_map/all_to_all | solution.py:311
  34.2 2.6 %collective-permute-done.6.a = bf16[4,128,512]{2,1,0:T(8,128)(2,1)} collective-permute-done((bf16[4,128,512]{2,1,0:T(8,128)(2,1)S(1)}, bf16[4,128,512]{2,1,0:T(8,128)(2,1)}, u32[]{:S(2)}, u32[]{:S(2)}) %collective-permute-start.6) | collective-permute-done | bytes 524320 | tf_op jit(solution)/shard_map/ppermute | solution.py:305
  36.8 6.7 %all-to-all-done.got = bf16[16,16,768]{2,1,0:T(8,128)(2,1)S(1)} async-done(((bf16[16,16,768]{2,1,0:T(8,128)(2,1)}), bf16[16,16,768]{2,1,0:T(8,128)(2,1)S(1)}, u32[]{:S(2)}, u32[]{:S(2)}) %all-to-all-start) | async-done | bytes 393248 | tf_op jit(solution)/shard_map/all_to_all | solution.py:311
  43.5 1.6 %shard_map.137 = (bf16[512,512]{1,0:T(8,128)(2,1)S(1)}, bf16[3,512,512]{2,1,0:T(8,128)(2,1)S(1)}) custom-call(bf16[4,128,512]{2,1,0:T(8,128)(2,1)S(1)} %get-tuple-element.44.own, bf16[4,128,512]{2,1,0:T(8,128)(2,1)} %collective-permute-done.6.a, bf16[4,128,512]{2,1,0:T(8,128)(2,1)} %collective-permute-done.7.b, bf16[4,128,512]{2,1,0:T(8,128)(2,1)} %collective-permute-done.8.c), custom_call_target="tpu_custom_call" | custom-call | bytes 4194304 | tf_op jit(solution)/shard_map/pallas_call | solution.py:281
  46.4 1.6 %collective-permute-start.12 = (bf16[16,768]{1,0:T(8,128)(2,1)S(1)}, bf16[16,768]{1,0:T(8,128)(2,1)S(1)}, u32[]{:S(2)}, u32[]{:S(2)}) collective-permute-start(bf16[16,768]{1,0:T(8,128)(2,1)S(1)} %shard_map.136.own), channel_id=1, source_target_pairs={{0,48},{16,32},{32,16},{48,0},{64,112},{80,96},{96,80},{112,64},{1... | collective-permute-start | bytes 73736 | tf_op jit(solution)/shard_map/ppermute | solution.py:293
  48.4 1.2 %collective-permute-done.12.c = bf16[16,768]{1,0:T(8,128)(2,1)S(1)} collective-permute-done((bf16[16,768]{1,0:T(8,128)(2,1)S(1)}, bf16[16,768]{1,0:T(8,128)(2,1)S(1)}, u32[]{:S(2)}, u32[]{:S(2)}) %collective-permute-start.12) | collective-permute-done | bytes 24608 | tf_op jit(solution)/shard_map/ppermute | solution.py:293
  49.6 2.2 %collective-permute-done.11.b = bf16[16,768]{1,0:T(8,128)(2,1)S(1)} collective-permute-done((bf16[16,768]{1,0:T(8,128)(2,1)S(1)}, bf16[16,768]{1,0:T(8,128)(2,1)S(1)}, u32[]{:S(2)}, u32[]{:S(2)}) %collective-permute-start.11) | collective-permute-done | bytes 24608 | tf_op jit(solution)/shard_map/ppermute | solution.py:293
  52.4 6.3 %collective-permute-start.15 = (bf16[16,768]{1,0:T(8,128)(2,1)S(1)}, bf16[16,768]{1,0:T(8,128)(2,1)S(1)}, u32[]{:S(2)}, u32[]{:S(2)}) collective-permute-start(bf16[16,768]{1,0:T(8,128)(2,1)S(1)} %get-tuple-element.56.own), channel_id=1, source_target_pairs={{0,128},{16,144},{32,160},{48,176},{64,192},{80,208},{96,224},{112... | collective-permute-start | bytes 73736 | tf_op jit(solution)/shard_map/ppermute | solution.py:293
  61.4 2.7 %collective-permute-done.14.near = bf16[16,512]{1,0:T(8,128)(2,1)S(1)} collective-permute-done((bf16[16,512]{1,0:T(8,128)(2,1)S(1)}, bf16[16,512]{1,0:T(8,128)(2,1)S(1)}, u32[]{:S(2)}, u32[]{:S(2)}) %collective-permute-start.14) | collective-permute-done | bytes 16416 | tf_op jit(solution)/shard_map/ppermute | solution.py:293
  64.5 1.5 %shard_map.140 = bf16[16,16,768]{2,1,0:T(8,128)(2,1)S(1)} custom-call(bf16[16,768]{1,0:T(8,128)(2,1)S(1)} %get-tuple-element.56.own, bf16[16,512]{1,0:T(8,128)(2,1)S(1)} %collective-permute-done.14.near, bf16[16,768]{1,0:T(8,128)(2,1)S(1)} %collective-permute-done.15.far, bf16[16,256]{1,0:T(8,128)(2,1)S(1)} %collective-permute-done.16.other, ...), custom_call_target="tpu_custom_call" | custom-call | flops 1207959552 | bytes 5242880 | tf_op jit(solution)/shard_map/pallas_call | solution.py:281
  66.0 12.4 %all_to_all.15.got = bf16[16,16,768]{2,1,0:T(8,128)(2,1)S(1)} all-to-all(bf16[16,16,768]{2,1,0:T(8,128)(2,1)S(1)} %shard_map.140), channel_id=1, replica_groups=mesh['leaf'=16,'front'=16] {'front'}, dimensions={0} | all-to-all | bytes 786432 | tf_op jit(solution)/shard_map/all_to_all | solution.py:311
  78.5 1.5 %shard_map.141 = (bf16[16,128,128]{2,1,0:T(8,128)(2,1)}, f32[96,128]{1,0:T(8,128)S(1)}, bf16[64,128]{1,0:T(8,128)(2,1)S(1)}, bf16[32,128]{1,0:T(8,128)(2,1)S(1)}) custom-call(bf16[16,16,768]{2,1,0:T(8,128)(2,1)S(1)} %all_to_all.15.got, f32[128,128]{1,0:T(8,128)S(1)} %copy-done.4, bf16[128,1536]{1,0:T(8,128)(2,1)S(1)} %shard_map.139.picked), custom_call_target="tpu_custom_call" | custom-call | flops 100663296 | bytes 2097152 | tf_op jit(solution)/shard_map/pallas_call | solution.py:281
  79.9 4.8 %all-to-all-start.2 = ((bf16[16,128,128]{2,1,0:T(8,128)(2,1)}), bf16[16,128,128]{2,1,0:T(8,128)(2,1)S(1)}, u32[]{:S(2)}, u32[]{:S(2)}) async-start(bf16[16,128,128]{2,1,0:T(8,128)(2,1)} %get-tuple-element.64), calls=%async_computation.2 | async-start | bytes 1048576 | tf_op jit(solution)/shard_map/all_to_all | solution.py:311
  84.8 3.9 %collective-permute-start.19 = (bf16[64,128]{1,0:T(8,128)(2,1)S(1)}, bf16[64,128]{1,0:T(8,128)(2,1)S(1)}, u32[]{:S(2)}, u32[]{:S(2)}) collective-permute-start(bf16[64,128]{1,0:T(8,128)(2,1)S(1)} %get-tuple-element.67), channel_id=1, source_target_pairs={{0,128},{16,144},{32,160},{48,176},{64,192},{80,208},{96,224},{112... | collective-permute-start | bytes 49160 | tf_op jit(solution)/shard_map/ppermute | solution.py:293
  89.8 1.5 %collective-permute-start.18 = (bf16[32,128]{1,0:T(8,128)(2,1)S(1)}, bf16[32,128]{1,0:T(8,128)(2,1)S(1)}, u32[]{:S(2)}, u32[]{:S(2)}) collective-permute-start(bf16[32,128]{1,0:T(8,128)(2,1)S(1)} %get-tuple-element.66), channel_id=1, source_target_pairs={{0,64},{16,80},{32,96},{48,112},{64,0},{80,16},{96,32},{112,48},{1... | collective-permute-start | bytes 24584 | tf_op jit(solution)/shard_map/ppermute | solution.py:293
  91.3 3.2 %collective-permute-done.20.other = bf16[32,128]{1,0:T(8,128)(2,1)S(1)} collective-permute-done((bf16[32,128]{1,0:T(8,128)(2,1)S(1)}, bf16[32,128]{1,0:T(8,128)(2,1)S(1)}, u32[]{:S(2)}, u32[]{:S(2)}) %collective-permute-start.20) | collective-permute-done | bytes 8224 | tf_op jit(solution)/shard_map/ppermute | solution.py:293
  (53 shorter events, 15.1 us)
Async XLA Ops:
  1.6 5.7 %collective-permute-start.2 = (bf16[192,512]{1,0:T(8,128)(2,1)S(1)}, bf16[192,512]{1,0:T(8,128)(2,1)S(1)}, u32[]{:S(2)}, u32[]{:S(2)}) collective-permute-start(bf16[192,512]{1,0:T(8,128)(2,1)S(1)} %shard_map.131.own), channel_id=1, source_target_pairs={{0,3},{1,0},{2,1},{3,2},{4,7},{5,4},{6,5},{7,6},{8,11},{9,8},{10,9... | collective-permute-start | bytes 589832 | tf_op jit(solution)/shard_map/ppermute | solution.py:305
  4.0 7.2 %collective-permute-start.1 = (bf16[192,512]{1,0:T(8,128)(2,1)S(1)}, bf16[192,512]{1,0:T(8,128)(2,1)S(1)}, u32[]{:S(2)}, u32[]{:S(2)}) collective-permute-start(bf16[192,512]{1,0:T(8,128)(2,1)S(1)} %shard_map.131.own), channel_id=1, source_target_pairs={{0,2},{1,3},{2,0},{3,1},{4,6},{5,7},{6,4},{7,5},{8,10},{9,11},{10,... | collective-permute-start | bytes 589832 | tf_op jit(solution)/shard_map/ppermute | solution.py:305
  4.7 6.9 %collective-permute-start = (bf16[192,512]{1,0:T(8,128)(2,1)S(1)}, bf16[192,512]{1,0:T(8,128)(2,1)S(1)}, u32[]{:S(2)}, u32[]{:S(2)}) collective-permute-start(bf16[192,512]{1,0:T(8,128)(2,1)S(1)} %shard_map.131.own), channel_id=1, source_target_pairs={{0,1},{1,2},{2,3},{3,0},{4,5},{5,6},{6,7},{7,4},{8,9},{9,10},{10,1... | collective-permute-start | bytes 589832 | tf_op jit(solution)/shard_map/ppermute | solution.py:305
  11.6 9.8 %collective-permute-start.3 = (bf16[4,64,512]{2,1,0:T(8,128)(2,1)S(1)}, bf16[4,64,512]{2,1,0:T(8,128)(2,1)S(1)}, u32[]{:S(2)}, u32[]{:S(2)}) collective-permute-start(bf16[4,64,512]{2,1,0:T(8,128)(2,1)S(1)} %get-tuple-element.35.own), channel_id=1, source_target_pairs={{0,12},{1,13},{2,14},{3,15},{4,0},{5,1},{6,2},{7,3},{8,4},{9,5},{1... | collective-permute-start | bytes 786440 | tf_op jit(solution)/shard_map/ppermute | solution.py:305
  14.7 8.0 %collective-permute-start.5 = (bf16[4,64,512]{2,1,0:T(8,128)(2,1)S(1)}, bf16[4,64,512]{2,1,0:T(8,128)(2,1)S(1)}, u32[]{:S(2)}, u32[]{:S(2)}) collective-permute-start(bf16[4,64,512]{2,1,0:T(8,128)(2,1)S(1)} %get-tuple-element.35.own), channel_id=1, source_target_pairs={{0,8},{1,9},{2,10},{3,11},{4,12},{5,13},{6,14},{7,15},{8,0},{9,1},... | collective-permute-start | bytes 786440 | tf_op jit(solution)/shard_map/ppermute | solution.py:305
  15.3 10.1 %collective-permute-start.4 = (bf16[4,64,512]{2,1,0:T(8,128)(2,1)S(1)}, bf16[4,64,512]{2,1,0:T(8,128)(2,1)S(1)}, u32[]{:S(2)}, u32[]{:S(2)}) collective-permute-start(bf16[4,64,512]{2,1,0:T(8,128)(2,1)S(1)} %get-tuple-element.35.own), channel_id=1, source_target_pairs={{0,4},{1,5},{2,6},{3,7},{4,8},{5,9},{6,10},{7,11},{8,12},{9,13},{1... | collective-permute-start | bytes 786440 | tf_op jit(solution)/shard_map/ppermute | solution.py:305
  16.3 17.8 %collective-permute-start.8 = (bf16[4,128,512]{2,1,0:T(8,128)(2,1)S(1)}, bf16[4,128,512]{2,1,0:T(8,128)(2,1)}, u32[]{:S(2)}, u32[]{:S(2)}) collective-permute-start(bf16[4,128,512]{2,1,0:T(8,128)(2,1)S(1)} %get-tuple-element.44.own), channel_id=1, source_target_pairs={{0,12},{1,13},{2,14},{3,15},{4,0},{5,1},{6,2},{7,3},{8,4},{9,5},{1... | collective-permute-start | bytes 1572872 | tf_op jit(solution)/shard_map/ppermute | solution.py:305
  18.6 15.6 %collective-permute-start.7 = (bf16[4,128,512]{2,1,0:T(8,128)(2,1)S(1)}, bf16[4,128,512]{2,1,0:T(8,128)(2,1)}, u32[]{:S(2)}, u32[]{:S(2)}) collective-permute-start(bf16[4,128,512]{2,1,0:T(8,128)(2,1)S(1)} %get-tuple-element.44.own), channel_id=1, source_target_pairs={{0,8},{1,9},{2,10},{3,11},{4,12},{5,13},{6,14},{7,15},{8,0},{9,1},... | collective-permute-start | bytes 1572872 | tf_op jit(solution)/shard_map/ppermute | solution.py:305
  21.4 15.4 %collective-permute-start.6 = (bf16[4,128,512]{2,1,0:T(8,128)(2,1)S(1)}, bf16[4,128,512]{2,1,0:T(8,128)(2,1)}, u32[]{:S(2)}, u32[]{:S(2)}) collective-permute-start(bf16[4,128,512]{2,1,0:T(8,128)(2,1)S(1)} %get-tuple-element.44.own), channel_id=1, source_target_pairs={{0,4},{1,5},{2,6},{3,7},{4,8},{5,9},{6,10},{7,11},{8,12},{9,13},{1... | collective-permute-start | bytes 1572872 | tf_op jit(solution)/shard_map/ppermute | solution.py:305
  25.5 19.6 %collective-permute-start.9 = (bf16[512,512]{1,0:T(8,128)(2,1)S(1)}, bf16[512,512]{1,0:T(8,128)(2,1)S(1)}, u32[]{:S(2)}, u32[]{:S(2)}) collective-permute-start(bf16[512,512]{1,0:T(8,128)(2,1)S(1)} %shard_map.135.first), channel_id=1, source_target_pairs={{0,16},{16,0},{32,48},{48,32},{64,80},{80,64},{96,112},{112,96},{1... | collective-permute-start | bytes 1572872 | tf_op jit(solution)/shard_map/ppermute | solution.py:293
  27.4 16.1 %all-to-all-start = ((bf16[16,16,768]{2,1,0:T(8,128)(2,1)}), bf16[16,16,768]{2,1,0:T(8,128)(2,1)S(1)}, u32[]{:S(2)}, u32[]{:S(2)}) async-start(bf16[16,16,768]{2,1,0:T(8,128)(2,1)} %copy-done.2), calls=%async_computation | async-start | bytes 786432 | tf_op jit(solution)/shard_map/all_to_all | solution.py:311
  45.9 18.6 %collective-permute-start.17 = (bf16[3,512,512]{2,1,0:T(8,128)(2,1)S(1)}, bf16[3,512,512]{2,1,0:T(8,128)(2,1)S(1)}, u32[]{:S(2)}, u32[]{:S(2)}) collective-permute-start(bf16[3,512,512]{2,1,0:T(8,128)(2,1)S(1)} %get-tuple-element.61.later), channel_id=1, source_target_pairs={{0,16},{16,0},{32,48},{48,32},{64,80},{80,64},{96,112},{112,96},{1... | collective-permute-start | bytes 4718600 | tf_op jit(solution)/shard_map/ppermute | solution.py:293
  45.9 6.0 %collective-permute-start.13 = (bf16[512,512]{1,0:T(8,128)(2,1)S(1)}, bf16[512,512]{1,0:T(8,128)(2,1)S(1)}, u32[]{:S(2)}, u32[]{:S(2)}) collective-permute-start(bf16[512,512]{1,0:T(8,128)(2,1)S(1)} %get-tuple-element.53.first), channel_id=1, source_target_pairs={{0,16},{16,0},{32,48},{48,32},{64,80},{80,64},{96,112},{112,96},{1... | collective-permute-start | bytes 1572872 | tf_op jit(solution)/shard_map/ppermute | solution.py:293
  46.4 3.3 %collective-permute-start.12 = (bf16[16,768]{1,0:T(8,128)(2,1)S(1)}, bf16[16,768]{1,0:T(8,128)(2,1)S(1)}, u32[]{:S(2)}, u32[]{:S(2)}) collective-permute-start(bf16[16,768]{1,0:T(8,128)(2,1)S(1)} %shard_map.136.own), channel_id=1, source_target_pairs={{0,48},{16,32},{32,16},{48,0},{64,112},{80,96},{96,80},{112,64},{1... | collective-permute-start | bytes 73736 | tf_op jit(solution)/shard_map/ppermute | solution.py:293
  48.0 3.8 %collective-permute-start.11 = (bf16[16,768]{1,0:T(8,128)(2,1)S(1)}, bf16[16,768]{1,0:T(8,128)(2,1)S(1)}, u32[]{:S(2)}, u32[]{:S(2)}) collective-permute-start(bf16[16,768]{1,0:T(8,128)(2,1)S(1)} %shard_map.136.own), channel_id=1, source_target_pairs={{0,32},{16,48},{32,0},{48,16},{64,96},{80,112},{96,64},{112,80},{1... | collective-permute-start | bytes 73736 | tf_op jit(solution)/shard_map/ppermute | solution.py:293
  48.3 3.5 %collective-permute-start.10 = (bf16[16,768]{1,0:T(8,128)(2,1)S(1)}, bf16[16,768]{1,0:T(8,128)(2,1)S(1)}, u32[]{:S(2)}, u32[]{:S(2)}) collective-permute-start(bf16[16,768]{1,0:T(8,128)(2,1)S(1)} %shard_map.136.own), channel_id=1, source_target_pairs={{0,16},{16,0},{32,48},{48,32},{64,80},{80,64},{96,112},{112,96},{1... | collective-permute-start | bytes 73736 | tf_op jit(solution)/shard_map/ppermute | solution.py:293
  52.4 12.1 %collective-permute-start.15 = (bf16[16,768]{1,0:T(8,128)(2,1)S(1)}, bf16[16,768]{1,0:T(8,128)(2,1)S(1)}, u32[]{:S(2)}, u32[]{:S(2)}) collective-permute-start(bf16[16,768]{1,0:T(8,128)(2,1)S(1)} %get-tuple-element.56.own), channel_id=1, source_target_pairs={{0,128},{16,144},{32,160},{48,176},{64,192},{80,208},{96,224},{112... | collective-permute-start | bytes 73736 | tf_op jit(solution)/shard_map/ppermute | solution.py:293
  58.7 5.8 %collective-permute-start.16 = (bf16[16,256]{1,0:T(8,128)(2,1)S(1)}, bf16[16,256]{1,0:T(8,128)(2,1)S(1)}, u32[]{:S(2)}, u32[]{:S(2)}) collective-permute-start(bf16[16,256]{1,0:T(8,128)(2,1)S(1)} %get-tuple-element.60), channel_id=1, source_target_pairs={{0,192},{16,208},{32,224},{48,240},{64,128},{80,144},{96,160},{112... | collective-permute-start | bytes 24584 | tf_op jit(solution)/shard_map/ppermute | solution.py:293
  59.3 4.8 %collective-permute-start.14 = (bf16[16,512]{1,0:T(8,128)(2,1)S(1)}, bf16[16,512]{1,0:T(8,128)(2,1)S(1)}, u32[]{:S(2)}, u32[]{:S(2)}) collective-permute-start(bf16[16,512]{1,0:T(8,128)(2,1)S(1)} %get-tuple-element.57), channel_id=1, source_target_pairs={{0,64},{16,80},{32,96},{48,112},{64,0},{80,16},{96,32},{112,48},{1... | collective-permute-start | bytes 49160 | tf_op jit(solution)/shard_map/ppermute | solution.py:293
  66.0 28.5 %copy-start = (bf16[1,128,2048]{2,1,0:T(8,128)(2,1)S(1)}, bf16[1,128,2048]{2,1,0:T(8,128)(2,1)}, u32[]{:S(2)}) copy-start(bf16[1,128,2048]{2,1,0:T(8,128)(2,1)} %inverse.3) | copy-start | bytes 1572868
  79.9 14.5 %all-to-all-start.2 = ((bf16[16,128,128]{2,1,0:T(8,128)(2,1)}), bf16[16,128,128]{2,1,0:T(8,128)(2,1)S(1)}, u32[]{:S(2)}, u32[]{:S(2)}) async-start(bf16[16,128,128]{2,1,0:T(8,128)(2,1)} %get-tuple-element.64), calls=%async_computation.2 | async-start | bytes 1048576 | tf_op jit(solution)/shard_map/all_to_all | solution.py:311
  84.8 9.7 %collective-permute-start.19 = (bf16[64,128]{1,0:T(8,128)(2,1)S(1)}, bf16[64,128]{1,0:T(8,128)(2,1)S(1)}, u32[]{:S(2)}, u32[]{:S(2)}) collective-permute-start(bf16[64,128]{1,0:T(8,128)(2,1)S(1)} %get-tuple-element.67), channel_id=1, source_target_pairs={{0,128},{16,144},{32,160},{48,176},{64,192},{80,208},{96,224},{112... | collective-permute-start | bytes 49160 | tf_op jit(solution)/shard_map/ppermute | solution.py:293
  88.7 5.8 %collective-permute-start.20 = (bf16[32,128]{1,0:T(8,128)(2,1)S(1)}, bf16[32,128]{1,0:T(8,128)(2,1)S(1)}, u32[]{:S(2)}, u32[]{:S(2)}) collective-permute-start(bf16[32,128]{1,0:T(8,128)(2,1)S(1)} %get-tuple-element.66), channel_id=1, source_target_pairs={{0,192},{16,208},{32,224},{48,240},{64,128},{80,144},{96,160},{112... | collective-permute-start | bytes 24584 | tf_op jit(solution)/shard_map/ppermute | solution.py:293
  89.8 4.7 %collective-permute-start.18 = (bf16[32,128]{1,0:T(8,128)(2,1)S(1)}, bf16[32,128]{1,0:T(8,128)(2,1)S(1)}, u32[]{:S(2)}, u32[]{:S(2)}) collective-permute-start(bf16[32,128]{1,0:T(8,128)(2,1)S(1)} %get-tuple-element.66), channel_id=1, source_target_pairs={{0,64},{16,80},{32,96},{48,112},{64,0},{80,16},{96,32},{112,48},{1... | collective-permute-start | bytes 24584 | tf_op jit(solution)/shard_map/ppermute | solution.py:293
  (8 other events, 123.3 us)

commit v5 on v4

--- a/solution.py
+++ b/solution.py
@@ -379,7 +379,7 @@
         flops=2 * 256 * SEP * SEP * 4,
         size=4 << 20,
     )
-    send, second, later = lax.optimization_barrier((send, second, later))
+    send, second = lax.optimization_barrier((send, second))
     total, near, other = call(
         group_kernel,
         [((16, HALF), BF), ((16, SEP), BF), ((16, SEP // 2), BF)],
@@ -388,7 +388,7 @@
         size=2 << 20,
     )
     near, far, other = swap(near, 4), swap(total, 8), swap(other, 12)
-    total, leaf_upper_block = lax.optimization_barrier((total, leaf_upper_block))
+    total, later, leaf_upper_block = lax.optimization_barrier((total, later, leaf_upper_block))
     (picked,) = call(
         pick_kernel,
         [((PIECE, SPAN), BF)],

time: 95.8 us -> 96 us (level)
  transfers between devices with their start and end apart: 23 -> 23, of which waited for: 12 -> 12; matrix products, arithmetic and copies ran while one was open for 0% -> 0% of each run, Pallas kernels for 6% -> 5%
where the time goes in v5:
time: 96 us; the launch traced here: 95.6 us
  starting transfers between devices  41.7 us (43%)
  waiting for transfers between devices  28.3 us (29%)
  blocking collectives  12.4 us (13%)
  Pallas kernels  11.5 us (12%)
    ppermute x12, starting transfers between devices, swap(): return lax.ppermute(x, 'leaf', [(i, i ^ flip) for i in range(LEAVES)])  16.6 us
    ppermute x9, starting transfers between devices, shifts(): lax.ppermute(x, ('leaf', 'front'), [(leaf * FRONT + front, moved(leaf, fr...  13.5 us
    all_to_all x1, blocking collectives, exchange(): return lax.all_to_all(x, axis, 0, 0, tiled=True, axis_index_groups=groups)  12.4 us
    all_to_all x2, starting transfers between devices, exchange(): return lax.all_to_all(x, axis, 0, 0, tiled=True, axis_index_groups=groups)  11.6 us
    ppermute x9, waiting for transfers between devices, shifts(): lax.ppermute(x, ('leaf', 'front'), [(leaf * FRONT + front, moved(leaf, fr...  11.5 us
    pallas_call x12, Pallas kernels, call(): pl.pallas_call(kernel, out_shape=shapes, in_specs=specs or [VMEM] * len(a...  11.5 us
    ppermute x12, waiting for transfers between devices, swap(): return lax.ppermute(x, 'leaf', [(i, i ^ flip) for i in range(LEAVES)])  10 us
    all_to_all x2, waiting for transfers between devices, exchange(): return lax.all_to_all(x, axis, 0, 0, tiled=True, axis_index_groups=groups)  6.73 us
  transfers between devices with their start and end apart: 23, of which 12 were waited for; matrix products, arithmetic and copies ran while one was open for 0% of the time, Pallas kernels for 5%

profile of v5, /device:TPU:2, one launch (start us, length us, event | category | flops | bytes accessed | tf_op | source)
XLA Modules:
  0.0 95.6 jit_solution(14579228771106236114)
XLA Ops:
  1.6 2.3 %collective-permute-start.2 = (bf16[192,512]{1,0:T(8,128)(2,1)S(1)}, bf16[192,512]{1,0:T(8,128)(2,1)S(1)}, u32[]{:S(2)}, u32[]{:S(2)}) collective-permute-start(bf16[192,512]{1,0:T(8,128)(2,1)S(1)} %shard_map.131.own), channel_id=1, source_target_pairs={{0,3},{1,0},{2,1},{3,2},{4,7},{5,4},{6,5},{7,6},{8,11},{9,8},{10,9... | collective-permute-start | bytes 589832 | tf_op jit(solution)/shard_map/ppermute | solution.py:305
  4.7 1.8 %collective-permute-start = (bf16[192,512]{1,0:T(8,128)(2,1)S(1)}, bf16[192,512]{1,0:T(8,128)(2,1)S(1)}, u32[]{:S(2)}, u32[]{:S(2)}) collective-permute-start(bf16[192,512]{1,0:T(8,128)(2,1)S(1)} %shard_map.131.own), channel_id=1, source_target_pairs={{0,1},{1,2},{2,3},{3,0},{4,5},{5,6},{6,7},{7,4},{8,9},{9,10},{10,1... | collective-permute-start | bytes 589832 | tf_op jit(solution)/shard_map/ppermute | solution.py:305
  7.4 3.8 %collective-permute-done.1.b = bf16[192,512]{1,0:T(8,128)(2,1)S(1)} collective-permute-done((bf16[192,512]{1,0:T(8,128)(2,1)S(1)}, bf16[192,512]{1,0:T(8,128)(2,1)S(1)}, u32[]{:S(2)}, u32[]{:S(2)}) %collective-permute-start.1) | collective-permute-done | bytes 196640 | tf_op jit(solution)/shard_map/ppermute | solution.py:305
  11.6 3.1 %collective-permute-start.3 = (bf16[4,64,512]{2,1,0:T(8,128)(2,1)S(1)}, bf16[4,64,512]{2,1,0:T(8,128)(2,1)S(1)}, u32[]{:S(2)}, u32[]{:S(2)}) collective-permute-start(bf16[4,64,512]{2,1,0:T(8,128)(2,1)S(1)} %get-tuple-element.35.own), channel_id=1, source_target_pairs={{0,12},{1,13},{2,14},{3,15},{4,0},{5,1},{6,2},{7,3},{8,4},{9,5},{1... | collective-permute-start | bytes 786440 | tf_op jit(solution)/shard_map/ppermute | solution.py:305
  16.3 2.3 %collective-permute-start.8 = (bf16[4,128,512]{2,1,0:T(8,128)(2,1)S(1)}, bf16[4,128,512]{2,1,0:T(8,128)(2,1)}, u32[]{:S(2)}, u32[]{:S(2)}) collective-permute-start(bf16[4,128,512]{2,1,0:T(8,128)(2,1)S(1)} %get-tuple-element.44.own), channel_id=1, source_target_pairs={{0,12},{1,13},{2,14},{3,15},{4,0},{5,1},{6,2},{7,3},{8,4},{9,5},{1... | collective-permute-start | bytes 1572872 | tf_op jit(solution)/shard_map/ppermute | solution.py:305
  18.6 1.7 %collective-permute-start.7 = (bf16[4,128,512]{2,1,0:T(8,128)(2,1)S(1)}, bf16[4,128,512]{2,1,0:T(8,128)(2,1)}, u32[]{:S(2)}, u32[]{:S(2)}) collective-permute-start(bf16[4,128,512]{2,1,0:T(8,128)(2,1)S(1)} %get-tuple-element.44.own), channel_id=1, source_target_pairs={{0,8},{1,9},{2,10},{3,11},{4,12},{5,13},{6,14},{7,15},{8,0},{9,1},... | collective-permute-start | bytes 1572872 | tf_op jit(solution)/shard_map/ppermute | solution.py:305
  21.4 1.3 %shard_map.133 = (bf16[1536,128]{1,0:T(8,128)(2,1)S(1)}, bf16[512,512]{1,0:T(8,128)(2,1)S(1)}, bf16[1024,512]{1,0:T(8,128)(2,1)S(1)}) custom-call(bf16[1,1024,128]{2,1,0:T(8,128)(2,1)S(1)} %copy-done.5, s32[1,1024]{1,0:T(1,128)S(1)} %copy-done.8, s32[6,512]{1,0:T(8,128)S(1)} %copy-done.7), custom_call_target="tpu_custom_call" | custom-call | flops 402653184 | bytes 2097152 | tf_op jit(solution)/shard_map/pallas_call | solution.py:281
  22.7 2.7 %collective-permute-done.4.a = bf16[4,64,512]{2,1,0:T(8,128)(2,1)S(1)} collective-permute-done((bf16[4,64,512]{2,1,0:T(8,128)(2,1)S(1)}, bf16[4,64,512]{2,1,0:T(8,128)(2,1)S(1)}, u32[]{:S(2)}, u32[]{:S(2)}) %collective-permute-start.4) | collective-permute-done | bytes 262176 | tf_op jit(solution)/shard_map/ppermute | solution.py:305
  27.4 6.7 %all-to-all-start = ((bf16[16,16,768]{2,1,0:T(8,128)(2,1)}), bf16[16,16,768]{2,1,0:T(8,128)(2,1)S(1)}, u32[]{:S(2)}, u32[]{:S(2)}) async-start(bf16[16,16,768]{2,1,0:T(8,128)(2,1)} %copy-done.2), calls=%async_computation | async-start | bytes 786432 | tf_op jit(solution)/shard_map/all_to_all | solution.py:311
  34.2 2.6 %collective-permute-done.6.a = bf16[4,128,512]{2,1,0:T(8,128)(2,1)} collective-permute-done((bf16[4,128,512]{2,1,0:T(8,128)(2,1)S(1)}, bf16[4,128,512]{2,1,0:T(8,128)(2,1)}, u32[]{:S(2)}, u32[]{:S(2)}) %collective-permute-start.6) | collective-permute-done | bytes 524320 | tf_op jit(solution)/shard_map/ppermute | solution.py:305
  36.8 6.7 %all-to-all-done.got = bf16[16,16,768]{2,1,0:T(8,128)(2,1)S(1)} async-done(((bf16[16,16,768]{2,1,0:T(8,128)(2,1)}), bf16[16,16,768]{2,1,0:T(8,128)(2,1)S(1)}, u32[]{:S(2)}, u32[]{:S(2)}) %all-to-all-start) | async-done | bytes 393248 | tf_op jit(solution)/shard_map/all_to_all | solution.py:311
  43.5 1.6 %shard_map.137 = (bf16[512,512]{1,0:T(8,128)(2,1)S(1)}, bf16[3,512,512]{2,1,0:T(8,128)(2,1)S(1)}) custom-call(bf16[4,128,512]{2,1,0:T(8,128)(2,1)S(1)} %get-tuple-element.44.own, bf16[4,128,512]{2,1,0:T(8,128)(2,1)} %collective-permute-done.6.a, bf16[4,128,512]{2,1,0:T(8,128)(2,1)} %collective-permute-done.7.b, bf16[4,128,512]{2,1,0:T(8,128)(2,1)} %collective-permute-done.8.c), custom_call_target="tpu_custom_call" | custom-call | bytes 4194304 | tf_op jit(solution)/shard_map/pallas_call | solution.py:281
  45.9 2.0 %collective-permute-start.12 = (bf16[16,768]{1,0:T(8,128)(2,1)S(1)}, bf16[16,768]{1,0:T(8,128)(2,1)S(1)}, u32[]{:S(2)}, u32[]{:S(2)}) collective-permute-start(bf16[16,768]{1,0:T(8,128)(2,1)S(1)} %shard_map.136.own), channel_id=1, source_target_pairs={{0,48},{16,32},{32,16},{48,0},{64,112},{80,96},{96,80},{112,64},{1... | collective-permute-start | bytes 73736 | tf_op jit(solution)/shard_map/ppermute | solution.py:293
  48.1 1.4 %collective-permute-done.12.c = bf16[16,768]{1,0:T(8,128)(2,1)S(1)} collective-permute-done((bf16[16,768]{1,0:T(8,128)(2,1)S(1)}, bf16[16,768]{1,0:T(8,128)(2,1)S(1)}, u32[]{:S(2)}, u32[]{:S(2)}) %collective-permute-start.12) | collective-permute-done | bytes 24608 | tf_op jit(solution)/shard_map/ppermute | solution.py:293
  49.4 2.3 %collective-permute-done.11.b = bf16[16,768]{1,0:T(8,128)(2,1)S(1)} collective-permute-done((bf16[16,768]{1,0:T(8,128)(2,1)S(1)}, bf16[16,768]{1,0:T(8,128)(2,1)S(1)}, u32[]{:S(2)}, u32[]{:S(2)}) %collective-permute-start.11) | collective-permute-done | bytes 24608 | tf_op jit(solution)/shard_map/ppermute | solution.py:293
  52.5 6.4 %collective-permute-start.15 = (bf16[16,768]{1,0:T(8,128)(2,1)S(1)}, bf16[16,768]{1,0:T(8,128)(2,1)S(1)}, u32[]{:S(2)}, u32[]{:S(2)}) collective-permute-start(bf16[16,768]{1,0:T(8,128)(2,1)S(1)} %get-tuple-element.56.own), channel_id=1, source_target_pairs={{0,128},{16,144},{32,160},{48,176},{64,192},{80,208},{96,224},{112... | collective-permute-start | bytes 73736 | tf_op jit(solution)/shard_map/ppermute | solution.py:293
  61.6 2.6 %collective-permute-done.14.near = bf16[16,512]{1,0:T(8,128)(2,1)S(1)} collective-permute-done((bf16[16,512]{1,0:T(8,128)(2,1)S(1)}, bf16[16,512]{1,0:T(8,128)(2,1)S(1)}, u32[]{:S(2)}, u32[]{:S(2)}) %collective-permute-start.14) | collective-permute-done | bytes 16416 | tf_op jit(solution)/shard_map/ppermute | solution.py:293
  64.7 1.5 %shard_map.140 = bf16[16,16,768]{2,1,0:T(8,128)(2,1)S(1)} custom-call(bf16[16,768]{1,0:T(8,128)(2,1)S(1)} %get-tuple-element.56.own, bf16[16,512]{1,0:T(8,128)(2,1)S(1)} %collective-permute-done.14.near, bf16[16,768]{1,0:T(8,128)(2,1)S(1)} %collective-permute-done.15.far, bf16[16,256]{1,0:T(8,128)(2,1)S(1)} %collective-permute-done.16.other, ...), custom_call_target="tpu_custom_call" | custom-call | flops 1207959552 | bytes 5242880 | tf_op jit(solution)/shard_map/pallas_call | solution.py:281
  66.2 12.4 %all_to_all.15.got = bf16[16,16,768]{2,1,0:T(8,128)(2,1)S(1)} all-to-all(bf16[16,16,768]{2,1,0:T(8,128)(2,1)S(1)} %shard_map.140), channel_id=1, replica_groups=mesh['leaf'=16,'front'=16] {'front'}, dimensions={0} | all-to-all | bytes 786432 | tf_op jit(solution)/shard_map/all_to_all | solution.py:311
  78.6 1.5 %shard_map.141 = (bf16[16,128,128]{2,1,0:T(8,128)(2,1)}, f32[96,128]{1,0:T(8,128)S(1)}, bf16[64,128]{1,0:T(8,128)(2,1)S(1)}, bf16[32,128]{1,0:T(8,128)(2,1)S(1)}) custom-call(bf16[16,16,768]{2,1,0:T(8,128)(2,1)S(1)} %all_to_all.15.got, f32[128,128]{1,0:T(8,128)S(1)} %copy-done.4, bf16[128,1536]{1,0:T(8,128)(2,1)S(1)} %shard_map.139.picked), custom_call_target="tpu_custom_call" | custom-call | flops 100663296 | bytes 2097152 | tf_op jit(solution)/shard_map/pallas_call | solution.py:281
  80.1 4.8 %all-to-all-start.2 = ((bf16[16,128,128]{2,1,0:T(8,128)(2,1)}), bf16[16,128,128]{2,1,0:T(8,128)(2,1)S(1)}, u32[]{:S(2)}, u32[]{:S(2)}) async-start(bf16[16,128,128]{2,1,0:T(8,128)(2,1)} %get-tuple-element.64), calls=%async_computation.2 | async-start | bytes 1048576 | tf_op jit(solution)/shard_map/all_to_all | solution.py:311
  85.0 3.9 %collective-permute-start.19 = (bf16[64,128]{1,0:T(8,128)(2,1)S(1)}, bf16[64,128]{1,0:T(8,128)(2,1)S(1)}, u32[]{:S(2)}, u32[]{:S(2)}) collective-permute-start(bf16[64,128]{1,0:T(8,128)(2,1)S(1)} %get-tuple-element.67), channel_id=1, source_target_pairs={{0,128},{16,144},{32,160},{48,176},{64,192},{80,208},{96,224},{112... | collective-permute-start | bytes 49160 | tf_op jit(solution)/shard_map/ppermute | solution.py:293
  90.0 1.5 %collective-permute-start.18 = (bf16[32,128]{1,0:T(8,128)(2,1)S(1)}, bf16[32,128]{1,0:T(8,128)(2,1)S(1)}, u32[]{:S(2)}, u32[]{:S(2)}) collective-permute-start(bf16[32,128]{1,0:T(8,128)(2,1)S(1)} %get-tuple-element.66), channel_id=1, source_target_pairs={{0,64},{16,80},{32,96},{48,112},{64,0},{80,16},{96,32},{112,48},{1... | collective-permute-start | bytes 24584 | tf_op jit(solution)/shard_map/ppermute | solution.py:293
  91.5 3.2 %collective-permute-done.20.other = bf16[32,128]{1,0:T(8,128)(2,1)S(1)} collective-permute-done((bf16[32,128]{1,0:T(8,128)(2,1)S(1)}, bf16[32,128]{1,0:T(8,128)(2,1)S(1)}, u32[]{:S(2)}, u32[]{:S(2)}) %collective-permute-start.20) | collective-permute-done | bytes 8224 | tf_op jit(solution)/shard_map/ppermute | solution.py:293
  (53 shorter events, 14.6 us)
Async XLA Ops:
  1.6 5.7 %collective-permute-start.2 = (bf16[192,512]{1,0:T(8,128)(2,1)S(1)}, bf16[192,512]{1,0:T(8,128)(2,1)S(1)}, u32[]{:S(2)}, u32[]{:S(2)}) collective-permute-start(bf16[192,512]{1,0:T(8,128)(2,1)S(1)} %shard_map.131.own), channel_id=1, source_target_pairs={{0,3},{1,0},{2,1},{3,2},{4,7},{5,4},{6,5},{7,6},{8,11},{9,8},{10,9... | collective-permute-start | bytes 589832 | tf_op jit(solution)/shard_map/ppermute | solution.py:305
  4.0 7.2 %collective-permute-start.1 = (bf16[192,512]{1,0:T(8,128)(2,1)S(1)}, bf16[192,512]{1,0:T(8,128)(2,1)S(1)}, u32[]{:S(2)}, u32[]{:S(2)}) collective-permute-start(bf16[192,512]{1,0:T(8,128)(2,1)S(1)} %shard_map.131.own), channel_id=1, source_target_pairs={{0,2},{1,3},{2,0},{3,1},{4,6},{5,7},{6,4},{7,5},{8,10},{9,11},{10,... | collective-permute-start | bytes 589832 | tf_op jit(solution)/shard_map/ppermute | solution.py:305
  4.7 6.9 %collective-permute-start = (bf16[192,512]{1,0:T(8,128)(2,1)S(1)}, bf16[192,512]{1,0:T(8,128)(2,1)S(1)}, u32[]{:S(2)}, u32[]{:S(2)}) collective-permute-start(bf16[192,512]{1,0:T(8,128)(2,1)S(1)} %shard_map.131.own), channel_id=1, source_target_pairs={{0,1},{1,2},{2,3},{3,0},{4,5},{5,6},{6,7},{7,4},{8,9},{9,10},{10,1... | collective-permute-start | bytes 589832 | tf_op jit(solution)/shard_map/ppermute | solution.py:305
  11.6 9.8 %collective-permute-start.3 = (bf16[4,64,512]{2,1,0:T(8,128)(2,1)S(1)}, bf16[4,64,512]{2,1,0:T(8,128)(2,1)S(1)}, u32[]{:S(2)}, u32[]{:S(2)}) collective-permute-start(bf16[4,64,512]{2,1,0:T(8,128)(2,1)S(1)} %get-tuple-element.35.own), channel_id=1, source_target_pairs={{0,12},{1,13},{2,14},{3,15},{4,0},{5,1},{6,2},{7,3},{8,4},{9,5},{1... | collective-permute-start | bytes 786440 | tf_op jit(solution)/shard_map/ppermute | solution.py:305
  14.7 8.0 %collective-permute-start.5 = (bf16[4,64,512]{2,1,0:T(8,128)(2,1)S(1)}, bf16[4,64,512]{2,1,0:T(8,128)(2,1)S(1)}, u32[]{:S(2)}, u32[]{:S(2)}) collective-permute-start(bf16[4,64,512]{2,1,0:T(8,128)(2,1)S(1)} %get-tuple-element.35.own), channel_id=1, source_target_pairs={{0,8},{1,9},{2,10},{3,11},{4,12},{5,13},{6,14},{7,15},{8,0},{9,1},... | collective-permute-start | bytes 786440 | tf_op jit(solution)/shard_map/ppermute | solution.py:305
  15.3 10.1 %collective-permute-start.4 = (bf16[4,64,512]{2,1,0:T(8,128)(2,1)S(1)}, bf16[4,64,512]{2,1,0:T(8,128)(2,1)S(1)}, u32[]{:S(2)}, u32[]{:S(2)}) collective-permute-start(bf16[4,64,512]{2,1,0:T(8,128)(2,1)S(1)} %get-tuple-element.35.own), channel_id=1, source_target_pairs={{0,4},{1,5},{2,6},{3,7},{4,8},{5,9},{6,10},{7,11},{8,12},{9,13},{1... | collective-permute-start | bytes 786440 | tf_op jit(solution)/shard_map/ppermute | solution.py:305
  16.3 17.8 %collective-permute-start.8 = (bf16[4,128,512]{2,1,0:T(8,128)(2,1)S(1)}, bf16[4,128,512]{2,1,0:T(8,128)(2,1)}, u32[]{:S(2)}, u32[]{:S(2)}) collective-permute-start(bf16[4,128,512]{2,1,0:T(8,128)(2,1)S(1)} %get-tuple-element.44.own), channel_id=1, source_target_pairs={{0,12},{1,13},{2,14},{3,15},{4,0},{5,1},{6,2},{7,3},{8,4},{9,5},{1... | collective-permute-start | bytes 1572872 | tf_op jit(solution)/shard_map/ppermute | solution.py:305
  18.6 15.6 %collective-permute-start.7 = (bf16[4,128,512]{2,1,0:T(8,128)(2,1)S(1)}, bf16[4,128,512]{2,1,0:T(8,128)(2,1)}, u32[]{:S(2)}, u32[]{:S(2)}) collective-permute-start(bf16[4,128,512]{2,1,0:T(8,128)(2,1)S(1)} %get-tuple-element.44.own), channel_id=1, source_target_pairs={{0,8},{1,9},{2,10},{3,11},{4,12},{5,13},{6,14},{7,15},{8,0},{9,1},... | collective-permute-start | bytes 1572872 | tf_op jit(solution)/shard_map/ppermute | solution.py:305
  21.4 15.4 %collective-permute-start.6 = (bf16[4,128,512]{2,1,0:T(8,128)(2,1)S(1)}, bf16[4,128,512]{2,1,0:T(8,128)(2,1)}, u32[]{:S(2)}, u32[]{:S(2)}) collective-permute-start(bf16[4,128,512]{2,1,0:T(8,128)(2,1)S(1)} %get-tuple-element.44.own), channel_id=1, source_target_pairs={{0,4},{1,5},{2,6},{3,7},{4,8},{5,9},{6,10},{7,11},{8,12},{9,13},{1... | collective-permute-start | bytes 1572872 | tf_op jit(solution)/shard_map/ppermute | solution.py:305
  25.5 19.6 %collective-permute-start.9 = (bf16[512,512]{1,0:T(8,128)(2,1)S(1)}, bf16[512,512]{1,0:T(8,128)(2,1)S(1)}, u32[]{:S(2)}, u32[]{:S(2)}) collective-permute-start(bf16[512,512]{1,0:T(8,128)(2,1)S(1)} %shard_map.135.first), channel_id=1, source_target_pairs={{0,16},{16,0},{32,48},{48,32},{64,80},{80,64},{96,112},{112,96},{1... | collective-permute-start | bytes 1572872 | tf_op jit(solution)/shard_map/ppermute | solution.py:293
  27.4 16.1 %all-to-all-start = ((bf16[16,16,768]{2,1,0:T(8,128)(2,1)}), bf16[16,16,768]{2,1,0:T(8,128)(2,1)S(1)}, u32[]{:S(2)}, u32[]{:S(2)}) async-start(bf16[16,16,768]{2,1,0:T(8,128)(2,1)} %copy-done.2), calls=%async_computation | async-start | bytes 786432 | tf_op jit(solution)/shard_map/all_to_all | solution.py:311
  45.9 5.9 %collective-permute-start.13 = (bf16[512,512]{1,0:T(8,128)(2,1)S(1)}, bf16[512,512]{1,0:T(8,128)(2,1)S(1)}, u32[]{:S(2)}, u32[]{:S(2)}) collective-permute-start(bf16[512,512]{1,0:T(8,128)(2,1)S(1)} %get-tuple-element.52.first), channel_id=1, source_target_pairs={{0,16},{16,0},{32,48},{48,32},{64,80},{80,64},{96,112},{112,96},{1... | collective-permute-start | bytes 1572872 | tf_op jit(solution)/shard_map/ppermute | solution.py:293
  45.9 3.6 %collective-permute-start.12 = (bf16[16,768]{1,0:T(8,128)(2,1)S(1)}, bf16[16,768]{1,0:T(8,128)(2,1)S(1)}, u32[]{:S(2)}, u32[]{:S(2)}) collective-permute-start(bf16[16,768]{1,0:T(8,128)(2,1)S(1)} %shard_map.136.own), channel_id=1, source_target_pairs={{0,48},{16,32},{32,16},{48,0},{64,112},{80,96},{96,80},{112,64},{1... | collective-permute-start | bytes 73736 | tf_op jit(solution)/shard_map/ppermute | solution.py:293
  47.9 3.8 %collective-permute-start.11 = (bf16[16,768]{1,0:T(8,128)(2,1)S(1)}, bf16[16,768]{1,0:T(8,128)(2,1)S(1)}, u32[]{:S(2)}, u32[]{:S(2)}) collective-permute-start(bf16[16,768]{1,0:T(8,128)(2,1)S(1)} %shard_map.136.own), channel_id=1, source_target_pairs={{0,32},{16,48},{32,0},{48,16},{64,96},{80,112},{96,64},{112,80},{1... | collective-permute-start | bytes 73736 | tf_op jit(solution)/shard_map/ppermute | solution.py:293
  48.0 3.7 %collective-permute-start.10 = (bf16[16,768]{1,0:T(8,128)(2,1)S(1)}, bf16[16,768]{1,0:T(8,128)(2,1)S(1)}, u32[]{:S(2)}, u32[]{:S(2)}) collective-permute-start(bf16[16,768]{1,0:T(8,128)(2,1)S(1)} %shard_map.136.own), channel_id=1, source_target_pairs={{0,16},{16,0},{32,48},{48,32},{64,80},{80,64},{96,112},{112,96},{1... | collective-permute-start | bytes 73736 | tf_op jit(solution)/shard_map/ppermute | solution.py:293
  52.5 12.2 %collective-permute-start.17 = (bf16[3,512,512]{2,1,0:T(8,128)(2,1)S(1)}, bf16[3,512,512]{2,1,0:T(8,128)(2,1)S(1)}, u32[]{:S(2)}, u32[]{:S(2)}) collective-permute-start(bf16[3,512,512]{2,1,0:T(8,128)(2,1)S(1)} %get-tuple-element.61.later), channel_id=1, source_target_pairs={{0,16},{16,0},{32,48},{48,32},{64,80},{80,64},{96,112},{112,96},{1... | collective-permute-start | bytes 4718600 | tf_op jit(solution)/shard_map/ppermute | solution.py:293
  52.5 12.1 %collective-permute-start.15 = (bf16[16,768]{1,0:T(8,128)(2,1)S(1)}, bf16[16,768]{1,0:T(8,128)(2,1)S(1)}, u32[]{:S(2)}, u32[]{:S(2)}) collective-permute-start(bf16[16,768]{1,0:T(8,128)(2,1)S(1)} %get-tuple-element.56.own), channel_id=1, source_target_pairs={{0,128},{16,144},{32,160},{48,176},{64,192},{80,208},{96,224},{112... | collective-permute-start | bytes 73736 | tf_op jit(solution)/shard_map/ppermute | solution.py:293
  58.9 5.8 %collective-permute-start.16 = (bf16[16,256]{1,0:T(8,128)(2,1)S(1)}, bf16[16,256]{1,0:T(8,128)(2,1)S(1)}, u32[]{:S(2)}, u32[]{:S(2)}) collective-permute-start(bf16[16,256]{1,0:T(8,128)(2,1)S(1)} %get-tuple-element.60), channel_id=1, source_target_pairs={{0,192},{16,208},{32,224},{48,240},{64,128},{80,144},{96,160},{112... | collective-permute-start | bytes 24584 | tf_op jit(solution)/shard_map/ppermute | solution.py:293
  59.5 4.7 %collective-permute-start.14 = (bf16[16,512]{1,0:T(8,128)(2,1)S(1)}, bf16[16,512]{1,0:T(8,128)(2,1)S(1)}, u32[]{:S(2)}, u32[]{:S(2)}) collective-permute-start(bf16[16,512]{1,0:T(8,128)(2,1)S(1)} %get-tuple-element.57), channel_id=1, source_target_pairs={{0,64},{16,80},{32,96},{48,112},{64,0},{80,16},{96,32},{112,48},{1... | collective-permute-start | bytes 49160 | tf_op jit(solution)/shard_map/ppermute | solution.py:293
  66.2 28.5 %copy-start = (bf16[1,128,2048]{2,1,0:T(8,128)(2,1)S(1)}, bf16[1,128,2048]{2,1,0:T(8,128)(2,1)}, u32[]{:S(2)}) copy-start(bf16[1,128,2048]{2,1,0:T(8,128)(2,1)} %inverse.3) | copy-start | bytes 1572868
  80.1 14.5 %all-to-all-start.2 = ((bf16[16,128,128]{2,1,0:T(8,128)(2,1)}), bf16[16,128,128]{2,1,0:T(8,128)(2,1)S(1)}, u32[]{:S(2)}, u32[]{:S(2)}) async-start(bf16[16,128,128]{2,1,0:T(8,128)(2,1)} %get-tuple-element.64), calls=%async_computation.2 | async-start | bytes 1048576 | tf_op jit(solution)/shard_map/all_to_all | solution.py:311
  85.0 9.7 %collective-permute-start.19 = (bf16[64,128]{1,0:T(8,128)(2,1)S(1)}, bf16[64,128]{1,0:T(8,128)(2,1)S(1)}, u32[]{:S(2)}, u32[]{:S(2)}) collective-permute-start(bf16[64,128]{1,0:T(8,128)(2,1)S(1)} %get-tuple-element.67), channel_id=1, source_target_pairs={{0,128},{16,144},{32,160},{48,176},{64,192},{80,208},{96,224},{112... | collective-permute-start | bytes 49160 | tf_op jit(solution)/shard_map/ppermute | solution.py:293
  88.9 5.8 %collective-permute-start.20 = (bf16[32,128]{1,0:T(8,128)(2,1)S(1)}, bf16[32,128]{1,0:T(8,128)(2,1)S(1)}, u32[]{:S(2)}, u32[]{:S(2)}) collective-permute-start(bf16[32,128]{1,0:T(8,128)(2,1)S(1)} %get-tuple-element.66), channel_id=1, source_target_pairs={{0,192},{16,208},{32,224},{48,240},{64,128},{80,144},{96,160},{112... | collective-permute-start | bytes 24584 | tf_op jit(solution)/shard_map/ppermute | solution.py:293
  90.0 4.7 %collective-permute-start.18 = (bf16[32,128]{1,0:T(8,128)(2,1)S(1)}, bf16[32,128]{1,0:T(8,128)(2,1)S(1)}, u32[]{:S(2)}, u32[]{:S(2)}) collective-permute-start(bf16[32,128]{1,0:T(8,128)(2,1)S(1)} %get-tuple-element.66), channel_id=1, source_target_pairs={{0,64},{16,80},{32,96},{48,112},{64,0},{80,16},{96,32},{112,48},{1... | collective-permute-start | bytes 24584 | tf_op jit(solution)/shard_map/ppermute | solution.py:293
  (8 other events, 123.4 us)
